TPU v7x, 32 devices: a whole 2x2x4 slice. The times are simulated.
32 devices in a mesh: dp: 8 (over y, x, core), mp: 4 (over z).
Axes of the slice: x: 2, y: 2, z: 4, core: 2. Of those that a mesh axis runs over, the one named last changes fastest.
Arguments:
- tokens: bfloat16 [2048, 16, 512], P('mp', 'dp'), may hold values from -6 to 6
- lengths: int32 [16], P('dp'), may hold values from 256 to 2048, as said below
- gain_one: float32 [512], replicated, may hold values from 0.25 to 1.75
- shift_one: float32 [512], replicated, may hold values from -3 to 3
- w_query: bfloat16 [512, 512], P(None, 'mp'), may hold values from -0.375 to 0.375
- w_key: bfloat16 [512, 512], P(None, 'mp'), may hold values from -0.25 to 0.25
- w_value: bfloat16 [512, 512], P(None, 'mp'), may hold values from -0.25 to 0.25
- w_output: bfloat16 [512, 512], P('mp'), may hold values from -1 to 1
- gain_two: float32 [512], replicated, may hold values from 0.25 to 1.75
- shift_two: float32 [512], replicated, may hold values from -3 to 3
- w_up: bfloat16 [512, 2048], P(None, 'mp'), may hold values from -0.25 to 0.25
- w_down: bfloat16 [2048, 512], P('mp'), may hold values from -0.125 to 0.125
- cotangent: bfloat16 [2048, 16, 512], P('mp', 'dp'), may hold values from -6 to 6
Outputs:
- mixed: bfloat16 [2048, 16, 512], P('mp', 'dp')
- grad_tokens: float32 [2048, 16, 512], P('mp', 'dp')
- grad_query: float32 [512, 512], P(None, 'mp')
- grad_key: float32 [512, 512], P(None, 'mp')
- grad_value: float32 [512, 512], P(None, 'mp')
- grad_output: float32 [512, 512], P('mp')
- grad_up: float32 [512, 2048], P(None, 'mp')
- grad_down: float32 [2048, 512], P('mp')
- grad_gain_one: float32 [512], replicated
- grad_shift_one: float32 [512], replicated
- grad_gain_two: float32 [512], replicated
- grad_shift_two: float32 [512], replicated
Inputs may be any that keep to these rules, and one draw needn't show every extreme that they name: `lengths`: in every group of 2 consecutive documents one has length 2048; the others vary from document to document.
All inputs are finite; a program needn't handle non-finite values.
Results may differ from a plain program's by a relative error of at most 0.018.
Values may be sent and summed in bfloat16 or wider, within the bound.
A program may use at most 256 MiB of HBM per device.

v0:
```python
from functools import reduce

import jax
import jax.numpy as jnp
from jax import lax
from jax.sharding import PartitionSpec as P

HEAD_DIM = 64
BLOCK = 16


def layer_norm(values, gain_vec, shift_vec):
    row_mean = jnp.mean(values, axis=-1, keepdims=True)
    centered = values - row_mean
    variance = jnp.mean(centered * centered, axis=-1, keepdims=True)
    return centered * lax.rsqrt(variance + 1e-05) * gain_vec + shift_vec


def sibling(array):
    shaped = array.reshape((array.shape[0] // 2, 2) + array.shape[1:])
    return jnp.flip(shaped, axis=1).reshape(array.shape)


def upsample(array, stride):
    wide = jnp.broadcast_to(array[:, None], (array.shape[0], stride) + array.shape[1:])
    return wide.reshape((array.shape[0] * stride,) + array.shape[1:])


def hier_attend(queries, key_rows, value_rows, live_mask, span):
    length, head_count, head_size = queries.shape
    levels = (length // span).bit_length() - 1
    scaling = head_size ** (-0.5)
    row_tops, row_sums, row_nums = ([], [], [])
    for level_idx in range(levels):
        stride = 2**level_idx
        coarse = length // stride
        blocks = coarse // span
        counts = jnp.sum(live_mask.reshape(coarse, stride), axis=1)
        safe_count = jnp.maximum(counts, 1.0)
        query_mean = jnp.mean(queries.reshape(coarse, stride, head_count, head_size), axis=1)
        key_mean = (
            jnp.sum(
                (key_rows * live_mask[:, None, None]).reshape(
                    coarse, stride, head_count, head_size
                ),
                axis=1,
            )
            / safe_count[:, None, None]
        )
        value_mean = (
            jnp.sum(
                (value_rows * live_mask[:, None, None]).reshape(
                    coarse, stride, head_count, head_size
                ),
                axis=1,
            )
            / safe_count[:, None, None]
        )
        query_blocks = query_mean.reshape(blocks, span, head_count, head_size)
        key_blocks = key_mean.reshape(blocks, span, head_count, head_size)
        value_blocks = value_mean.reshape(blocks, span, head_count, head_size)
        count_blocks = counts.reshape(blocks, span)
        if level_idx == 0:
            key_set = jnp.concatenate([key_blocks, sibling(key_blocks)], axis=1)
            value_set = jnp.concatenate([value_blocks, sibling(value_blocks)], axis=1)
            count_set = jnp.concatenate([count_blocks, sibling(count_blocks)], axis=1)
        else:
            key_set = sibling(key_blocks)
            value_set = sibling(value_blocks)
            count_set = sibling(count_blocks)
        score = (
            jnp.einsum("bqhe,bkhe->bhqk", query_blocks, key_set, precision=lax.Precision.HIGHEST)
            * scaling
        )
        present = (count_set > 0.0)[:, None, None, :]
        score = jnp.where(present, score, -1e30)
        row_top = jnp.max(score, axis=-1)
        weight = count_set[:, None, None, :] * jnp.exp(score - row_top[..., None])
        row_sum = jnp.sum(weight, axis=-1)
        row_num = jnp.einsum("bhqk,bkhe->bqhe", weight, value_set, precision=lax.Precision.HIGHEST)
        row_top = jnp.transpose(row_top, (0, 2, 1)).reshape(coarse, head_count)
        row_sum = jnp.transpose(row_sum, (0, 2, 1)).reshape(coarse, head_count)
        row_num = row_num.reshape(coarse, head_count, head_size)
        row_tops.append(upsample(row_top, stride))
        row_sums.append(upsample(row_sum, stride))
        row_nums.append(upsample(row_num, stride))
    overall = reduce(jnp.maximum, row_tops)
    total_sum = jnp.zeros_like(overall)
    total_num = jnp.zeros_like(queries)
    for level_idx in range(levels):
        factor = jnp.exp(row_tops[level_idx] - overall)
        total_sum = total_sum + row_sums[level_idx] * factor
        total_num = total_num + row_nums[level_idx] * factor[..., None]
    return total_num / total_sum[..., None]


def attend_one(queries, key_rows, value_rows, live_mask):
    return hier_attend(queries, key_rows, value_rows, live_mask, BLOCK)


def doc_sum(values):
    return (
        lax.psum(values[0].astype(jnp.bfloat16), "dp").astype(jnp.float32),
        lax.psum(values[1].astype(jnp.bfloat16), "dp").astype(jnp.float32),
        lax.psum(values[2].astype(jnp.bfloat16), "dp").astype(jnp.float32),
        lax.psum(values[3].astype(jnp.bfloat16), "dp").astype(jnp.float32),
        lax.psum(values[4].astype(jnp.bfloat16), "dp").astype(jnp.float32),
        lax.psum(values[5].astype(jnp.bfloat16), "dp").astype(jnp.float32),
    )


def per_device(
    tokens,
    lengths,
    gain_one,
    shift_one,
    w_query,
    w_key,
    w_value,
    w_output,
    gain_two,
    shift_two,
    w_up,
    w_down,
    cotangent,
):
    local_rows, doc_count, width_all = tokens.shape
    group_count = lax.axis_size("mp")
    length = local_rows * group_count
    heads_here = w_query.shape[1] // HEAD_DIM
    head_width = heads_here * HEAD_DIM
    live_mask = (jnp.arange(length, dtype=jnp.int32)[:, None] < lengths[None, :]).astype(
        jnp.float32
    )

    def attend(query_rows, key_rows, value_rows):

        def to_heads(array):
            return array.reshape(length, doc_count, heads_here, HEAD_DIM)

        result = jax.vmap(attend_one, in_axes=(1, 1, 1, 1), out_axes=1)(
            to_heads(query_rows), to_heads(key_rows), to_heads(value_rows), live_mask
        )
        return result.reshape(length, doc_count, head_width)

    base_rows = tokens.astype(jnp.float32)
    normed_one = layer_norm(base_rows, gain_one, shift_one).astype(jnp.bfloat16)
    complete_first = lax.all_gather(normed_one, "mp", axis=0, tiled=True)

    def project(weight_portion):
        return jnp.einsum(
            "gix,xh->gih", complete_first, weight_portion, preferred_element_type=jnp.float32
        ).astype(jnp.bfloat16)

    query_rows = project(w_query)
    key_rows = project(w_key)
    value_rows = project(w_value)
    context = attend(
        query_rows.astype(jnp.float32), key_rows.astype(jnp.float32), value_rows.astype(jnp.float32)
    ).astype(jnp.bfloat16)
    rows_now = lax.slice_in_dim(context, 0, local_rows * lax.axis_size("mp"), axis=0)
    attn_out = lax.psum_scatter(
        jnp.einsum("snw,wd->snd", rows_now, w_output, preferred_element_type=jnp.float32).astype(
            jnp.bfloat16
        ),
        "mp",
        scatter_dimension=0,
        tiled=True,
    ).astype(jnp.float32)
    middle = base_rows + attn_out
    normed_two = layer_norm(middle, gain_two, shift_two).astype(jnp.bfloat16)
    full_two = lax.all_gather(normed_two, "mp", axis=0, tiled=True)
    pre_act = jnp.einsum("snd,df->snf", full_two, w_up, preferred_element_type=jnp.float32)
    active = jax.nn.gelu(pre_act, approximate=False).astype(jnp.bfloat16)
    rows_now = lax.slice_in_dim(active, 0, local_rows * lax.axis_size("mp"), axis=0)
    ffn_out = lax.psum_scatter(
        jnp.einsum("snf,fd->snd", rows_now, w_down, preferred_element_type=jnp.float32).astype(
            jnp.bfloat16
        ),
        "mp",
        scatter_dimension=0,
        tiled=True,
    ).astype(jnp.float32)
    mixed = (middle + ffn_out).astype(jnp.bfloat16)
    grad_full = lax.all_gather(cotangent, "mp", axis=0, tiled=True)
    grad_down = jnp.einsum("snf,snd->fd", active, grad_full, preferred_element_type=jnp.float32)
    grad_act = jnp.einsum("snd,fd->snf", grad_full, w_down, preferred_element_type=jnp.float32)

    def gelu_exact(values):
        return jax.nn.gelu(values, approximate=False)

    gelu_value, gelu_pull = jax.vjp(gelu_exact, pre_act)
    grad_pre = gelu_pull(grad_act)[0].astype(jnp.bfloat16)
    grad_up = jnp.einsum("snd,snf->df", full_two, grad_pre, preferred_element_type=jnp.float32)
    rows_now = lax.slice_in_dim(grad_pre, 0, local_rows * lax.axis_size("mp"), axis=0)
    grad_norm_two = lax.psum_scatter(
        jnp.einsum("snf,df->snd", rows_now, w_up, preferred_element_type=jnp.float32).astype(
            jnp.bfloat16
        ),
        "mp",
        scatter_dimension=0,
        tiled=True,
    ).astype(jnp.float32)
    norm_value_two, norm_pull_two = jax.vjp(layer_norm, middle, gain_two, shift_two)
    grad_mid_norm, grad_gain_two, grad_shift_two = norm_pull_two(grad_norm_two)
    grad_middle = cotangent.astype(jnp.float32) + grad_mid_norm
    grad_attn_full = lax.all_gather(grad_middle.astype(jnp.bfloat16), "mp", axis=0, tiled=True)
    grad_output = jnp.einsum(
        "snw,snd->wd", context, grad_attn_full, preferred_element_type=jnp.float32
    )
    grad_context = jnp.einsum(
        "snd,wd->snw", grad_attn_full, w_output, preferred_element_type=jnp.float32
    )
    attend_value, attend_pull = jax.vjp(
        attend,
        query_rows.astype(jnp.float32),
        key_rows.astype(jnp.float32),
        value_rows.astype(jnp.float32),
    )
    grad_q_full, grad_k_full, grad_v_full = attend_pull(grad_context)
    grad_q_low = grad_q_full.astype(jnp.bfloat16)
    grad_k_low = grad_k_full.astype(jnp.bfloat16)
    grad_v_low = grad_v_full.astype(jnp.bfloat16)
    grad_query = jnp.einsum(
        "snd,snw->dw", complete_first, grad_q_low, preferred_element_type=jnp.float32
    )
    grad_key = jnp.einsum(
        "snd,snw->dw", complete_first, grad_k_low, preferred_element_type=jnp.float32
    )
    grad_value = jnp.einsum(
        "snd,snw->dw", complete_first, grad_v_low, preferred_element_type=jnp.float32
    )
    total = jnp.einsum("snw,dw->snd", grad_q_low, w_query, preferred_element_type=jnp.float32)
    total = total + jnp.einsum("snw,dw->snd", grad_k_low, w_key, preferred_element_type=jnp.float32)
    grad_norm_one = lax.psum_scatter(
        (
            total
            + jnp.einsum("snw,dw->snd", grad_v_low, w_value, preferred_element_type=jnp.float32)
        ).astype(jnp.bfloat16),
        "mp",
        scatter_dimension=0,
        tiled=True,
    ).astype(jnp.float32)
    norm_value_one, norm_pull_one = jax.vjp(layer_norm, base_rows, gain_one, shift_one)
    grad_base_norm, grad_gain_one, grad_shift_one = norm_pull_one(grad_norm_one)
    grad_tokens = grad_middle + grad_base_norm
    grad_query, grad_key, grad_value, grad_output, grad_up, grad_down = doc_sum(
        (grad_query, grad_key, grad_value, grad_output, grad_up, grad_down)
    )
    grad_gain_one, grad_shift_one, grad_gain_two, grad_shift_two = lax.psum(
        (grad_gain_one, grad_shift_one, grad_gain_two, grad_shift_two), ("dp", "mp")
    )
    return (
        mixed,
        grad_tokens,
        grad_query,
        grad_key,
        grad_value,
        grad_output,
        grad_up,
        grad_down,
        grad_gain_one,
        grad_shift_one,
        grad_gain_two,
        grad_shift_two,
    )


def solution(mesh):
    return jax.shard_map(
        per_device,
        mesh=mesh,
        in_specs=(
            P("mp", "dp", None),
            P("dp"),
            P(),
            P(),
            P(None, "mp"),
            P(None, "mp"),
            P(None, "mp"),
            P("mp", None),
            P(),
            P(),
            P(None, "mp"),
            P("mp", None),
            P("mp", "dp", None),
        ),
        out_specs=(
            P("mp", "dp", None),
            P("mp", "dp", None),
            P(None, "mp"),
            P(None, "mp"),
            P(None, "mp"),
            P("mp", None),
            P(None, "mp"),
            P("mp", None),
            P(),
            P(),
            P(),
            P(),
        ),
        check_vma=False,
    )
```

profile of v0, /device:TPU:0, one launch (start us, length us, event | category | flops | bytes accessed | tf_op | source)
XLA Modules:
  0.0 1572.6 jit_solution(14115811025590680287)
XLA Ops:
  27.3 70.7 %all-gather.5.cloned.1.call-done = bf16[2048,2,512]{2,0,1:T(8,128)(2,1)} async-done(((bf16[512,2,512]{2,0,1:T(8,128)(2,1)}), bf16[2048,2,512]{2,0,1:T(8,128)(2,1)}) %all-gather.5.cloned.1.call-update) | async-done | bytes 4194320 | tf_op jit(solution)/shard_map/all_gather | solution.py:148
  123.7 8.0 bitcast_reduce_fusion.6
  197.7 5.8 reduce_sum.951
  203.4 5.8 reduce_sum.986
  217.0 9.0 reduce_sum.944
  226.0 8.7 reduce_sum.981
  234.7 5.1 broadcast_divide_fusion.2
  246.0 5.8 reduce_sum.947
  251.8 9.2 reduce_sum.940
  283.2 5.2 fusion.366
  304.0 6.3 fusion.103
  338.8 8.4 fusion.367
  347.5 7.7 convert_reduce_fusion
  355.3 11.4 fusion.46
  375.8 11.7 fusion.67
  394.0 75.4 %reduce-scatter.5.cloned.1.call-done = bf16[512,2,512]{2,0,1:T(8,128)(2,1)} async-done(((bf16[2048,2,512]{2,0,1:T(8,128)(2,1)}), bf16[512,2,512]{2,0,1:T(8,128)(2,1)}) %reduce-scatter.5.cloned.1.call-update) | async-done | bytes 1048592 | tf_op jit(solution)/shard_map/reduce_scatter | solution.py:162
  476.8 78.9 %all-gather.7.cloned.1.call-done = bf16[2048,2,512]{2,0,1:T(8,128)(2,1)} async-done(((bf16[512,2,512]{2,0,1:T(8,128)(2,1)}), bf16[2048,2,512]{2,0,1:T(8,128)(2,1)}) %all-gather.7.cloned.1.call-update) | async-done | bytes 4194320 | tf_op jit(solution)/shard_map/all_gather | solution.py:172
  555.7 7.8 fusion.69
  566.8 20.2 %multiply_convert_fusion = (bf16[2048,2,512]{2,0,1:T(8,128)(2,1)}, f32[2048,2,512]{2,0,1:T(8,128)}) fusion(f32[2048,2,512]{2,0,1:T(8,128)S(1)} %get-tuple-element.241, u8[2048,512]{1,0:T(8,128)(4,1)S(1)} %get-tuple-element.109, u8[2048,512]{1,0:T(8,128)(4,1)S(1)} %get-tuple-element.108), kind=kLoop, calls=%fused_computation.11 | loop fusion | flops 146800640 | bytes 23068672 | tf_op jit(solution)/shard_map/convert_element_type | solution.py:174
  587.0 49.5 %all-gather.9.cloned.1.call-done = bf16[2048,2,512]{2,0,1:T(8,128)(2,1)} async-done(((bf16[512,2,512]{2,0,1:T(8,128)(2,1)}), bf16[2048,2,512]{2,0,1:T(8,128)(2,1)}) %all-gather.9.cloned.1.call-update) | async-done | bytes 4194320 | tf_op jit(solution)/shard_map/all_gather | solution.py:185
  636.5 9.7 add_convert_fusion.1
  652.7 75.4 %reduce-scatter.9.cloned.1.call-done = bf16[512,2,512]{2,0,1:T(8,128)(2,1)} async-done(((bf16[2048,2,512]{2,0,1:T(8,128)(2,1)}), bf16[512,2,512]{2,0,1:T(8,128)(2,1)}) %reduce-scatter.9.cloned.1.call-update) | async-done | bytes 1048592 | tf_op jit(solution)/shard_map/reduce_scatter | solution.py:196
  840.5 6.7 fusion.119
  861.7 19.9 %broadcast_multiply_fusion.3 = (f32[2,2048,2,64]{3,1,2,0:T(8,128)}, f32[2,2048,2,64]{3,1,2,0:T(8,128)}, f32[2,2048,2,64]{3,1,2,0:T(8,128)}, f32[2,2048,2]{1,2,0:...) fusion(f32[2,2048,2]{1,2,0:T(2,128)} %get-tuple-element.158, ...), kind=kLoop, calls=%fused_computation.163 | loop fusion | flops 10944512 | bytes 17694720 | tf_op jit(solution)/shard_map/transpose(jvp(vmap()))/mul | solution.py:93
  907.5 6.2 bitcast_reduce_fusion
  967.6 5.0 add_reduce_fusion.2
  979.8 18.3 %fusion.32 = f32[2,128,32,2,64]{4,2,3,1,0:T(8,128)} fusion(f32[2,128,2,64,16]{3,4,1,2,0:T(8,128)} %bitcast.1118, f32[2,128,2,16,32]{4,3,2,1,0:T(8,128)} %get-tuple-element.240, f32[2,128,2,16]{3,2,1,0:T(2,128)S(1)} %copy-done.52, f32[2,128,32]{2,1,0:T(8,128)S(1)} %copy-done.118), kind=kOutput, calls=%fused_computation.107 | convolution fusion | flops 201850880 | bytes 7405568 | tf_op jit(solution)/shard_map/transpose(jvp(vmap(bhqk,bkhe->bqhe)))/dot_general | solution.py:80
  998.2 16.8 %fusion.368 = (f32[2,128,2,16]{3,2,1,0:T(2,128)S(1)}, f32[2,128,2,16,32]{4,3,2,1,0:T(8,128)}) fusion(f32[2,128,2,16,32]{4,3,2,1,0:T(8,128)S(1)} %copy-done.16, f32[2,128,2,16]{3,2,1,0:T(2,128)S(1)} %copy-done.52, f32[2,128,2,16]{3,2,1,0:T(2,128)S(1)} %copy.1342, f32[2,128,16,2,64]{4,2,3,1,0:T(8,128)S(1)} %bitcast.1124, ...), kind=kOutput, calls=%fused_computation.622 | convolution fusion | flops 203677696 | bytes 8519680 | tf_op jit(solution)/shard_map/transpose(jvp(vmap(bhqk,bkhe->bqhe)))/dot_general | solution.py:80
  1015.5 13.2 fusion.49
  1028.8 10.4 convolution_bitcast_fusion
  1056.0 5.9 reduce_sum.1120
  1074.1 8.1 add_reduce_fusion.1
  1117.4 8.9 reduce_sum.1141
  1126.4 7.2 multiply_reduce_fusion.2
  1133.9 5.4 fusion.76
  1139.5 5.2 fusion.369
  1144.9 11.7 add_reduce_fusion
  1158.6 6.2 fusion.87
  1164.9 5.3 multiply_bitcast_fusion
  1258.3 5.0 broadcast_in_dim.929
  1265.9 7.5 multiply_convert_fusion.1
  1277.9 5.9 fusion.236
  1296.7 9.1 add_convert_fusion
  1306.8 6.6 convolution_convert_fusion.1
  1313.5 44.4 %all-reduce.4.cloned.1.call-done = (bf16[512,128]{1,0:T(8,128)(2,1)}, bf16[512,128]{1,0:T(8,128)(2,1)}, bf16[512,128]{1,0:T(8,128)(2,1)}, bf16[128,512]{1,0:T(8,...) async-done(((bf16[512,128]{1,0:T(8,128)(2,1)}, bf16[512,128]{1,0:T(8,128)(2,1)}, bf16[512,128]{1,0:T(8,128)(2,1)}, bf16[128,512]{1,0:T(8,128)(2,1)}, ...) | async-done | bytes 1572880 | tf_op jit(solution)/shard_map/psum | solution.py:103
  1368.9 67.2 %reduce-scatter.11.cloned.1.call-done = bf16[512,2,512]{2,0,1:T(8,128)(2,1)} async-done(((bf16[2048,2,512]{2,0,1:T(8,128)(2,1)}), bf16[512,2,512]{2,0,1:T(8,128)(2,1)}) %reduce-scatter.11.cloned.1.call-update) | async-done | bytes 1048592 | tf_op jit(solution)/shard_map/reduce_scatter | solution.py:235
  1440.7 75.1 %reduce-scatter.7.cloned.1.call-done = bf16[512,2,512]{2,0,1:T(8,128)(2,1)} async-done(((bf16[2048,2,512]{2,0,1:T(8,128)(2,1)}), bf16[512,2,512]{2,0,1:T(8,128)(2,1)}) %reduce-scatter.7.cloned.1.call-update) | async-done | bytes 1048592 | tf_op jit(solution)/shard_map/reduce_scatter | solution.py:176
  1524.8 40.8 %all-reduce = (f32[512]{0:T(512)}, f32[512]{0:T(512)}, f32[512]{0:T(512)}, f32[512]{0:T(512)}) all-reduce(f32[512]{0:T(512)S(1)} %get-tuple-element.120, f32[512]{0:T(512)S(1)} %get-tuple-element.124, f32[512]{0:T(512)S(1)} %copy-done.370, f32[512]{0:T(512)S(1)} %copy-done.369), channel_id=1, replica_groups=mesh['dp'=8,'mp'=4] {'dp','mp'}, use_global_device_ids=true, to_apply=%region_97.98 | all-reduce | flops 2048 | bytes 16384 | tf_op jit(solution)/shard_map/psum | solution.py:250
  (1266 shorter events, 635.7 us)
Async XLA Ops:
  7.2 548.5 %copy-start = (bf16[512,512]{1,0:T(8,128)(2,1)S(1)}, bf16[512,512]{1,0:T(8,128)(2,1)}, u32[]{:S(2)}) copy-start(bf16[512,512]{1,0:T(8,128)(2,1)} %param.23) | copy-start | bytes 1572868
  7.2 90.8 %copy-start.198 = (bf16[512,128]{1,0:T(8,128)(2,1)S(1)}, bf16[512,128]{1,0:T(8,128)(2,1)}, u32[]{:S(2)}) copy-start(bf16[512,128]{1,0:T(8,128)(2,1)} %param.17) | copy-start | bytes 393220
  7.2 90.8 %all-gather.5.cloned.1.call-start = ((), (), s32[]{:S(2)}) async-start(), calls=%async_computation.4 | async-start | bytes 5242880 | tf_op jit(solution)/shard_map/all_gather | solution.py:148
  14.4 454.9 %reduce-scatter.5.cloned.1.call-start = ((), (), s32[]{:S(2)}) async-start(), calls=%async_computation.5 | async-start | bytes 5242880 | tf_op jit(solution)/shard_map/reduce_scatter | solution.py:162
  14.7 179.9 %copy-start.176 = (f32[2,8,2,16]{3,2,1,0:T(2,128)}, f32[2,8,2,16]{3,2,1,0:T(2,128)S(1)}, u32[]{:S(2)}) copy-start(f32[2,8,2,16]{3,2,1,0:T(2,128)S(1)} %rev.157) | copy-start | bytes 6148
  15.3 89.4 %copy-start.267 = (f32[2,2,2,16]{3,2,1,0:T(2,128)}, f32[2,2,2,16]{3,2,1,0:T(2,128)S(1)}, u32[]{:S(2)}) copy-start(f32[2,2,2,16]{3,2,1,0:T(2,128)S(1)} %rev.161) | copy-start | bytes 1540
  15.6 89.1 %copy-start.319 = (f32[2,1,2,16]{3,2,0,1:T(2,128)}, f32[2,1,2,16]{3,2,0,1:T(2,128)S(1)}, u32[]{:S(2)}) copy-start(f32[2,1,2,16]{3,2,0,1:T(2,128)S(1)} %rev.163) | copy-start | bytes 772
  17.2 261.1 %copy-start.152 = (f32[2,16,2,16]{3,2,1,0:T(2,128)}, f32[2,16,2,16]{3,2,1,0:T(2,128)S(1)}, u32[]{:S(2)}) copy-start(f32[2,16,2,16]{3,2,1,0:T(2,128)S(1)} %rev.155) | copy-start | bytes 12292
  17.6 286.3 %copy-start.107 = (f32[2,32,2,16]{3,2,1,0:T(2,128)}, f32[2,32,2,16]{3,2,1,0:T(2,128)S(1)}, u32[]{:S(2)}) copy-start(f32[2,32,2,16]{3,2,1,0:T(2,128)S(1)} %rev.153) | copy-start | bytes 24580
  18.8 85.9 %copy-start.365 = (f32[2,128]{1,0:T(2,128)}, f32[2,128]{1,0:T(2,128)S(1)}, u32[]{:S(2)}) copy-start(f32[2,128]{1,0:T(2,128)S(1)} %get-tuple-element.198) | copy-start | bytes 3076
  19.0 158.0 %copy-start.226 = (f32[2,4,2,16]{3,2,1,0:T(2,128)}, f32[2,4,2,16]{3,2,1,0:T(2,128)S(1)}, u32[]{:S(2)}) copy-start(f32[2,4,2,16]{3,2,1,0:T(2,128)S(1)} %rev.159) | copy-start | bytes 3076
  27.3 96.3 %copy-start.265 = (f32[2,2048]{1,0:T(2,128)}, f32[2,2048]{1,0:T(2,128)S(1)}, u32[]{:S(2)}) copy-start(f32[2,2048]{1,0:T(2,128)S(1)} %compare_convert_fusion.3) | copy-start | bytes 49156
  104.7 234.1 %copy-start.12 = (bf16[2048,2,2,64]{3,0,2,1:T(8,128)(2,1)}, bf16[2048,2,2,64]{3,0,2,1:T(8,128)(2,1)S(1)}, u32[]{:S(2)}) copy-start(bf16[2048,2,2,64]{3,0,2,1:T(8,128)(2,1)S(1)} %copy.1196) | copy-start | bytes 3145732
  267.3 569.5 %copy-start.256 = (f32[2,512,2]{1,2,0:T(2,128)}, f32[2,512,2]{1,2,0:T(2,128)S(1)}, u32[]{:S(2)}) copy-start(f32[2,512,2]{1,2,0:T(2,128)S(1)} %broadcast_in_dim.769) | copy-start | bytes 24580
  389.4 80.0 %copy-start.8 = (bf16[512,2,512]{2,1,0:T(2,128)(2,1)S(1)}, bf16[512,2,512]{2,1,0:T(2,128)(2,1)}, u32[]{:S(2)}) copy-start(bf16[512,2,512]{2,1,0:T(2,128)(2,1)} %param.13) | copy-start | bytes 3145732
  393.9 78.8 %copy-start.340 = (f32[512]{0:T(512)S(1)}, f32[512]{0:T(512)}, u32[]{:S(2)}) copy-start(f32[512]{0:T(512)} %param.21) | copy-start | bytes 6148
  393.9 78.9 %copy-start.374 = (f32[512]{0:T(512)S(1)}, f32[512]{0:T(512)}, u32[]{:S(2)}) copy-start(f32[512]{0:T(512)} %param.22) | copy-start | bytes 6148
  393.9 161.8 %all-gather.7.cloned.1.call-start = ((), (), s32[]{:S(2)}) async-start(), calls=%async_computation.6 | async-start | bytes 5242880 | tf_op jit(solution)/shard_map/all_gather | solution.py:172
  470.9 263.2 %copy-start.258 = (f32[512,2]{0,1:T(2,128)}, f32[512,2]{0,1:T(2,128)S(1)}, u32[]{:S(2)}) copy-start(f32[512,2]{0,1:T(2,128)S(1)} %broadcast_multiply_fusion.12) | copy-start | bytes 12292
  472.7 261.4 %copy-start.312 = (f32[512,2]{0,1:T(2,128)}, f32[512,2]{0,1:T(2,128)S(1)}, u32[]{:S(2)}) copy-start(f32[512,2]{0,1:T(2,128)S(1)} %fusion.324) | copy-start | bytes 12292
  474.2 162.3 %all-gather.9.cloned.1.call-start = ((), (), s32[]{:S(2)}) async-start(), calls=%async_computation.8 | async-start | bytes 5242880 | tf_op jit(solution)/shard_map/all_gather | solution.py:185
  476.7 251.4 %reduce-scatter.9.cloned.1.call-start = ((), (), s32[]{:S(2)}) async-start(), calls=%async_computation.9 | async-start | bytes 5242880 | tf_op jit(solution)/shard_map/reduce_scatter | solution.py:196
  652.7 197.8 %all-gather.11.cloned.1.call-start = ((), (), s32[]{:S(2)}) async-start(), calls=%async_computation.10 | async-start | bytes 5242880 | tf_op jit(solution)/shard_map/all_gather | solution.py:207
  737.6 620.3 %all-reduce.4.cloned.1.call-start = ((), (), s32[]{:S(2)}) async-start(), calls=%async_computation.12 | async-start | bytes 3145728 | tf_op jit(solution)/shard_map/psum | solution.py:103
  881.7 32.9 %copy-start.134 = (f32[2,2048,2]{1,2,0:T(2,128)}, f32[2,2048,2]{1,2,0:T(2,128)S(1)}, u32[]{:S(2)}) copy-start(f32[2,2048,2]{1,2,0:T(2,128)S(1)} %get-tuple-element.178) | copy-start | bytes 98308
  881.7 33.7 %copy-start.136 = (f32[2,2048,2]{1,2,0:T(2,128)}, f32[2,2048,2]{1,2,0:T(2,128)S(1)}, u32[]{:S(2)}) copy-start(f32[2,2048,2]{1,2,0:T(2,128)S(1)} %get-tuple-element.179) | copy-start | bytes 98308
  881.7 34.6 %copy-start.138 = (f32[2,2048,2]{1,2,0:T(2,128)}, f32[2,2048,2]{1,2,0:T(2,128)S(1)}, u32[]{:S(2)}) copy-start(f32[2,2048,2]{1,2,0:T(2,128)S(1)} %get-tuple-element.180) | copy-start | bytes 98308
  881.7 34.7 %copy-start.140 = (f32[2,2048,2]{1,2,0:T(2,128)}, f32[2,2048,2]{1,2,0:T(2,128)S(1)}, u32[]{:S(2)}) copy-start(f32[2,2048,2]{1,2,0:T(2,128)S(1)} %get-tuple-element.181) | copy-start | bytes 98308
  881.7 34.8 %copy-start.142 = (f32[2,2048,2]{1,2,0:T(2,128)}, f32[2,2048,2]{1,2,0:T(2,128)S(1)}, u32[]{:S(2)}) copy-start(f32[2,2048,2]{1,2,0:T(2,128)S(1)} %get-tuple-element.182) | copy-start | bytes 98308
  881.7 35.0 %copy-start.144 = (f32[2,2048,2]{1,2,0:T(2,128)}, f32[2,2048,2]{1,2,0:T(2,128)S(1)}, u32[]{:S(2)}) copy-start(f32[2,2048,2]{1,2,0:T(2,128)S(1)} %get-tuple-element.183) | copy-start | bytes 98308
  881.7 35.1 %copy-start.146 = (f32[2,2048,2]{1,2,0:T(2,128)}, f32[2,2048,2]{1,2,0:T(2,128)S(1)}, u32[]{:S(2)}) copy-start(f32[2,2048,2]{1,2,0:T(2,128)S(1)} %get-tuple-element.184) | copy-start | bytes 98308
  881.8 31.9 %copy-start.148 = (f32[2,2048,2]{1,2,0:T(2,128)}, f32[2,2048,2]{1,2,0:T(2,128)S(1)}, u32[]{:S(2)}) copy-start(f32[2,2048,2]{1,2,0:T(2,128)S(1)} %neg.265) | copy-start | bytes 98308
  926.7 30.3 %copy-start.80 = (f32[2,256,8,2]{2,1,3,0:T(8,128)S(1)}, f32[2,256,8,2]{2,1,3,0:T(8,128)}, u32[]{:S(2)}) copy-start(f32[2,256,8,2]{2,1,3,0:T(8,128)} %reshape.2138) | copy-start | bytes 98308
  926.7 30.3 %copy-start.82 = (f32[2,256,8,2]{2,1,3,0:T(8,128)S(1)}, f32[2,256,8,2]{2,1,3,0:T(8,128)}, u32[]{:S(2)}) copy-start(f32[2,256,8,2]{2,1,3,0:T(8,128)} %reshape.2137) | copy-start | bytes 98308
  1296.7 139.5 %reduce-scatter.11.cloned.1.call-start = ((), (), s32[]{:S(2)}) async-start(), calls=%async_computation.11 | async-start | bytes 5242880 | tf_op jit(solution)/shard_map/reduce_scatter | solution.py:235
  1305.8 210.0 %reduce-scatter.7.cloned.1.call-start = ((), (), s32[]{:S(2)}) async-start(), calls=%async_computation.7 | async-start | bytes 5242880 | tf_op jit(solution)/shard_map/reduce_scatter | solution.py:176
  1313.5 122.7 %copy-start.9 = (bf16[512,2,512]{2,1,0:T(2,128)(2,1)S(1)}, bf16[512,2,512]{2,1,0:T(2,128)(2,1)}, u32[]{:S(2)}) copy-start(bf16[512,2,512]{2,1,0:T(2,128)(2,1)} %param.13) | copy-start | bytes 3145732
  1313.5 122.7 %copy-start.263 = (f32[512,2]{0,1:T(2,128)S(1)}, f32[512,2]{0,1:T(2,128)}, u32[]{:S(2)}) copy-start(f32[512,2]{0,1:T(2,128)} %copy-done.262) | copy-start | bytes 12292
  1313.5 122.7 %copy-start.355 = (f32[512]{0:T(512)S(1)}, f32[512]{0:T(512)}, u32[]{:S(2)}) copy-start(f32[512]{0:T(512)} %param.15) | copy-start | bytes 6148
  1313.5 124.8 %copy-start.345 = (f32[512,2]{0,1:T(2,128)S(1)}, f32[512,2]{0,1:T(2,128)}, u32[]{:S(2)}) copy-start(f32[512,2]{0,1:T(2,128)} %copy-done.344) | copy-start | bytes 12292
  1313.5 124.8 %copy-start.331 = (f32[512,2]{0,1:T(2,128)S(1)}, f32[512,2]{0,1:T(2,128)}, u32[]{:S(2)}) copy-start(f32[512,2]{0,1:T(2,128)} %copy-done.330) | copy-start | bytes 12292
  1359.5 156.3 %copy-start.19 = (bf16[512,2,512]{2,0,1:T(8,128)(2,1)S(1)}, bf16[512,2,512]{2,0,1:T(8,128)(2,1)}, u32[]{:S(2)}) copy-start(bf16[512,2,512]{2,0,1:T(8,128)(2,1)} %reduce-scatter.5.cloned.1.call-done) | copy-start | bytes 3145732
  1359.5 156.3 %copy-start.259 = (f32[512,2]{0,1:T(2,128)S(1)}, f32[512,2]{0,1:T(2,128)}, u32[]{:S(2)}) copy-start(f32[512,2]{0,1:T(2,128)} %copy-done.258) | copy-start | bytes 12292
  1359.5 156.3 %copy-start.313 = (f32[512,2]{0,1:T(2,128)S(1)}, f32[512,2]{0,1:T(2,128)}, u32[]{:S(2)}) copy-start(f32[512,2]{0,1:T(2,128)} %copy-done.312) | copy-start | bytes 12292
  1359.5 156.3 %copy-start.328 = (f32[512,2]{0,1:T(2,128)S(1)}, f32[512,2]{0,1:T(2,128)}, u32[]{:S(2)}) copy-start(f32[512,2]{0,1:T(2,128)} %copy-done.327) | copy-start | bytes 12292
  1359.5 156.3 %copy-start.341 = (f32[512]{0:T(512)S(1)}, f32[512]{0:T(512)}, u32[]{:S(2)}) copy-start(f32[512]{0:T(512)} %param.21) | copy-start | bytes 6148
  1359.5 156.3 %copy-start.343 = (f32[512,2]{0,1:T(2,128)S(1)}, f32[512,2]{0,1:T(2,128)}, u32[]{:S(2)}) copy-start(f32[512,2]{0,1:T(2,128)} %copy-done.342) | copy-start | bytes 12292
  1515.8 49.8 %copy-start.1 = (bf16[512,512]{1,0:T(8,128)(2,1)S(1)}, bf16[512,512]{1,0:T(8,128)(2,1)}, u32[]{:S(2)}) copy-start(bf16[512,512]{1,0:T(8,128)(2,1)} %param.23) | copy-start | bytes 1572868
  (339 other events, 3235.6 us)
Sparse Core Ops, SparseCore 0:
  14.5 83.4 all-gather.4
  394.0 75.2 reduce-scatter.4
  474.4 81.2 all-gather.6
  557.2 79.2 all-gather.8
  652.8 75.2 reduce-scatter.8
  737.7 81.2 all-gather.10
  1296.8 61.0 all-reduce.3
  1360.3 75.8 reduce-scatter.10
  1438.5 77.2 reduce-scatter.6
where the time goes:
time: 1590 us; the launch traced here: 1570 us
  waiting for transfers between devices  537 us (34%)
  local copies, waits for them, and re-layouts  392 us (25%)
  other arithmetic  330 us (21%)
  matrix products  253 us (16%)
  blocking collectives  40.8 us (3%)
  between operations  19.2 us (1%)
    dot_general x21, matrix products, hier_attend(): jnp.einsum('bhqk,bkhe->bqhe', weight, value_set, precision=lax.Precision....  91.4 us
    reshape x60, local copies, waits for them, and re-layouts, upsample(): return wide.reshape((array.shape[0] * stride,) + array.shape[1:])  86.8 us
    all_gather x1, waiting for transfers between devices, per_device(): full_two = lax.all_gather(normed_two, 'mp', axis=0, tiled=True)  78.9 us
    reduce_sum x17, other arithmetic, upsample(): jnp.broadcast_to(array[:, None], (array.shape[0], stride) + array.shape[1:])  78.3 us
    dot_general x21, matrix products, hier_attend(): jnp.einsum('bqhe,bkhe->bhqk', query_blocks, key_set, precision=lax.Precis...  76.5 us
    reduce_scatter x1, waiting for transfers between devices, per_device(): lax.psum_scatter(jnp.einsum('snf,df->snd', rows_now, w_up, preferred_elem...  75.4 us
    reduce_scatter x1, waiting for transfers between devices, per_device(): lax.psum_scatter(jnp.einsum('snw,wd->snd', rows_now, w_output, preferred_...  75.4 us
    reduce_scatter x1, waiting for transfers between devices, per_device(): lax.psum_scatter(jnp.einsum('snf,fd->snd', rows_now, w_down, preferred_el...  75.1 us
  transfers between devices with their start and end apart: 9, of which 8 were waited for; matrix products, arithmetic and copies ran while one was open for 12% of the time, Pallas kernels for 0%

commit v1 on v0

v1 whole, which is shorter than its diff:
```python
import types

import jax
import jax.numpy as jnp
from jax import lax
from jax.experimental import pallas as pl
from jax.experimental.pallas import tpu as pltpu
from jax.sharding import PartitionSpec as P

HD = 64
BLK = 16
NEG = -1e30
FLOOR = -1e29
EPS = 1e-05
LOC = 512
ND = 2
D = 512
FF = 2048
NMP = 4
T = ND * LOC
HEADS = D // HD
LEVELS = 7
LOCAL_LEVELS = 5
EXT = 1024
RT = 256
G = [LOC >> lev for lev in range(LEVELS)]
OFF = [sum(G[:lev]) for lev in range(LEVELS)]
bf16 = jnp.bfloat16
f32 = jnp.float32
i32 = jnp.int32


def dot(a, b, ca=1, cb=0):
    return lax.dot_general(a, b, (((ca,), (cb,)), ((), ())), preferred_element_type=f32)


def iota(shape, axis):
    return lax.broadcasted_iota(i32, shape, axis)


def loop(n, body):
    lax.fori_loop(0, n, lambda i, c: (body(i), c)[1], 0)


def rows_at(i, size):
    return pl.ds(pl.multiple_of(i * size, size), size)


def own_groups(e):
    size = jnp.zeros_like(e)
    start = jnp.zeros_like(e)
    for lev in range(LEVELS):
        here = (e >= OFF[lev]) & (e < OFF[lev] + G[lev])
        size = jnp.where(here, 1 << lev, size)
        start = jnp.where(here, (e - OFF[lev]) << lev, start)
    return size, start


def key_groups(e, z):
    size, start = own_groups(e)
    start = start + z * LOC
    near = z + 1 - 2 * lax.rem(z, 2)
    far = 1 - z // 2
    size = jnp.where(e >= OFF[5], 32, size)
    start = jnp.where(e >= OFF[5], near * LOC + (e - OFF[5]) * 32, start)
    size = jnp.where(e >= OFF[6], 64, size)
    start = jnp.where(e >= OFF[6], far * 2 * LOC + (e - OFF[6]) * 64, start)
    return size, start


def count_live(size, start, length):
    return jnp.clip(length - start, 0, size).astype(f32)


def build_tables(r, z):
    for d in range(ND):
        length = r.lens[d]

        def chunk(c, d=d, length=length):
            at = pl.ds(pl.multiple_of(d * EXT + c * 128, 128), 128)
            e_col = iota((128, 128), 0) + c * 128
            size, start = key_groups(e_col, z)
            r.cc[at, :] = count_live(size, start, length).astype(bf16)
            e_row = iota((1, 128), 1) + c * 128
            size, start = key_groups(e_row, z)
            dead = count_live(size, start, length)
            q_blk, k_blk = e_col // BLK, jnp.broadcast_to(e_row // BLK, (128, 128))
            span = jnp.where(q_blk // 2 == k_blk // 2, 0.0, NEG)
            same = jnp.where(q_blk == k_blk, 0.0, NEG)
            cross = jnp.where(q_blk == k_blk, NEG, span)
            bias = jnp.where(e_col < LOC, span, jnp.where(e_col < OFF[5], cross, same))
            r.bias[at, :] = jnp.where(jnp.broadcast_to(dead, (128, 128)) > 0.0, bias, NEG)

        loop(EXT // 128, chunk)


def build_maps(r):
    def tile(c):
        rows = rows_at(c, 128)
        size, start = own_groups(iota((128, LOC), 0) + c * 128 + LOC)
        pos = iota((128, LOC), 1)
        r.pool[rows, :] = ((pos >= start) & (pos < start + size)).astype(f32).astype(bf16)
        size, start = own_groups(iota((128, EXT - LOC), 1) + LOC)
        pos = iota((128, EXT - LOC), 0) + c * 128
        r.unpool[rows, :] = ((pos >= start) & (pos < start + size)).astype(f32).astype(bf16)

    loop((EXT - LOC) // 128, tile)


def inv_counts(r, z, d):
    e = iota((EXT - LOC, 128), 0) + LOC
    size, start = own_groups(e)
    cnt = count_live(size, start + z * LOC, r.lens[d])
    return 1.0 / jnp.maximum(cnt, 1.0), 1.0 / jnp.maximum(size, 1).astype(f32)


def wide(col):
    return jnp.concatenate([col] * (D // 128), axis=1)


def live_rows(r, z, d, first, count):
    pos = iota((count, D), 0) + first + z * LOC
    return pos < r.lens[d]


def stats(v):
    mean = jnp.mean(v, axis=-1, keepdims=True)
    cen = v - mean
    var = jnp.mean(cen * cen, axis=-1, keepdims=True)
    return cen, lax.rsqrt(var + EPS)


def norm_one(r):
    def tile(t):
        rows = rows_at(t, RT)
        cen, rstd = stats(r.x[rows, :].astype(f32))
        r.h1[rows, :] = (cen * rstd * r.g1[...] + r.b1[...]).astype(bf16)

    loop(T // RT, tile)


def ext_rows(d, off, count):
    return pl.ds(d * EXT + off, count)


def project(r, z):
    per = LOC // RT
    for d in range(ND):

        def tile(t, d=d):
            rows = pl.ds(pl.multiple_of(d * LOC + t * RT, RT), RT)
            at = pl.ds(pl.multiple_of(d * EXT + t * RT, RT), RT)
            h = r.h1[rows, :]
            live = live_rows(r, z, d, t * RT, RT)
            q = dot(h, r.wqkv[:, 0:D]).astype(bf16).astype(f32)
            r.qe[at, :] = (q * (HD**-0.5)).astype(bf16)
            k = dot(h, r.wqkv[:, D : 2 * D])
            r.ke[at, :] = jnp.where(live, k, 0.0).astype(bf16)
            v = dot(h, r.wqkv[:, 2 * D : 3 * D])
            r.ve[at, :] = jnp.where(live, v, 0.0).astype(bf16)

        loop(per, tile)


def pool_levels(r, z):
    keep = OFF[5] - LOC
    for d in range(ND):
        inv, inv_size = inv_counts(r, z, d)
        fine = ext_rows(d, 0, LOC)
        coarse = ext_rows(d, LOC, LOC)
        r.qe[coarse, :] = (dot(r.pool[...], r.qe[fine, :]) * wide(inv_size)).astype(bf16)
        k = dot(r.pool[...], r.ke[fine, :]) * wide(inv)
        v = dot(r.pool[...], r.ve[fine, :])
        r.ke[ext_rows(d, LOC, keep), :] = k[:keep].astype(bf16)
        r.ve[ext_rows(d, LOC, keep), :] = v[:keep].astype(bf16)
        r.sums[pl.ds(d * 48, 24), :] = k[keep : keep + 24]
        r.sums[pl.ds(d * 48 + 24, 24), :] = v[keep : keep + 24]


def place_remote(r):
    for d in range(ND):
        r.ke[ext_rows(d, OFF[5], 32), :] = r.rem[pl.ds(d * 64, 32), :].astype(bf16)
        r.ve[ext_rows(d, OFF[5], 32), :] = r.rem[pl.ds(d * 64 + 32, 32), :].astype(bf16)


def split_heads(pair):
    first = iota(pair.shape, 1) < HD
    zero = jnp.zeros_like(pair)
    return jnp.concatenate([jnp.where(first, pair, zero), jnp.where(first, zero, pair)], axis=0)


def count_lanes(cc, d, p):
    lane = iota(cc.shape, 1)
    zero = jnp.zeros_like(cc)
    a = jnp.where(lane == d * HEADS + 2 * p, cc, zero)
    b = jnp.where(lane == d * HEADS + 2 * p + 1, cc, zero)
    return jnp.concatenate([a, b], axis=0)


def attend_chunk(r, c):
    lane = iota((128, 128), 1)
    tops = jnp.zeros((128, 128), f32)
    sums = jnp.zeros((128, 128), f32)
    for d in range(ND):
        at = pl.ds(pl.multiple_of(d * EXT + c * 128, 128), 128)
        bias = r.bias[at, :]
        cc = r.cc[at, :]
        for p in range(HEADS // 2):
            lanes = pl.ds(p * 128, 128)
            s = dot(r.qe[at, lanes], split_heads(r.ke[at, lanes]), 1, 1)
            parts = []
            for j in range(2):
                sj = s[:, j * 128 : (j + 1) * 128] + bias
                top = jnp.maximum(jnp.max(sj, axis=1, keepdims=True), FLOOR)
                parts.append(jnp.exp(sj - top))
                tops = jnp.where(lane == d * HEADS + 2 * p + j, top, tops)
            e = jnp.concatenate(parts, axis=1).astype(bf16)
            slot = pl.ds(pl.multiple_of(((c * ND + d) * 4 + p) * 128, 128), 128)
            r.wts[slot, :] = e
            vo = jnp.concatenate([split_heads(r.ve[at, lanes]), count_lanes(cc, d, p)], axis=1)
            o = dot(e, vo)
            r.num[at, lanes] = o[:, :128]
            sums = sums + o[:, 128:]
    here = rows_at(c, 128)
    r.tops[here, :] = tops
    r.sumz[here, :] = sums


def combine_sums(r):
    last = pl.ds(OFF[6], G[6])
    top = r.tops[last, :]
    tot = r.sumz[last, :]
    for lev in range(LEVELS - 2, -1, -1):
        n = G[lev]
        for half in range(2):
            r.up[pl.ds(half, n // 2, stride=2), :] = top
            r.up2[pl.ds(half, n // 2, stride=2), :] = tot
        at = pl.ds(OFF[lev], n)
        up_top = r.up[pl.ds(0, n), :]
        own = r.tops[at, :]
        top = jnp.maximum(own, up_top)
        a = jnp.exp(own - top)
        b = jnp.exp(up_top - top)
        tot = a * r.sumz[at, :] + b * r.up2[pl.ds(0, n), :]
        if lev == 0:
            used = iota(tot.shape, 1) < ND * HEADS
            inv = 1.0 / jnp.where(used, tot, 1.0)
            a, b = a * inv, b * inv
        r.fa[at, :] = a
        r.fb[at, :] = b


def spread(fac, d):
    hi = fac.astype(bf16)
    lo = (fac - hi.astype(f32)).astype(bf16)
    row = lax.rem(iota((256, D), 0), 128)
    sel = (row == d * HEADS + iota((256, D), 1) // HD).astype(f32).astype(bf16)
    return dot(jnp.concatenate([hi, lo], axis=1), sel)


def up_map(n):
    return (iota((n, n // 2), 0) // 2 == iota((n, n // 2), 1)).astype(f32).astype(bf16)


def combine_values(r):
    for d in range(ND):
        cur = r.num[ext_rows(d, OFF[6], G[6]), :]
        for lev in range(LEVELS - 2, -1, -1):
            n = G[lev]
            low = cur.astype(bf16)
            parts = []
            step = min(n, 128)
            for t in range(n // step):
                at = pl.ds(OFF[lev] + t * step, step)
                own = spread(r.fa[at, :], d) * r.num[ext_rows(d, OFF[lev] + t * step, step), :]
                up = dot(up_map(step), low[t * step // 2 : (t + 1) * step // 2])
                parts.append(own + spread(r.fb[at, :], d) * up)
                if lev == 0:
                    r.ctx[pl.ds(d * LOC + t * step, step), :] = parts[-1].astype(bf16)
            cur = jnp.concatenate(parts, axis=0) if len(parts) > 1 else parts[0]


def attn_out(r):
    def tile(t):
        rows = rows_at(t, RT)
        mid = r.x[rows, :].astype(f32) + dot(r.ctx[rows, :], r.wo[...])
        r.mid[rows, :] = mid
        cen, rstd = stats(mid)
        r.h2[rows, :] = (cen * rstd * r.g2[...] + r.b2[...]).astype(bf16)

    loop(T // RT, tile)


def ffn_inner(r):
    def step(i):
        f, t = i // (T // RT), lax.rem(i, T // RT)
        rows = rows_at(t, RT)
        cols = rows_at(f, 512)
        pre = dot(r.h2[rows, :], r.wup[:, cols])
        ga = dot(r.gy[rows, :], r.wdn[cols, :], 1, 1)
        cdf = 0.5 + 0.5 * lax.erf(pre * (0.5**0.5))
        r.act[rows, cols] = (pre * cdf).astype(bf16)
        pdf = jnp.exp(pre * pre * -0.5) * 0.3989422804014327
        r.gp[rows, cols] = (ga * (cdf + pre * pdf)).astype(bf16)

    loop((FF // 512) * (T // RT), step)


def ffn_grads(r):
    def tile(f):
        cols = rows_at(f, 512)
        r.gdn[cols, :] = dot(r.act[:, cols], r.gy[...], 0, 0).astype(r.gdn.dtype)
        r.gup[:, cols] = dot(r.h2[...], r.gp[:, cols], 0, 0).astype(r.gup.dtype)

    loop(FF // 512, tile)


def norm_back(v, gain, gh, g_gain, g_shift):
    cen, rstd = stats(v)
    xhat = cen * rstd
    g_gain[...] += jnp.sum(gh * xhat, axis=0, keepdims=True)
    g_shift[...] += jnp.sum(gh, axis=0, keepdims=True)
    u = gh * gain
    return rstd * (
        u - jnp.mean(u, axis=-1, keepdims=True) - xhat * jnp.mean(u * xhat, axis=-1, keepdims=True)
    )


def ffn_outer(r):
    r.gg2[...] = jnp.zeros_like(r.gg2)
    r.gb2[...] = jnp.zeros_like(r.gb2)

    def tile(t):
        rows = rows_at(t, RT)
        mid = r.mid[rows, :]
        r.mixed[rows, :] = (mid + dot(r.act[rows, :], r.wdn[...])).astype(bf16)
        gh2 = dot(r.gp[rows, :], r.wup[...], 1, 1)
        g_mid = r.gy[rows, :].astype(f32) + norm_back(mid, r.g2[...], gh2, r.gg2, r.gb2)
        r.gmid[rows, :] = g_mid
        r.gm[rows, :] = g_mid.astype(bf16)

    loop(T // RT, tile)


def out_grads(r):
    r.gwo[...] = dot(r.ctx[...], r.gm[...], 0, 0).astype(r.gwo.dtype)


def attn_back_rows(r):
    lane_head = iota((D, 128), 0) // HD
    for t in range(LOC // 128):
        at = pl.ds(t * 128, 128)
        delta = jnp.zeros((128, 128), f32)
        for d in range(ND):
            rows = pl.ds(d * LOC + t * 128, 128)
            gctx = dot(r.gm[rows, :], r.wo[...], 1, 1)
            sel = (lane_head + d * HEADS == iota((D, 128), 1)).astype(f32).astype(bf16)
            delta = delta + dot((gctx * r.ctx[rows, :].astype(f32)).astype(bf16), sel)
            r.ge[ext_rows(d, t * 128, 128), :] = (spread(r.fa[at, :], d) * gctx).astype(bf16)
            down = (spread(r.fb[at, :], d) * gctx).astype(bf16)
            r.hc[pl.ds(d * LOC // 2 + t * 64, 64), :] = dot(up_map(128), down, 0, 0)
        r.dl[at, :] = (r.fa[at, :] * -delta).astype(bf16)
        r.up[at, :] = r.fb[at, :] * -delta
    acc = r.up[pl.ds(0, LOC // 2, stride=2), :] + r.up[pl.ds(1, LOC // 2, stride=2), :]
    for lev in range(1, LEVELS - 1):
        n = G[lev]
        at = pl.ds(OFF[lev], n)
        r.dl[at, :] = (r.fa[at, :] * acc).astype(bf16)
        r.up[pl.ds(0, n), :] = r.fb[at, :] * acc
        acc = r.up[pl.ds(0, n // 2, stride=2), :] + r.up[pl.ds(1, n // 2, stride=2), :]
    r.dl[pl.ds(OFF[6], 2 * G[6]), :] = jnp.concatenate([acc, jnp.zeros_like(acc)], 0).astype(bf16)
    for d in range(ND):
        cur = r.hc[pl.ds(d * LOC // 2, LOC // 2), :]
        for lev in range(1, LEVELS - 1):
            n = G[lev]
            parts = []
            step = min(n, 128)
            for t in range(n // step):
                at = pl.ds(OFF[lev] + t * step, step)
                seg = cur[t * step : (t + 1) * step]
                own = spread(r.fa[at, :], d) * seg
                r.ge[ext_rows(d, OFF[lev] + t * step, step), :] = own.astype(bf16)
                down = (spread(r.fb[at, :], d) * seg).astype(bf16)
                parts.append(dot(up_map(step), down, 0, 0))
            cur = jnp.concatenate(parts, axis=0) if len(parts) > 1 else parts[0]
        tail = jnp.concatenate([cur, jnp.zeros_like(cur)], axis=0)
        r.ge[ext_rows(d, OFF[6], 2 * G[6]), :] = tail.astype(bf16)


def attend_back_chunk(r, c):
    first = iota((128, 128), 1) < HD
    dl = r.dl[rows_at(c, 128), :]
    for d in range(ND):
        at = pl.ds(pl.multiple_of(d * EXT + c * 128, 128), 128)
        cc = r.cc[at, :]
        for p in range(HEADS // 2):
            lanes = pl.ds(p * 128, 128)
            g = r.ge[at, lanes]
            q = r.qe[at, lanes]
            kcat = split_heads(r.ke[at, lanes])
            vo = jnp.concatenate([split_heads(r.ve[at, lanes]), count_lanes(cc, d, p)], axis=1)
            dp = dot(jnp.concatenate([g, dl], axis=1), vo, 1, 1)
            slot = pl.ds(pl.multiple_of(((c * ND + d) * 4 + p) * 128, 128), 128)
            e = r.wts[slot, :]
            ds = (e.astype(f32) * dp).astype(bf16)
            r.dqe[at, lanes] = dot(ds, kcat).astype(bf16)
            dk = dot(ds, q, 0, 0)
            r.dke[at, lanes] = jnp.where(first, dk[:128], dk[128:]).astype(bf16)
            dv = dot(e, g, 0, 0)
            r.dve[at, lanes] = jnp.where(first, dv[:128], dv[128:]).astype(bf16)


def save_remote(r):
    for d in range(ND):
        r.back[pl.ds(d * 64, 32), :] = r.dke[ext_rows(d, OFF[5], 32), :].astype(f32)
        r.back[pl.ds(d * 64 + 32, 32), :] = r.dve[ext_rows(d, OFF[5], 32), :].astype(f32)


def unpool_levels(r, z):
    keep = OFF[5] - LOC
    zeros = jnp.zeros((LOC - keep - 24, D), f32)
    for d in range(ND):
        inv, inv_size = inv_counts(r, z, d)
        fine = ext_rows(d, 0, LOC)
        rows = pl.ds(d * LOC, LOC)
        live = live_rows(r, z, d, 0, LOC)
        q = (r.dqe[ext_rows(d, LOC, LOC), :].astype(f32) * wide(inv_size)).astype(bf16)
        q = r.dqe[fine, :].astype(f32) + dot(r.unpool[...], q)
        r.gqkv[rows, 0:D] = (q * (HD**-0.5)).astype(bf16)
        own = r.dke[ext_rows(d, LOC, keep), :].astype(f32)
        k = jnp.concatenate([own, r.cg[pl.ds(d * 48, 24), :], zeros], axis=0)
        k = (k * wide(inv)).astype(bf16)
        k = r.dke[fine, :].astype(f32) + dot(r.unpool[...], k)
        r.gqkv[rows, D : 2 * D] = jnp.where(live, k, 0.0).astype(bf16)
        own = r.dve[ext_rows(d, LOC, keep), :].astype(f32)
        v = jnp.concatenate([own, r.cg[pl.ds(d * 48 + 24, 24), :], zeros], axis=0).astype(bf16)
        v = r.dve[fine, :].astype(f32) + dot(r.unpool[...], v)
        r.gqkv[rows, 2 * D : 3 * D] = jnp.where(live, v, 0.0).astype(bf16)


def qkv_grads(r):
    def tile(i):
        cols = rows_at(i, 512)
        r.gwqkv[:, cols] = dot(r.h1[...], r.gqkv[:, cols], 0, 0).astype(r.gwqkv.dtype)

    loop(3, tile)


def input_grads(r):
    r.gg1[...] = jnp.zeros_like(r.gg1)
    r.gb1[...] = jnp.zeros_like(r.gb1)

    def tile(t):
        rows = rows_at(t, RT)
        gh1 = dot(r.gqkv[rows, :], r.wqkv[...], 1, 1)
        x = r.x[rows, :].astype(f32)
        r.gx[rows, :] = r.gmid[rows, :] + norm_back(x, r.g1[...], gh1, r.gg1, r.gb1)

    loop(T // RT, tile)


def first_kernel(r):
    z = lax.axis_index("mp")
    build_maps(r)
    norm_one(r)
    project(r, z)
    pool_levels(r, z)


def second_kernel(r):
    z = lax.axis_index("mp")
    build_tables(r, z)
    loop(EXT // 128, lambda c: attend_chunk(r, c))
    combine_sums(r)
    combine_values(r)
    attn_out(r)
    ffn_inner(r)
    ffn_grads(r)
    ffn_outer(r)
    out_grads(r)
    attn_back_rows(r)
    loop(EXT // 128, lambda c: attend_back_chunk(r, c))
    save_remote(r)


def third_kernel(r):
    z = lax.axis_index("mp")
    build_maps(r)
    unpool_levels(r, z)
    qkv_grads(r)
    input_grads(r)


def run(body, ins, outs, scratch):
    names = list(ins) + list(outs) + list(scratch)

    def kernel(*refs):
        body(types.SimpleNamespace(**dict(zip(names, refs))))

    vmem = pl.BlockSpec(memory_space=pltpu.VMEM)
    smem = pl.BlockSpec(memory_space=pltpu.SMEM)
    result = pl.pallas_call(
        kernel,
        out_shape=[jax.ShapeDtypeStruct(*v) for v in outs.values()],
        in_specs=[smem if n == "lens" else vmem for n in ins],
        out_specs=[vmem] * len(outs),
        scratch_shapes=[pltpu.VMEM(*v) for v in scratch.values()],
        compiler_params=pltpu.CompilerParams(vmem_limit_bytes=60 * 1024 * 1024),
    )(*ins.values())
    return dict(zip(outs, result))


def gather_columns(w):
    full = lax.all_gather(w, "mp", axis=0)
    return jnp.moveaxis(full, 0, 1).reshape(w.shape[0], -1)


def per_device(
    tokens,
    lengths,
    gain_one,
    shift_one,
    w_query,
    w_key,
    w_value,
    w_output,
    gain_two,
    shift_two,
    w_up,
    w_down,
    cotangent,
):
    z = lax.axis_index("mp")
    x = jnp.swapaxes(tokens, 0, 1).reshape(T, D)
    gy = jnp.swapaxes(cotangent, 0, 1).reshape(T, D)
    g1, b1, g2, b2 = (v.reshape(1, D) for v in (gain_one, shift_one, gain_two, shift_two))
    wqkv = jnp.concatenate([gather_columns(w) for w in (w_query, w_key, w_value)], axis=1)
    wo = lax.all_gather(w_output, "mp", axis=0, tiled=True)
    wup = gather_columns(w_up)
    wdn = lax.all_gather(w_down, "mp", axis=0, tiled=True)
    one = run(
        first_kernel,
        dict(lens=lengths, x=x, g1=g1, b1=b1, wqkv=wqkv),
        dict(
            h1=((T, D), bf16),
            qe=((ND * EXT, D), bf16),
            ke=((ND * EXT, D), bf16),
            ve=((ND * EXT, D), bf16),
            sums=((ND * 48, D), f32),
        ),
        dict(pool=((EXT - LOC, LOC), bf16), unpool=((LOC, EXT - LOC), bf16)),
    )
    everyone = lax.all_gather(one["sums"].reshape(ND, 2, 24, D), "mp", axis=0)
    near = z + 1 - 2 * (z % 2)
    far = (1 - z // 2) * 2

    def pick(i):
        return lax.dynamic_index_in_dim(everyone, i, 0, keepdims=False)

    rem = jnp.concatenate(
        [pick(near)[:, :, :16], pick(far)[:, :, 16:], pick(far + 1)[:, :, 16:]], axis=2
    )
    rem3 = rem.astype(bf16)
    ke = one["ke"].reshape(ND, EXT, D).at[:, OFF[5] :].set(rem3[:, 0]).reshape(ND * EXT, D)
    ve = one["ve"].reshape(ND, EXT, D).at[:, OFF[5] :].set(rem3[:, 1]).reshape(ND * EXT, D)
    two = run(
        second_kernel,
        dict(
            lens=lengths, x=x, gy=gy, g2=g2, b2=b2, qe=one["qe"], ke=ke, ve=ve,
            wo=wo, wup=wup, wdn=wdn,
        ),
        dict(
            mixed=((T, D), bf16),
            gmid=((T, D), f32),
            dqe=((ND * EXT, D), bf16),
            dke=((ND * EXT, D), bf16),
            dve=((ND * EXT, D), bf16),
            back=((ND * 64, D), f32),
            gwo=((D, D), bf16),
            gup=((D, FF), bf16),
            gdn=((FF, D), bf16),
            gg2=((1, D), f32),
            gb2=((1, D), f32),
        ),
        dict(
            cc=((ND * EXT, 128), bf16),
            bias=((ND * EXT, 128), f32),
            wts=((64 * 128, 256), bf16),
            num=((ND * EXT, D), f32),
            tops=((EXT, 128), f32),
            sumz=((EXT, 128), f32),
            up=((LOC, 128), f32),
            up2=((LOC, 128), f32),
            fa=((EXT, 128), f32),
            fb=((EXT, 128), f32),
            ctx=((T, D), bf16),
            mid=((T, D), f32),
            h2=((T, D), bf16),
            act=((T, FF), bf16),
            gp=((T, FF), bf16),
            gm=((T, D), bf16),
            ge=((ND * EXT, D), bf16),
            hc=((T // 2, D), f32),
            dl=((EXT, 128), bf16),
        ),
    )
    backs = lax.all_gather(two["back"].reshape(ND, 2, 32, D), "mp", axis=0)

    def pick_back(i, first, count):
        return lax.dynamic_index_in_dim(backs, i, 0, keepdims=False)[:, :, first : first + count]

    mine = z % 2
    from_far = [
        jnp.where(mine == 0, pick_back(far + j, 16, 8), pick_back(far + j, 24, 8)) for j in range(2)
    ]
    cg = jnp.concatenate([pick_back(near, 0, 16), from_far[0] + from_far[1]], axis=2)
    three = run(
        third_kernel,
        dict(
            lens=lengths, x=x, g1=g1, b1=b1, h1=one["h1"], wqkv=wqkv, gmid=two["gmid"],
            dqe=two["dqe"], dke=two["dke"], dve=two["dve"], cg=cg.reshape(ND * 48, D),
        ),
        dict(
            gx=((T, D), f32),
            gwqkv=((D, 3 * D), bf16),
            gg1=((1, D), f32),
            gb1=((1, D), f32),
        ),
        dict(
            pool=((EXT - LOC, LOC), bf16),
            unpool=((LOC, EXT - LOC), bf16),
            gqkv=((T, 3 * D), bf16),
        ),
    )

    def scatter(g, axis):
        part = lax.psum_scatter(g, "mp", scatter_dimension=axis, tiled=True)
        return lax.psum(part, "dp").astype(f32)

    gw = three["gwqkv"]
    norms = lax.psum((three["gg1"], three["gb1"], two["gg2"], two["gb2"]), ("dp", "mp"))

    def back_to(a):
        return jnp.swapaxes(a.reshape(ND, LOC, D), 0, 1)

    return (
        back_to(two["mixed"]),
        back_to(three["gx"]),
        scatter(gw[:, :D], 1),
        scatter(gw[:, D : 2 * D], 1),
        scatter(gw[:, 2 * D :], 1),
        scatter(two["gwo"], 0),
        scatter(two["gup"], 1),
        scatter(two["gdn"], 0),
        *(v.reshape(D) for v in norms),
    )


def solution(mesh):
    tok = P("mp", "dp", None)
    col, row, rep = P(None, "mp"), P("mp", None), P()
    return jax.shard_map(
        per_device,
        mesh=mesh,
        in_specs=(tok, P("dp"), rep, rep, col, col, col, row, rep, rep, col, row, tok),
        out_specs=(tok, tok, col, col, col, row, col, row, rep, rep, rep, rep),
        check_vma=False,
    )
```

time: 1590 us -> 510 us (0.32); the launches traced: 1570 us -> 509 us
  local copies, waits for them, and re-layouts: 392 us -> 26.6 us
  other arithmetic: 330 us -> 11.5 us
  waiting for transfers between devices: 537 us -> 223 us
  matrix products: 253 us -> 0 us
  blocking collectives: 40.8 us -> 143 us
  Pallas kernels: 0 us -> 90.8 us
    dot_general x60 -> x0, matrix products: 253 us -> none  [the longest x21 91.4 us: hier_attend(): jnp.einsum('bhqk,bkhe->bqhe', weight, value_set, precision=lax.Precision....]
    reduce_sum x51 -> x0, other arithmetic: 183 us -> none  [the longest x17 78.3 us: upsample(): jnp.broadcast_to(array[:, None], (array.shape[0], stride) + array.shape[1:])]
    reduce_scatter x4 -> x3, waiting for transfers between devices: 293 us -> 111 us  [scatter(): part = lax.psum_scatter(g, 'mp', scatter_dimension=axis, tiled=True)]
    all_gather x4 -> x3, waiting for transfers between devices: 199 us -> 30.4 us  [the longest x1 27.1 us: per_device(): backs = lax.all_gather(two['back'].reshape(ND, 2, 32, D), 'mp', axis=0)]
    all_gather x0 -> x5, blocking collectives: none -> 103 us  [the longest x3 64.1 us: gather_columns(): full = lax.all_gather(w, 'mp', axis=0)]
    reshape x91 -> x2, local copies, waits for them, and re-layouts: 107 us -> 4.99 us  [back_to(): return jnp.swapaxes(a.reshape(ND, LOC, D), 0, 1)]
    pallas_call x0 -> x3, Pallas kernels: none -> 90.8 us  [run(): pl.pallas_call(kernel, out_shape=[jax.ShapeDtypeStruct(*v) for v in outs....]
    reduce_sum x52 -> x0, local copies, waits for them, and re-layouts: 67.2 us -> none  [the longest x49 65.7 us: hier_attend(): total_num = total_num + row_nums[level_idx] * factor[..., None]]
  transfers between devices with their start and end apart: 9 -> 10, of which waited for: 8 -> 9; matrix products, arithmetic and copies ran while one was open for 12% -> 4% of each run, Pallas kernels for 0% -> 2%
where the time goes in v1:
time: 510 us; the launch traced here: 509 us
  waiting for transfers between devices  223 us (44%)
  blocking collectives  143 us (28%)
  Pallas kernels  90.8 us (18%)
  local copies, waits for them, and re-layouts  26.6 us (5%)
  between operations  14.5 us (3%)
  other arithmetic  11.5 us (2%)
    reduce_scatter x3, waiting for transfers between devices, scatter(): part = lax.psum_scatter(g, 'mp', scatter_dimension=axis, tiled=True)  111 us
    pallas_call x3, Pallas kernels, run(): pl.pallas_call(kernel, out_shape=[jax.ShapeDtypeStruct(*v) for v in outs....  90.8 us
    all_gather x3, blocking collectives, gather_columns(): full = lax.all_gather(w, 'mp', axis=0)  64.1 us
    unnamed x13, waiting for transfers between devices  62.3 us
    psum x1, blocking collectives, per_device(): lax.psum((three['gg1'], three['gb1'], two['gg2'], two['gb2']), ('dp', 'mp'))  39.7 us
    all_gather x1, waiting for transfers between devices, per_device(): backs = lax.all_gather(two['back'].reshape(ND, 2, 32, D), 'mp', axis=0)  27.1 us
    all_gather x1, blocking collectives, per_device(): wo = lax.all_gather(w_output, 'mp', axis=0, tiled=True)  20.8 us
    psum x1, waiting for transfers between devices, scatter(): return lax.psum(part, 'dp').astype(f32)  19.5 us
  transfers between devices with their start and end apart: 10, of which 9 were waited for; matrix products, arithmetic and copies ran while one was open for 4% of the time, Pallas kernels for 2%

profile of v1, /device:TPU:0, one launch (start us, length us, event | category | flops | bytes accessed | tf_op | source)
XLA Modules:
  0.0 509.3 jit_solution(3175289549230543728)
XLA Ops:
  7.2 0.7 all-gather.12.cloned.1.call-update
  8.0 0.7 all-gather.8.cloned.1.call-update
  8.8 20.6 %all-gather = bf16[2048,128]{1,0:T(8,128)(2,1)S(1)} all-gather(bf16[512,128]{1,0:T(8,128)(2,1)} %param.21), channel_id=2, replica_groups=mesh['dp'=8,'mp'=4] {'mp'}, dimensions={0}, use_global_device_ids=true | all-gather | bytes 655360 | tf_op jit(solution)/shard_map/all_gather | solution.py:514
  29.3 0.4 copy.36
  29.7 22.4 %all-gather.1 = bf16[2048,128]{1,0:T(8,128)(2,1)S(1)} all-gather(bf16[512,128]{1,0:T(8,128)(2,1)S(1)} %copy-done.6), channel_id=3, replica_groups=mesh['dp'=8,'mp'=4] {'mp'}, dimensions={0}, use_global_device_ids=true | all-gather | bytes 655360 | tf_op jit(solution)/shard_map/all_gather | solution.py:514
  52.5 21.2 %all-gather.2 = bf16[2048,128]{1,0:T(8,128)(2,1)S(1)} all-gather(bf16[512,128]{1,0:T(8,128)(2,1)S(1)} %copy-done.7), channel_id=4, replica_groups=mesh['dp'=8,'mp'=4] {'mp'}, dimensions={0}, use_global_device_ids=true | all-gather | bytes 655360 | tf_op jit(solution)/shard_map/all_gather | solution.py:514
  74.1 1.1 copy.34
  75.3 1.1 copy.35
  76.6 1.2 copy-done
  77.8 9.6 %shard_map.220 = (bf16[1024,512]{1,0:T(8,128)(2,1)}, bf16[2048,512]{1,0:T(8,128)(2,1)}, bf16[2048,512]{1,0:T(8,128)(2,1)}, bf16[2048,512]{1,0:T(8,128)(2,1)}, f32[96,512]{1,0:T(8,128)}) custom-call(s32[2]{0:T(128)} %refs_0_.5, bf16[1024,512]{1,0:T(8,128)(2,1)} %bitcast.72, f32[1,512]{1,0:T(1,128)} %bitcast.104, f32[1,512]{1,0:T(1,128)} %bitcast.106, ...), custom_call_target="tpu_custom_call" | custom-call | tf_op jit(solution)/shard_map/pallas_call | solution.py:502
  87.4 0.9 convert.27
  88.4 18.1 %all_gather.42 = bf16[4,2,2,24,512]{4,3,2,1,0:T(8,128)(2,1)S(1)} all-gather(bf16[1,2,2,24,512]{4,3,2,1,0:T(8,128)(2,1)S(1)} %convert.27), channel_id=1, replica_groups=mesh['dp'=8,'mp'=4] {'mp'}, dimensions={0}, use_global_device_ids=true | all-gather | bytes 491520 | tf_op jit(solution)/shard_map/all_gather | solution.py:553
  106.6 20.8 %all_gather.43.refs_8_ = bf16[512,512]{1,0:T(8,128)(2,1)} all-gather(bf16[128,512]{1,0:T(8,128)(2,1)S(1)} %copy-done.8), channel_id=1, replica_groups=mesh['dp'=8,'mp'=4] {'mp'}, dimensions={0}, use_global_device_ids=true | all-gather | bytes 655360 | tf_op jit(solution)/shard_map/all_gather | solution.py:538
  127.4 0.7 fusion.4
  128.1 3.2 copy.39
  131.3 1.9 copy.51
  133.3 3.3 all-gather.8.cloned.1.call-done.refs_10_
  136.6 67.7 %shard_map.221 = (bf16[1024,512]{1,0:T(8,128)(2,1)}, f32[1024,512]{1,0:T(8,128)}, bf16[2048,512]{1,0:T(8,128)(2,1)}, bf16[2048,512]{1,0:T(8,128)(2,1)}, bf16[204...) custom-call(s32[2]{0:T(128)} %refs_0_.5, ...), custom_call_target="tpu_custom_call" | custom-call | tf_op jit(solution)/shard_map/pallas_call | solution.py:502
  204.4 27.1 %all-gather.10.cloned.1.call-done = f32[4,2,2,32,512]{4,3,2,1,0:T(8,128)} async-done(((f32[1,2,2,32,512]{4,3,2,1,0:T(8,128)}), f32[4,2,2,32,512]{4,3,2,1,0:T(8,128)}) %all-gather.10.cloned.1.call-update) | async-done | bytes 1048592 | tf_op jit(solution)/shard_map/all_gather | solution.py:607
  231.5 1.2 dynamic-slice_bitcast_fusion.2
  232.8 0.7 pad_maximum_fusion
  233.4 13.4 %shard_map.222 = (f32[1024,512]{1,0:T(8,128)}, bf16[512,1536]{1,0:T(8,128)(2,1)}, f32[1,512]{1,0:T(1,128)}, f32[1,512]{1,0:T(1,128)}) custom-call(s32[2]{0:T(128)} %refs_0_.5, bf16[1024,512]{1,0:T(8,128)(2,1)} %bitcast.74, f32[1,512]{1,0:T(1,128)} %bitcast.105, f32[1,512]{1,0:T(1,128)} %bitcast.107, bf16[1024,512]{1,0:T(8,128)(2,1)} %get-tuple-element.61.refs_4_, ...), custom_call_target="tpu_custom_call" | custom-call | tf_op jit(solution)/shard_map/pallas_call | solution.py:502
  246.9 1.5 fusion.6
  248.3 1.0 copy.46
  249.4 1.0 copy.44
  250.5 1.0 copy.42
  251.6 0.7 reduce-scatter.13.cloned.1.call-update
  252.3 0.7 reduce-scatter.15.cloned.1.call-update
  253.1 0.7 reduce-scatter.17.cloned.1.call-update
  253.8 16.9 %reduce-scatter.23.cloned.1.call-done = bf16[128,512]{1,0:T(8,128)(2,1)} async-done(((bf16[512,512]{1,0:T(8,128)(2,1)}), bf16[128,512]{1,0:T(8,128)(2,1)}) %reduce-scatter.23.cloned.1.call-update) | async-done | bytes 131088
  270.7 1.7 copy.47
  272.4 21.0 %reduce-scatter.21.cloned.1.call-done = bf16[128,512]{1,0:T(8,128)(2,1)} async-done(((bf16[512,512]{1,0:T(8,128)(2,1)}), bf16[128,512]{1,0:T(8,128)(2,1)}) %reduce-scatter.21.cloned.1.call-update) | async-done | bytes 131088
  293.4 1.8 copy.45
  295.2 20.9 %reduce-scatter.19.cloned.1.call-done = bf16[128,512]{1,0:T(8,128)(2,1)} async-done(((bf16[512,512]{1,0:T(8,128)(2,1)}), bf16[128,512]{1,0:T(8,128)(2,1)}) %reduce-scatter.19.cloned.1.call-update) | async-done | bytes 131088
  316.1 1.7 copy.43
  317.7 20.6 %reduce-scatter.13.cloned.1.call-done = bf16[128,512]{1,0:T(8,128)(2,1)} async-done(((bf16[512,512]{1,0:T(8,128)(2,1)}), bf16[128,512]{1,0:T(8,128)(2,1)}) %reduce-scatter.13.cloned.1.call-update) | async-done | bytes 131088 | tf_op jit(solution)/shard_map/reduce_scatter | solution.py:637
  338.3 44.4 %reduce-scatter.15.cloned.1.call-done = bf16[512,512]{1,0:T(8,128)(2,1)} async-done(((bf16[512,2048]{1,0:T(8,128)(2,1)}), bf16[512,512]{1,0:T(8,128)(2,1)}) %reduce-scatter.15.cloned.1.call-update) | async-done | bytes 524304 | tf_op jit(solution)/shard_map/reduce_scatter | solution.py:637
  382.7 45.6 %reduce-scatter.17.cloned.1.call-done = bf16[512,512]{1,0:T(8,128)(2,1)} async-done(((bf16[2048,512]{1,0:T(8,128)(2,1)}), bf16[512,512]{1,0:T(8,128)(2,1)}) %reduce-scatter.17.cloned.1.call-update) | async-done | bytes 524304 | tf_op jit(solution)/shard_map/reduce_scatter | solution.py:637
  428.4 2.0 copy.58
  430.5 2.9 copy.57
  433.4 39.7 %all-reduce = (f32[512]{0:T(512)}, f32[512]{0:T(512)}, f32[512]{0:T(512)}, f32[512]{0:T(512)}) all-reduce(f32[512]{0:T(512)S(1)} %bitcast.112, f32[512]{0:T(512)S(1)} %bitcast.113, f32[512]{0:T(512)S(1)} %bitcast.110, f32[512]{0:T(512)S(1)} %bitcast.111), channel_id=1, replica_groups=mesh['dp'=8,'mp'=4] {'dp','mp'}, use_global_device_ids=true, to_apply=%region_12.13 | all-reduce | flops 2048 | bytes 16384 | tf_op jit(solution)/shard_map/psum | solution.py:641
  473.2 19.5 %all-reduce.4.cloned.1.call-done = (bf16[512,128]{1,0:T(8,128)(2,1)}, bf16[512,128]{1,0:T(8,128)(2,1)}, bf16[512,128]{1,0:T(8,128)(2,1)}, bf16[128,512]{1,0:T(8,...) async-done(((bf16[512,128]{1,0:T(8,128)(2,1)}, bf16[512,128]{1,0:T(8,128)(2,1)}, bf16[512,128]{1,0:T(8,128)(2,1)}, bf16[128,512]{1,0:T(8,128)(2,1)}, ...) | async-done | bytes 1572880 | tf_op jit(solution)/shard_map/psum | solution.py:638
  492.7 1.7 convert_element_type.19
  494.3 1.6 convert_element_type.20
  496.0 1.6 convert_element_type.21
  497.6 1.6 convert_element_type.22
  499.2 2.1 convert_element_type.23
  501.4 1.1 convert_element_type.24
  (53 shorter events, 1.6 us)
Async XLA Ops:
  7.2 22.6 %copy-start.6 = (bf16[512,128]{1,0:T(8,128)(2,1)S(1)}, bf16[512,128]{1,0:T(8,128)(2,1)}, u32[]{:S(2)}) copy-start(bf16[512,128]{1,0:T(8,128)(2,1)} %param.22) | copy-start | bytes 393220
  7.2 120.9 %all-gather.12.cloned.1.call-start = ((), (), s32[]{:S(2)}) async-start(), calls=%async_computation.11 | async-start | bytes 2621440 | tf_op jit(solution)/shard_map/all_gather | solution.py:514
  7.9 44.6 %copy-start.7 = (bf16[512,128]{1,0:T(8,128)(2,1)S(1)}, bf16[512,128]{1,0:T(8,128)(2,1)}, u32[]{:S(2)}) copy-start(bf16[512,128]{1,0:T(8,128)(2,1)} %param.23) | copy-start | bytes 393220
  7.9 128.6 %all-gather.8.cloned.1.call-start = ((), (), s32[]{:S(2)}) async-start(), calls=%async_computation.6 | async-start | bytes 2621440 | tf_op jit(solution)/shard_map/all_gather | solution.py:540
  8.7 222.8 %all-gather.10.cloned.1.call-start = ((), (), s32[]{:S(2)}) async-start(), calls=%async_computation.7 | async-start | bytes 1310720 | tf_op jit(solution)/shard_map/all_gather | solution.py:607
  29.3 44.8 %copy-start.2 = (bf16[512,2,512]{2,1,0:T(2,128)(2,1)S(1)}, bf16[512,2,512]{2,1,0:T(2,128)(2,1)}, u32[]{:S(2)}) copy-start(bf16[512,2,512]{2,1,0:T(2,128)(2,1)} %param.17) | copy-start | bytes 3145732
  52.5 22.7 %copy-start.3 = (bf16[512,2,512]{2,1,0:T(2,128)(2,1)S(1)}, bf16[512,2,512]{2,1,0:T(2,128)(2,1)}, u32[]{:S(2)}) copy-start(bf16[512,2,512]{2,1,0:T(2,128)(2,1)} %param.29) | copy-start | bytes 3145732
  76.6 1.2 copy-start
  77.8 28.8 %copy-start.8 = (bf16[128,512]{1,0:T(8,128)(2,1)S(1)}, bf16[128,512]{1,0:T(8,128)(2,1)}, u32[]{:S(2)}) copy-start(bf16[128,512]{1,0:T(8,128)(2,1)} %param.24) | copy-start | bytes 393220
  204.3 66.4 %reduce-scatter.23.cloned.1.call-start = ((), (), s32[]{:S(2)}) async-start(), calls=%async_computation.14 | async-start | bytes 655360
  249.4 44.0 %reduce-scatter.21.cloned.1.call-start = ((), (), s32[]{:S(2)}) async-start(), calls=%async_computation.13 | async-start | bytes 655360
  250.5 65.6 %reduce-scatter.19.cloned.1.call-start = ((), (), s32[]{:S(2)}) async-start(), calls=%async_computation.12 | async-start | bytes 655360
  251.5 86.8 %reduce-scatter.13.cloned.1.call-start = ((), (), s32[]{:S(2)}) async-start(), calls=%async_computation.8 | async-start | bytes 655360 | tf_op jit(solution)/shard_map/reduce_scatter | solution.py:637
  252.3 130.5 %reduce-scatter.15.cloned.1.call-start = ((), (), s32[]{:S(2)}) async-start(), calls=%async_computation.9 | async-start | bytes 2621440 | tf_op jit(solution)/shard_map/reduce_scatter | solution.py:637
  253.0 175.3 %reduce-scatter.17.cloned.1.call-start = ((), (), s32[]{:S(2)}) async-start(), calls=%async_computation.10 | async-start | bytes 2621440 | tf_op jit(solution)/shard_map/reduce_scatter | solution.py:637
  253.1 175.3 %copy-start.4 = (bf16[1024,512]{1,0:T(8,128)(2,1)S(1)}, bf16[1024,512]{1,0:T(8,128)(2,1)}, u32[]{:S(2)}) copy-start(bf16[1024,512]{1,0:T(8,128)(2,1)} %get-tuple-element.60) | copy-start | bytes 3145732
  253.8 238.9 %all-reduce.4.cloned.1.call-start = ((), (), s32[]{:S(2)}) async-start(), calls=%async_computation.15 | async-start | bytes 3145728 | tf_op jit(solution)/shard_map/psum | solution.py:638
  293.4 137.1 %copy-start.1 = (f32[1024,512]{1,0:T(8,128)S(1)}, f32[1024,512]{1,0:T(8,128)}, u32[]{:S(2)}) copy-start(f32[1024,512]{1,0:T(8,128)} %get-tuple-element.67) | copy-start | bytes 6291460
  430.5 3.0 copy-start.9
  430.5 3.0 copy-start.10
  430.5 3.0 copy-start.11
  430.5 3.0 copy-start.12
  492.7 8.7 %copy-start.5 = (bf16[512,512]{1,0:T(8,128)(2,1)S(1)}, bf16[512,512]{1,0:T(8,128)(2,1)}, u32[]{:S(2)}) copy-start(bf16[512,512]{1,0:T(8,128)(2,1)} %get-tuple-element.85) | copy-start | bytes 1572868
Sparse Core Ops, SparseCore 0:
  9.6 67.0 all-gather.11
  78.2 58.3 all-gather.7
  204.5 27.0 all-gather.9
  249.5 21.1 reduce-scatter.22
  273.4 19.9 reduce-scatter.20
  296.1 19.9 reduce-scatter.18
  318.3 19.9 reduce-scatter.12
  340.6 42.1 reduce-scatter.14
  385.2 43.1 reduce-scatter.16
  432.8 59.8 all-reduce.3

commit v2 on v1

v2 whole, which is shorter than its diff:
```python
import types

import jax
import jax.numpy as jnp
from jax import lax
from jax.experimental import pallas as pl
from jax.experimental.pallas import tpu as pltpu
from jax.sharding import PartitionSpec as P

HD = 64
BLK = 16
NEG = -1e30
FLOOR = -1e29
EPS = 1e-05
LOC = 512
ND = 2
D = 512
FF = 2048
NMP = 4
HALF = 256
T = ND * LOC
HEADS = D // HD
LEVELS = 7
LOCAL_LEVELS = 5
EXT = 1024
RT = 256
G = [LOC >> lev for lev in range(LEVELS)]
OFF = [sum(G[:lev]) for lev in range(LEVELS)]
bf16 = jnp.bfloat16
f32 = jnp.float32
i32 = jnp.int32


def dot(a, b, ca=1, cb=0):
    return lax.dot_general(a, b, (((ca,), (cb,)), ((), ())), preferred_element_type=f32)


def iota(shape, axis):
    return lax.broadcasted_iota(i32, shape, axis)


def loop(n, body):
    lax.fori_loop(0, n, lambda i, c: (body(i), c)[1], 0)


def rows_at(i, size):
    return pl.ds(pl.multiple_of(i * size, size), size)


def own_groups(e):
    size = jnp.zeros_like(e)
    start = jnp.zeros_like(e)
    for lev in range(LEVELS):
        here = (e >= OFF[lev]) & (e < OFF[lev] + G[lev])
        size = jnp.where(here, 1 << lev, size)
        start = jnp.where(here, (e - OFF[lev]) << lev, start)
    return size, start


def key_groups(e, z):
    size, start = own_groups(e)
    start = start + z * LOC
    near = z + 1 - 2 * lax.rem(z, 2)
    far = 1 - z // 2
    size = jnp.where(e >= OFF[5], 32, size)
    start = jnp.where(e >= OFF[5], near * LOC + (e - OFF[5]) * 32, start)
    size = jnp.where(e >= OFF[6], 64, size)
    start = jnp.where(e >= OFF[6], far * 2 * LOC + (e - OFF[6]) * 64, start)
    return size, start


def count_live(size, start, length):
    return jnp.clip(length - start, 0, size).astype(f32)


def build_tables(r, z):
    for d in range(ND):
        r.ee[d] = head_map(d)
        length = r.lens[d]

        def chunk(c, d=d, length=length):
            at = pl.ds(pl.multiple_of(d * EXT + c * 128, 128), 128)
            e_col = iota((128, 128), 0) + c * 128
            size, start = key_groups(e_col, z)
            r.cc[at, :] = count_live(size, start, length).astype(bf16)
            e_row = iota((1, 128), 1) + c * 128
            size, start = key_groups(e_row, z)
            dead = count_live(size, start, length)
            r.crow[pl.ds(d * (EXT // 128) + c, 1), :] = dead
            q_blk, k_blk = e_col // BLK, jnp.broadcast_to(e_row // BLK, (128, 128))
            span = jnp.where(q_blk // 2 == k_blk // 2, 0.0, NEG)
            same = jnp.where(q_blk == k_blk, 0.0, NEG)
            cross = jnp.where(q_blk == k_blk, NEG, span)
            bias = jnp.where(e_col < LOC, span, jnp.where(e_col < OFF[5], cross, same))
            r.bias[at, :] = jnp.where(jnp.broadcast_to(dead, (128, 128)) > 0.0, bias, NEG)

        loop(EXT // 128, chunk)


def build_maps(r):
    def tile(c):
        rows = rows_at(c, 128)
        size, start = own_groups(iota((128, LOC), 0) + c * 128 + LOC)
        pos = iota((128, LOC), 1)
        r.pool[rows, :] = ((pos >= start) & (pos < start + size)).astype(f32).astype(bf16)
        size, start = own_groups(iota((128, EXT - LOC), 1) + LOC)
        pos = iota((128, EXT - LOC), 0) + c * 128
        r.unpool[rows, :] = ((pos >= start) & (pos < start + size)).astype(f32).astype(bf16)

    loop((EXT - LOC) // 128, tile)


def inv_counts(r, z, d):
    e = iota((EXT - LOC, 128), 0) + LOC
    size, start = own_groups(e)
    cnt = count_live(size, start + z * LOC, r.lens[d])
    return 1.0 / jnp.maximum(cnt, 1.0), 1.0 / jnp.maximum(size, 1).astype(f32)


def wide(col):
    return jnp.concatenate([col] * (D // 128), axis=1)


def live_rows(r, z, d, first, count):
    pos = iota((count, D), 0) + first + z * LOC
    return pos < r.lens[d]


def stats(v):
    mean = jnp.mean(v, axis=-1, keepdims=True)
    cen = v - mean
    var = jnp.mean(cen * cen, axis=-1, keepdims=True)
    return cen, lax.rsqrt(var + EPS)


def norm_one(r):
    def tile(t):
        rows = rows_at(t, RT)
        cen, rstd = stats(r.x[rows, :].astype(f32))
        r.h1[rows, :] = (cen * rstd * r.g1[...] + r.b1[...]).astype(bf16)

    loop(T // RT, tile)


def ext_rows(d, off, count):
    return pl.ds(d * EXT + off, count)


def attn_weight(r, t):
    return jnp.concatenate([r.wat[s, :, t * 128 : (t + 1) * 128] for s in range(NMP)], axis=1)


def project(r, z, d):
    def tile(t):
        rows = pl.ds(pl.multiple_of(d * LOC + t * RT, RT), RT)
        at = pl.ds(pl.multiple_of(d * EXT + t * RT, RT), RT)
        h = r.h1[rows, :]
        live = live_rows(r, z, d, t * RT, RT)
        q = dot(h, attn_weight(r, 0)).astype(bf16).astype(f32)
        r.qe[at, :] = (q * (HD**-0.5)).astype(bf16)
        k = dot(h, attn_weight(r, 1))
        r.ke[at, :] = jnp.where(live, k, 0.0).astype(bf16)
        v = dot(h, attn_weight(r, 2))
        r.ve[at, :] = jnp.where(live, v, 0.0).astype(bf16)

    loop(LOC // RT, tile)


def pool_levels(r, z):
    keep = OFF[5] - LOC
    for d in range(ND):
        inv, inv_size = inv_counts(r, z, d)
        fine = ext_rows(d, 0, LOC)
        coarse = ext_rows(d, LOC, LOC)
        r.qe[coarse, :] = (dot(r.pool[...], r.qe[fine, :]) * wide(inv_size)).astype(bf16)
        k = dot(r.pool[...], r.ke[fine, :]) * wide(inv)
        v = dot(r.pool[...], r.ve[fine, :])
        r.ke[ext_rows(d, LOC, keep), :] = k[:keep].astype(bf16)
        r.ve[ext_rows(d, LOC, keep), :] = v[:keep].astype(bf16)
        r.sums[2 * d] = k[keep : keep + 24]
        r.sums[2 * d + 1] = v[keep : keep + 24]


def place_remote(r):
    for d in range(ND):
        r.ke[ext_rows(d, OFF[5], 32), :] = r.rem[2 * d].astype(bf16)
        r.ve[ext_rows(d, OFF[5], 32), :] = r.rem[2 * d + 1].astype(bf16)


def split_heads(pair):
    first = iota(pair.shape, 1) < HD
    zero = jnp.zeros_like(pair)
    return jnp.concatenate([jnp.where(first, pair, zero), jnp.where(first, zero, pair)], axis=0)


def count_lanes(cc, d, p):
    lane = iota(cc.shape, 1)
    zero = jnp.zeros_like(cc)
    a = jnp.where(lane == d * HEADS + 2 * p, cc, zero)
    b = jnp.where(lane == d * HEADS + 2 * p + 1, cc, zero)
    return jnp.concatenate([a, b], axis=0)


def attend_chunk(r, c):
    lane = iota((128, 128), 1)
    tops = jnp.zeros((128, 128), f32)
    sums = jnp.zeros((128, 128), f32)
    for d in range(ND):
        at = pl.ds(pl.multiple_of(d * EXT + c * 128, 128), 128)
        bias = r.bias[at, :]
        cc = r.cc[at, :]
        for p in range(HEADS // 2):
            lanes = pl.ds(p * 128, 128)
            s = dot(r.qe[at, lanes], split_heads(r.ke[at, lanes]), 1, 1)
            parts = []
            for j in range(2):
                sj = s[:, j * 128 : (j + 1) * 128] + bias
                top = jnp.maximum(jnp.max(sj, axis=1, keepdims=True), FLOOR)
                parts.append(jnp.exp(sj - top))
                tops = jnp.where(lane == d * HEADS + 2 * p + j, top, tops)
            e = jnp.concatenate(parts, axis=1).astype(bf16)
            slot = pl.ds(pl.multiple_of(((c * ND + d) * 4 + p) * 128, 128), 128)
            r.wts[slot, :] = e
            vo = jnp.concatenate([split_heads(r.ve[at, lanes]), count_lanes(cc, d, p)], axis=1)
            o = dot(e, vo)
            r.num[at, lanes] = o[:, :128]
            sums = sums + o[:, 128:]
    here = rows_at(c, 128)
    r.tops[here, :] = tops
    r.sumz[here, :] = sums


def combine_sums(r):
    last = pl.ds(OFF[6], G[6])
    top = r.tops[last, :]
    tot = r.sumz[last, :]
    for lev in range(LEVELS - 2, -1, -1):
        n = G[lev]
        for half in range(2):
            r.up[pl.ds(half, n // 2, stride=2), :] = top
            r.up2[pl.ds(half, n // 2, stride=2), :] = tot
        at = pl.ds(OFF[lev], n)
        up_top = r.up[pl.ds(0, n), :]
        own = r.tops[at, :]
        top = jnp.maximum(own, up_top)
        a = jnp.exp(own - top)
        b = jnp.exp(up_top - top)
        tot = a * r.sumz[at, :] + b * r.up2[pl.ds(0, n), :]
        if lev == 0:
            used = iota(tot.shape, 1) < ND * HEADS
            inv = 1.0 / jnp.where(used, tot, 1.0)
            a, b = a * inv, b * inv
        r.fa[at, :] = a
        r.fb[at, :] = b


def high_low(v, axis):
    hi = v.astype(bf16).astype(f32)
    return jnp.concatenate([hi, v - hi], axis=axis).astype(bf16)


def spread(r, fac, d):
    return dot(high_low(fac, 1), r.ee[d])


def head_map(d):
    row = lax.rem(iota((256, D), 0), 128)
    return (row == d * HEADS + iota((256, D), 1) // HD).astype(f32).astype(bf16)


def up_map(n):
    return (iota((n, n), 0) // 2 == lax.rem(iota((n, n), 1), n // 2)).astype(f32).astype(bf16)


def down_map(n):
    return (lax.rem(iota((2 * n, n // 2), 0), n) // 2 == iota((2 * n, n // 2), 1)).astype(f32).astype(bf16)


def combine_values(r):
    for d in range(ND):
        cur = r.num[ext_rows(d, OFF[6], G[6]), :]
        for lev in range(LEVELS - 2, -1, -1):
            n = G[lev]
            parts = []
            step = min(n, 128)
            for t in range(n // step):
                at = pl.ds(OFF[lev] + t * step, step)
                here = ext_rows(d, OFF[lev] + t * step, step)
                own = spread(r, r.fa[at, :], d) * r.num[here, :]
                up = dot(up_map(step), high_low(cur[t * step // 2 : (t + 1) * step // 2], 0))
                parts.append(own + spread(r, r.fb[at, :], d) * up)
                if lev == 0:
                    r.ctx[pl.ds(d * LOC + t * step, step), :] = parts[-1].astype(bf16)
                    r.num[here, :] = parts[-1]
            cur = jnp.concatenate(parts, axis=0) if len(parts) > 1 else parts[0]


def spare_rows(t):
    per = LOC // RT
    return pl.ds(pl.multiple_of((t // per) * EXT + LOC + lax.rem(t, per) * RT, RT), RT)


def attn_out(r):
    def tile(t):
        rows = rows_at(t, RT)
        mid = r.x[rows, :].astype(f32) + dot(r.ctx[rows, :], attn_weight(r, 3), 1, 1)
        r.num[spare_rows(t), :] = mid
        cen, rstd = stats(mid)
        r.h2[rows, :] = (cen * rstd * r.g2[...] + r.b2[...]).astype(bf16)

    loop(T // RT, tile)


def ffn_inner(r):
    def step(i):
        f, t = i // (T // RT), lax.rem(i, T // RT)
        rows = rows_at(t, RT)
        cols = rows_at(f, 512)
        pre = dot(r.h2[rows, :], r.wup[f])
        ga = dot(r.gy[rows, :], r.wdn[f], 1, 1)
        cdf = 0.5 + 0.5 * lax.erf(pre * (0.5**0.5))
        r.act[rows, cols] = (pre * cdf).astype(bf16)
        pdf = jnp.exp(pre * pre * -0.5) * 0.3989422804014327
        r.gp[rows, cols] = (ga * (cdf + pre * pdf)).astype(bf16)

    loop((FF // 512) * (T // RT), step)


def down_grads(r):
    def tile(f):
        r.gdn[f] = dot(r.act[:, rows_at(f, 512)], r.gy[...], 0, 0).astype(bf16)

    loop(NMP, tile)


def up_grads(r):
    def tile(f):
        r.gup[f] = dot(r.h2[...], r.gp[:, rows_at(f, 512)], 0, 0).astype(bf16)

    loop(NMP, tile)


def norm_back(v, gain, gh, r, row):
    cen, rstd = stats(v)
    xhat = cen * rstd
    r.norms[row : row + 1, :] += jnp.sum(gh * xhat, axis=0, keepdims=True)
    r.norms[row + 1 : row + 2, :] += jnp.sum(gh, axis=0, keepdims=True)
    u = gh * gain
    return rstd * (
        u - jnp.mean(u, axis=-1, keepdims=True) - xhat * jnp.mean(u * xhat, axis=-1, keepdims=True)
    )


def ffn_outer(r):
    def tile(t):
        rows = rows_at(t, RT)
        mid = r.num[spare_rows(t), :]
        ffn = dot(r.act[rows, 0:512], r.wdn[0])
        gh2 = dot(r.gp[rows, 0:512], r.wup[0], 1, 1)
        for f in range(1, NMP):
            cols = slice(f * 512, (f + 1) * 512)
            ffn = ffn + dot(r.act[rows, cols], r.wdn[f])
            gh2 = gh2 + dot(r.gp[rows, cols], r.wup[f], 1, 1)
        r.mixed[rows, :] = (mid + ffn).astype(bf16)
        g_mid = r.gy[rows, :].astype(f32) + norm_back(mid, r.g2[...], gh2, r, 2)
        r.gx[rows, :] = g_mid
        r.gm[rows, :] = g_mid.astype(bf16)

    loop(T // RT, tile)


def store_shards(dst, full):
    for s in range(NMP):
        dst[s] = full[:, s * 128 : (s + 1) * 128].astype(bf16)


def out_grads(r):
    store_shards(r.gw3, dot(r.gm[...], r.ctx[...], 0, 0))


def store_pair(r, d, off, count, v):
    hi = v.astype(bf16)
    r.ge[ext_rows(d, off, count), :] = hi
    lo = (v - hi.astype(f32)).astype(bf16)
    if off < LOC:
        r.dqe[ext_rows(d, off, count), :] = lo
    else:
        r.dke[ext_rows(d, off - LOC, count), :] = lo


def attn_back_rows(r):
    lane_head = lax.rem(iota((2 * D, 128), 0), D) // HD
    for t in range(LOC // 128):
        at = pl.ds(t * 128, 128)
        delta = jnp.zeros((128, 128), f32)
        for d in range(ND):
            rows = pl.ds(d * LOC + t * 128, 128)
            gctx = dot(r.gm[rows, :], attn_weight(r, 3))
            sel = (lane_head + d * HEADS == iota((2 * D, 128), 1)).astype(f32).astype(bf16)
            delta = delta + dot(high_low(gctx * r.num[ext_rows(d, t * 128, 128), :], 1), sel)
            store_pair(r, d, t * 128, 128, spread(r, r.fa[at, :], d) * gctx)
            down = high_low(spread(r, r.fb[at, :], d) * gctx, 0)
            r.hc[pl.ds(d * LOC // 2 + t * 64, 64), :] = dot(down_map(128), down, 0, 0)
        r.dl[at, :] = r.fa[at, :] * delta
        r.up[at, :] = r.fb[at, :] * delta
    acc = r.up[pl.ds(0, LOC // 2, stride=2), :] + r.up[pl.ds(1, LOC // 2, stride=2), :]
    for lev in range(1, LEVELS - 1):
        n = G[lev]
        at = pl.ds(OFF[lev], n)
        r.dl[at, :] = r.fa[at, :] * acc
        r.up[pl.ds(0, n), :] = r.fb[at, :] * acc
        acc = r.up[pl.ds(0, n // 2, stride=2), :] + r.up[pl.ds(1, n // 2, stride=2), :]
    r.dl[pl.ds(OFF[6], 2 * G[6]), :] = jnp.concatenate([acc, jnp.zeros_like(acc)], 0)
    for d in range(ND):
        cur = r.hc[pl.ds(d * LOC // 2, LOC // 2), :]
        for lev in range(1, LEVELS - 1):
            n = G[lev]
            parts = []
            step = min(n, 128)
            for t in range(n // step):
                at = pl.ds(OFF[lev] + t * step, step)
                seg = cur[t * step : (t + 1) * step]
                store_pair(r, d, OFF[lev] + t * step, step, spread(r, r.fa[at, :], d) * seg)
                down = high_low(spread(r, r.fb[at, :], d) * seg, 0)
                parts.append(dot(down_map(step), down, 0, 0))
            cur = jnp.concatenate(parts, axis=0) if len(parts) > 1 else parts[0]
        store_pair(r, d, OFF[6], 2 * G[6], jnp.concatenate([cur, jnp.zeros_like(cur)], axis=0))


def attend_back_chunk(r, c, fine):
    first = iota((128, 128), 1) < HD
    dl = r.dl[rows_at(c, 128), :]
    low = r.dqe if fine else r.dke
    for d in range(ND):
        at = pl.ds(pl.multiple_of(d * EXT + c * 128, 128), 128)
        low_at = at if fine else pl.ds(pl.multiple_of(d * EXT + c * 128 - LOC, 128), 128)
        cnt = jnp.broadcast_to(r.crow[pl.ds(d * (EXT // 128) + c, 1), :], (128, 128))
        for p in range(HEADS // 2):
            lanes = pl.ds(p * 128, 128)
            g = r.ge[at, lanes]
            q = r.qe[at, lanes]
            kcat = split_heads(r.ke[at, lanes])
            vcat = split_heads(r.ve[at, lanes])
            both = jnp.concatenate([g, low[low_at, lanes]], axis=1)
            dp = dot(both, jnp.concatenate([vcat, vcat], axis=1), 1, 1)
            slot = pl.ds(pl.multiple_of(((c * ND + d) * 4 + p) * 128, 128), 128)
            e = r.wts[slot, :]
            parts = []
            for j in range(2):
                lane = d * HEADS + 2 * p + j
                half = slice(j * 128, (j + 1) * 128)
                parts.append(e[:, half].astype(f32) * (dp[:, half] - dl[:, lane : lane + 1] * cnt))
            ds = jnp.concatenate(parts, axis=1).astype(bf16)
            dq = dot(ds, kcat)
            dk = dot(ds, q, 0, 0)
            dk = jnp.where(first, dk[:128], dk[128:])
            if fine:
                r.num[pl.ds(pl.multiple_of(d * EXT + c * 128, 128), 128), lanes] = dq
                r.num[pl.ds(pl.multiple_of(d * EXT + LOC + c * 128, 128), 128), lanes] = dk
            else:
                r.dqe[at, lanes] = dq.astype(bf16)
                r.dke[at, lanes] = dk.astype(bf16)
            dv = dot(e, g, 0, 0)
            r.dve[at, lanes] = jnp.where(first, dv[:128], dv[128:]).astype(bf16)


def save_remote(r):
    for d in range(ND):
        r.back[2 * d] = r.dke[ext_rows(d, OFF[5], 32), :].astype(f32)
        r.back[2 * d + 1] = r.dve[ext_rows(d, OFF[5], 32), :].astype(f32)


def coarse_rows(r, src, d, kv):
    keep = OFF[5] - LOC
    own = src[ext_rows(d, LOC, keep), :].astype(f32)
    i = 2 * d + kv
    rest = jnp.zeros((LOC - keep - 24, D), f32)
    return jnp.concatenate([own, r.near[i], r.far[0, i] + r.far[1, i], rest], axis=0)


def unpool_values(r, z):
    for d in range(ND):
        live = live_rows(r, z, d, 0, LOC)
        v = coarse_rows(r, r.dve, d, 1).astype(bf16)
        v = r.dve[ext_rows(d, 0, LOC), :].astype(f32) + dot(r.unpool[...], v)
        r.ve[pl.ds(d * LOC, LOC), :] = jnp.where(live, v, 0.0).astype(bf16)


def unpool_keys(r, z):
    for d in range(ND):
        inv, _ = inv_counts(r, z, d)
        live = live_rows(r, z, d, 0, LOC)
        k = (coarse_rows(r, r.dke, d, 0) * wide(inv)).astype(bf16)
        k = r.num[ext_rows(d, LOC, LOC), :] + dot(r.unpool[...], k)
        r.ke[pl.ds(d * LOC, LOC), :] = jnp.where(live, k, 0.0).astype(bf16)


def unpool_queries(r, z):
    for d in range(ND):
        _, inv_size = inv_counts(r, z, d)
        q = (r.dqe[ext_rows(d, LOC, LOC), :].astype(f32) * wide(inv_size)).astype(bf16)
        q = r.num[ext_rows(d, 0, LOC), :] + dot(r.unpool[...], q)
        r.qe[pl.ds(d * LOC, LOC), :] = (q * (HD**-0.5)).astype(bf16)


def weight_grad(r, dst, src):
    store_shards(dst, dot(r.h1[...], src[pl.ds(0, T), :], 0, 0))


def input_grads(r, t):
    rows = rows_at(t, RT)
    gh1 = dot(r.qe[rows, :], attn_weight(r, 0), 1, 1)
    gh1 = gh1 + dot(r.ke[rows, :], attn_weight(r, 1), 1, 1)
    gh1 = gh1 + dot(r.ve[rows, :], attn_weight(r, 2), 1, 1)
    x = r.x[rows, :].astype(f32)
    r.gx[rows, :] = r.gx[rows, :] + norm_back(x, r.g1[...], gh1, r, 0)


def remote(src, dst, send, recv, where):
    return pltpu.make_async_remote_copy(
        src_ref=src, dst_ref=dst, send_sem=send, recv_sem=recv, device_id=where,
        device_id_type=pl.DeviceIdType.MESH,
    )


class Links:
    def __init__(self, r, ndp):
        self.r, self.ndp, self.nq, self.piece = r, ndp, ndp // 2, LOC // ndp
        self.z, self.me = lax.axis_index("mp"), lax.axis_index("dp")
        self.c, self.q = lax.rem(self.me, 2), self.me // 2
        self.other = 2 * self.q + 1 - self.c
        self.near = self.z + 1 - 2 * lax.rem(self.z, 2)
        self.far = (1 - self.z // 2) * 2
        self.par = lax.rem(self.z, 2)
        self.sent = []

    def mp_peer(self, k):
        return lax.rem(self.z + k, NMP)

    def dp_peer(self, k):
        return lax.rem(self.me + k, self.ndp)

    def quarter(self, j):
        return lax.rem(self.q + j, self.nq)

    def piece_rows(self, q):
        return pl.ds(pl.multiple_of(self.c * HALF + q * self.piece, self.piece), self.piece)

    def rows_of(self, dev):
        first = lax.rem(dev, 2) * HALF + (dev // 2) * self.piece
        return pl.ds(pl.multiple_of(first, self.piece), self.piece)

    def half(self, c):
        return pl.ds(pl.multiple_of(c * HALF, HALF), HALF)

    def send(self, src, dst, send, recv, where):
        copy = remote(src, dst, send, recv, where)
        copy.start()
        self.sent.append(copy)

    def arrive(self, dst, send, recv, where):
        remote(dst, dst, send, recv, where).wait_recv()

    def barrier(self):
        sem = pltpu.get_barrier_semaphore()
        for k in range(1, NMP):
            pl.semaphore_signal(sem, inc=1, device_id={"mp": self.mp_peer(k)})
        for k in range(1, self.ndp):
            pl.semaphore_signal(sem, inc=1, device_id={"dp": self.dp_peer(k)})
        pl.semaphore_wait(sem, NMP + self.ndp - 2)

    def gather_z(self, m, w):
        rows = self.rows_of(self.me)
        for k in range(1, NMP):
            piece = w.at[self.z, rows, :]
            i = m * 3 + k - 1
            self.send(piece, piece, self.r.wz_s.at[i], self.r.wz_r.at[i], {"mp": self.mp_peer(k)})

    def gather_plane(self, m, w):
        rows = self.rows_of(self.me)
        for k in range(1, NMP):
            piece = w.at[self.mp_peer(NMP - k), rows, :]
            i = m * 3 + k - 1
            here = {"mp": self.mp_peer(k)}
            self.arrive(piece, self.r.wz_s.at[i], self.r.wz_r.at[i], here)
            for j in range(1, self.nq):
                n = i * (self.nq - 1) + j - 1
                where = {"dp": 2 * self.quarter(j) + self.c}
                self.send(piece, piece, self.r.wp_s.at[n], self.r.wp_r.at[n], where)

    def gather_core(self, m, w):
        for k in range(1, NMP):
            shard = self.mp_peer(NMP - k)
            i = m * 3 + k - 1
            for j in range(1, self.nq):
                n = i * (self.nq - 1) + j - 1
                got = w.at[shard, self.piece_rows(self.quarter(self.nq - j)), :]
                where = {"dp": 2 * self.quarter(j) + self.c}
                self.arrive(got, self.r.wp_s.at[n], self.r.wp_r.at[n], where)
            part = w.at[shard, self.half(self.c), :]
            self.send(part, part, self.r.wc_s.at[i], self.r.wc_r.at[i], {"dp": self.other})

    def gather_done(self, m, w):
        for k in range(1, NMP):
            i = m * 3 + k - 1
            part = w.at[self.mp_peer(NMP - k), self.half(1 - self.c), :]
            self.arrive(part, self.r.wc_s.at[i], self.r.wc_r.at[i], {"dp": self.other})

    def coarse_send(self):
        r = self.r
        dst = r.rem.at[:, pl.ds(0, 16), :]
        self.send(r.sums.at[:, pl.ds(0, 16), :], dst, r.cf_s.at[0], r.cf_r.at[0], {"mp": self.near})
        place = pl.ds(pl.multiple_of(16 + 8 * self.par, 8), 8)
        for j in range(2):
            where = {"mp": self.far + j}
            src = r.sums.at[:, pl.ds(16, 8), :]
            dst = r.rem.at[:, place, :]
            self.send(src, dst, r.cf_s.at[1 + j], r.cf_r.at[1 + self.par], where)

    def coarse_wait(self):
        r = self.r
        self.arrive(r.rem.at[:, pl.ds(0, 16), :], r.cf_s.at[0], r.cf_r.at[0], {"mp": self.near})
        for j in range(2):
            got = r.rem.at[:, pl.ds(16 + 8 * j, 8), :]
            self.arrive(got, r.cf_s.at[1 + j], r.cf_r.at[1 + j], {"mp": self.far + j})

    def coarse_back(self):
        r = self.r
        src = r.back.at[:, pl.ds(0, 16), :]
        self.send(src, r.near, r.cb_s.at[0], r.cb_r.at[0], {"mp": self.near})
        for j in range(2):
            src = r.back.at[:, pl.ds(16 + 8 * j, 8), :]
            dst = r.far.at[self.par]
            self.send(src, dst, r.cb_s.at[1 + j], r.cb_r.at[1 + self.par], {"mp": self.far + j})

    def coarse_back_wait(self):
        r = self.r
        self.arrive(r.near, r.cb_s.at[0], r.cb_r.at[0], {"mp": self.near})
        for j in range(2):
            self.arrive(r.far.at[j], r.cb_s.at[1 + j], r.cb_r.at[1 + j], {"mp": self.far + j})

    def sum_core(self, m, b):
        src = b.g.at[:, self.half(1 - self.c), :]
        self.send(src, b.rc, self.r.gc_s.at[m], self.r.gc_r.at[m], {"dp": self.other})

    def sum_plane(self, m, b):
        self.arrive(b.rc, self.r.gc_s.at[m], self.r.gc_r.at[m], {"dp": self.other})

        def add(s):
            for i in range(2):
                rows = pl.ds(pl.multiple_of(self.c * HALF + i * 128, 128), 128)
                more = b.rc[s, pl.ds(i * 128, 128), :].astype(f32)
                b.g[s, rows, :] = (b.g[s, rows, :].astype(f32) + more).astype(bf16)

        loop(NMP, add)
        for j in range(1, self.nq):
            n = m * (self.nq - 1) + j - 1
            to = self.quarter(j)
            src = b.g.at[:, self.piece_rows(to), :]
            where = {"dp": 2 * to + self.c}
            self.send(src, b.rp.at[j - 1], self.r.gp_s.at[n], self.r.gp_r.at[n], where)

    def sum_z(self, m, b):
        for j in range(1, self.nq):
            n = m * (self.nq - 1) + j - 1
            where = {"dp": 2 * self.quarter(j) + self.c}
            self.arrive(b.rp.at[j - 1], self.r.gp_s.at[n], self.r.gp_r.at[n], where)
        for s in range(NMP):
            tot = b.g[s, self.piece_rows(self.q), :].astype(f32)
            for j in range(self.nq - 1):
                tot = tot + b.rp[j, s].astype(f32)
            b.pz[s] = tot.astype(bf16)
        for k in range(1, NMP):
            to = self.mp_peer(k)
            i = m * 3 + k - 1
            self.send(b.pz.at[to], b.rz.at[k - 1], self.r.gz_s.at[i], self.r.gz_r.at[i], {"mp": to})

    def sum_share(self, m, b):
        tot = b.pz[self.z].astype(f32)
        for k in range(1, NMP):
            i = m * 3 + k - 1
            where = {"mp": self.mp_peer(k)}
            self.arrive(b.rz.at[k - 1], self.r.gz_s.at[i], self.r.gz_r.at[i], where)
            tot = tot + b.rz[k - 1].astype(f32)
        mine = self.rows_of(self.me)
        b.fin[mine, :] = tot.astype(bf16)
        for k in range(1, self.ndp):
            n = m * (self.ndp - 1) + k - 1
            where = {"dp": self.dp_peer(k)}
            part = b.fin.at[mine, :]
            self.send(part, part, self.r.gs_s.at[n], self.r.gs_r.at[n], where)

    def sum_done(self, m, b):
        for k in range(1, self.ndp):
            n = m * (self.ndp - 1) + k - 1
            got = b.fin.at[self.rows_of(self.dp_peer(self.ndp - k)), :]
            where = {"dp": self.dp_peer(k)}
            self.arrive(got, self.r.gs_s.at[n], self.r.gs_r.at[n], where)

    def norms_z(self):
        r = self.r
        r.nz[self.z] = r.norms[...]
        for k in range(1, NMP):
            dst = r.nz.at[self.z]
            where = {"mp": self.mp_peer(k)}
            self.send(r.norms, dst, r.nz_s.at[k - 1], r.nz_r.at[k - 1], where)

    def norms_dp(self):
        r = self.r
        for k in range(1, NMP):
            got = r.nz.at[self.mp_peer(NMP - k)]
            self.arrive(got, r.nz_s.at[k - 1], r.nz_r.at[k - 1], {"mp": self.mp_peer(k)})
        tot = r.nz[0]
        for k in range(1, NMP):
            tot = tot + r.nz[k]
        r.np[self.me] = tot
        for k in range(1, self.ndp):
            dst = r.np.at[self.me]
            where = {"dp": self.dp_peer(k)}
            self.send(dst, dst, r.np_s.at[k - 1], r.np_r.at[k - 1], where)

    def norms_done(self):
        r = self.r
        for k in range(1, self.ndp):
            got = r.np.at[self.dp_peer(self.ndp - k)]
            self.arrive(got, r.np_s.at[k - 1], r.np_r.at[k - 1], {"dp": self.dp_peer(k)})
        tot = r.np[0]
        for k in range(1, self.ndp):
            tot = tot + r.np[k]
        r.onorm[...] = tot

    def finish(self):
        for copy in self.sent:
            copy.wait_send()


FAR_OUTS = ("oat", "oup", "odn")
NAMES = ("w0", "w1", "w2", "w3", "up", "dn")


def grad_buffers(r, n):
    get = lambda k: getattr(r, k + n)
    return types.SimpleNamespace(
        g=get("g"), rc=get("rc_"), rp=get("rp_"), pz=get("pz_"), rz=get("rz_"), fin=get("fin_")
    )


def whole_kernel(ndp, r):
    net = Links(r, ndp)
    z = net.z
    r.act, r.gp = r.big.at[pl.ds(0, T), :], r.big.at[pl.ds(T, T), :]
    r.dqe, r.dke, r.dve, r.ge = (r.big.at[:, pl.ds(i * D, D)] for i in range(4))
    bufs = [grad_buffers(r, n) for n in NAMES]
    loads = []
    for i, w in enumerate((r.w_query, r.w_key, r.w_value)):
        dst = r.wat.at[z, :, pl.ds(i * 128, 128)]
        loads.append(pltpu.make_async_copy(w, dst, r.ld.at[i]))
    loads.append(pltpu.make_async_copy(r.w_up, r.wup.at[z], r.ld.at[3]))
    loads.append(pltpu.make_async_copy(r.w_down, r.wdn.at[z], r.ld.at[4]))
    for copy in loads:
        copy.start()
    net.barrier()
    r.wat[z, :, pl.ds(384, 128)] = r.w_output[...].T
    for copy in loads[:3]:
        copy.wait()
    net.gather_z(0, r.wat)
    for copy in loads[3:]:
        copy.wait()
    net.gather_z(1, r.wup)
    net.gather_z(2, r.wdn)
    r.norms[...] = jnp.zeros_like(r.norms)
    norm_one(r)
    net.gather_plane(0, r.wat)
    build_tables(r, z)
    build_maps(r)
    net.gather_core(0, r.wat)
    net.gather_done(0, r.wat)
    project(r, z, 0)
    net.gather_plane(1, r.wup)
    project(r, z, 1)
    net.gather_plane(2, r.wdn)
    pool_levels(r, z)
    net.coarse_send()
    loop(4, lambda c: attend_chunk(r, c))
    net.gather_core(1, r.wup)
    net.gather_core(2, r.wdn)
    loop(3, lambda c: attend_chunk(r, c + 4))
    net.coarse_wait()
    place_remote(r)
    attend_chunk(r, EXT // 128 - 1)
    combine_sums(r)
    combine_values(r)
    attn_out(r)
    net.gather_done(1, r.wup)
    net.gather_done(2, r.wdn)
    ffn_inner(r)
    down_grads(r)
    net.sum_core(5, bufs[5])
    up_grads(r)
    net.sum_core(4, bufs[4])
    net.sum_plane(5, bufs[5])
    ffn_outer(r)
    net.sum_plane(4, bufs[4])
    out_grads(r)
    net.sum_core(3, bufs[3])
    attn_back_rows(r)
    net.sum_z(5, bufs[5])
    net.sum_plane(3, bufs[3])
    attend_back_chunk(r, EXT // 128 - 1, False)
    save_remote(r)
    net.coarse_back()
    loop(2, lambda c: attend_back_chunk(r, c, True))
    net.sum_share(5, bufs[5])
    net.sum_z(4, bufs[4])
    loop(2, lambda c: attend_back_chunk(r, c + 2, True))
    net.sum_share(4, bufs[4])
    net.sum_z(3, bufs[3])
    loop(3, lambda c: attend_back_chunk(r, c + 4, False))
    net.sum_share(3, bufs[3])
    net.coarse_back_wait()
    unpool_values(r, z)
    weight_grad(r, r.gw2, r.ve)
    net.sum_core(2, bufs[2])
    unpool_keys(r, z)
    weight_grad(r, r.gw1, r.ke)
    net.sum_core(1, bufs[1])
    net.sum_plane(2, bufs[2])
    unpool_queries(r, z)
    weight_grad(r, r.gw0, r.qe)
    net.sum_core(0, bufs[0])
    net.sum_plane(1, bufs[1])
    input_grads(r, 0)
    net.sum_plane(0, bufs[0])
    net.sum_z(2, bufs[2])
    input_grads(r, 1)
    net.sum_z(1, bufs[1])
    input_grads(r, 2)
    net.sum_share(2, bufs[2])
    net.sum_z(0, bufs[0])
    input_grads(r, 3)
    net.norms_z()
    net.sum_share(1, bufs[1])
    net.sum_share(0, bufs[0])
    net.norms_dp()
    places = [r.oat.at[:, pl.ds(i * 128, 128)] for i in range(4)] + [r.oup, r.odn]
    stores = []
    for m in (5, 4, 3, 2, 1, 0):
        net.sum_done(m, bufs[m])
        stores.append(pltpu.make_async_copy(bufs[m].fin, places[m], r.st.at[m]))
        stores[-1].start()
    net.norms_done()
    for copy in stores:
        copy.wait()
    net.finish()


def run(body, ins, outs, scratch, sems):
    names = list(ins) + list(outs) + list(scratch) + list(sems)

    def kernel(*refs):
        body(types.SimpleNamespace(**dict(zip(names, refs))))

    result = pl.pallas_call(
        kernel,
        out_shape=[jax.ShapeDtypeStruct(*v) for v in outs.values()],
        in_specs=[pl.BlockSpec(memory_space=space) for _, space in ins.values()],
        out_specs=[
            pl.BlockSpec(memory_space=pl.ANY if n in FAR_OUTS else pltpu.VMEM) for n in outs
        ],
        scratch_shapes=[pltpu.VMEM(*v) for v in scratch.values()]
        + [pltpu.SemaphoreType.DMA((n,)) for n in sems.values()],
        compiler_params=pltpu.CompilerParams(
            vmem_limit_bytes=63 * 1024 * 1024, collective_id=0, has_side_effects=True
        ),
    )(*[a for a, _ in ins.values()])
    return dict(zip(outs, result))


def per_device(
    ndp,
    tokens,
    lengths,
    gain_one,
    shift_one,
    w_query,
    w_key,
    w_value,
    w_output,
    gain_two,
    shift_two,
    w_up,
    w_down,
    cotangent,
):
    x = jnp.swapaxes(tokens, 0, 1).reshape(T, D)
    gy = jnp.swapaxes(cotangent, 0, 1).reshape(T, D)
    g1, b1, g2, b2 = (v.reshape(1, D) for v in (gain_one, shift_one, gain_two, shift_two))
    nq, piece = ndp // 2, LOC // ndp
    vmem, any_space = pltpu.VMEM, pl.ANY
    ins = dict(
        lens=(lengths, pltpu.SMEM),
        x=(x, vmem),
        gy=(gy, vmem),
        g1=(g1, vmem),
        b1=(b1, vmem),
        g2=(g2, vmem),
        b2=(b2, vmem),
        w_query=(w_query, any_space),
        w_key=(w_key, any_space),
        w_value=(w_value, any_space),
        w_output=(w_output, vmem),
        w_up=(w_up, any_space),
        w_down=(w_down, any_space),
    )
    outs = dict(
        mixed=((T, D), bf16),
        gx=((T, D), f32),
        oat=((D, 512), bf16),
        oup=((D, 512), bf16),
        odn=((512, D), bf16),
        onorm=((8, D), f32),
    )
    scratch = dict(
        wat=((NMP, D, 512), bf16),
        wup=((NMP, D, 512), bf16),
        wdn=((NMP, 512, D), bf16),
        h1=((T, D), bf16),
        qe=((ND * EXT, D), bf16),
        ke=((ND * EXT, D), bf16),
        ve=((ND * EXT, D), bf16),
        pool=((EXT - LOC, LOC), bf16),
        unpool=((LOC, EXT - LOC), bf16),
        cc=((ND * EXT, 128), bf16),
        bias=((ND * EXT, 128), f32),
        wts=((64 * 128, 256), bf16),
        num=((ND * EXT, D), f32),
        tops=((EXT, 128), f32),
        sumz=((EXT, 128), f32),
        up=((LOC, 128), f32),
        up2=((LOC, 128), f32),
        fa=((EXT, 128), f32),
        fb=((EXT, 128), f32),
        ctx=((T, D), bf16),
        h2=((T, D), bf16),
        big=((2 * T, FF), bf16),
        gm=((T, D), bf16),
        hc=((T // 2, D), f32),
        dl=((EXT, 128), f32),
        ee=((ND, 256, D), bf16),
        crow=((ND * EXT // 128, 128), f32),
        sums=((2 * ND, 24, D), f32),
        rem=((2 * ND, 32, D), f32),
        back=((2 * ND, 32, D), f32),
        near=((2 * ND, 16, D), f32),
        far=((2, 2 * ND, 8, D), f32),
        norms=((8, D), f32),
        nz=((NMP, 8, D), f32),
        np=((ndp, 8, D), f32),
    )
    for n in NAMES:
        cols = 512 if n in ("up", "dn") else 128
        scratch["g" + n] = ((NMP, 512, cols), bf16)
        scratch["rc_" + n] = ((NMP, HALF, cols), bf16)
        scratch["rp_" + n] = ((nq - 1, NMP, piece, cols), bf16)
        scratch["pz_" + n] = ((NMP, piece, cols), bf16)
        scratch["rz_" + n] = ((3, piece, cols), bf16)
        scratch["fin_" + n] = ((512, cols), bf16)
    counts = dict(
        wz=9, wp=9 * (nq - 1), wc=9, cf=3, cb=3, gc=6, gp=6 * (nq - 1), gz=18, gs=6 * (ndp - 1),
        nz=3, np=ndp - 1,
    )
    sems = dict(ld=5, st=6)
    for n, count in counts.items():
        sems[n + "_s"] = count
        sems[n + "_r"] = count
    o = run(lambda r: whole_kernel(ndp, r), ins, outs, scratch, sems)

    def back_to(a):
        return jnp.swapaxes(a.reshape(ND, LOC, D), 0, 1)

    at = [o["oat"][:, i * 128 : (i + 1) * 128].astype(f32) for i in range(4)]
    return (
        back_to(o["mixed"]),
        back_to(o["gx"]),
        at[0],
        at[1],
        at[2],
        at[3].T,
        o["oup"].astype(f32),
        o["odn"].astype(f32),
        *(o["onorm"][i] for i in range(4)),
    )


def solution(mesh):
    tok = P("mp", "dp", None)
    col, row, rep = P(None, "mp"), P("mp", None), P()
    ndp = mesh.shape["dp"]
    return jax.shard_map(
        lambda *args: per_device(ndp, *args),
        mesh=mesh,
        in_specs=(tok, P("dp"), rep, rep, col, col, col, row, rep, rep, col, row, tok),
        out_specs=(tok, tok, col, col, col, row, col, row, rep, rep, rep, rep),
        check_vma=False,
    )
```

time: 510 us -> 150 us (0.29)
  waiting for transfers between devices: 223 us -> 0 us
  blocking collectives: 143 us -> 0 us
  Pallas kernels: 90.8 us -> 135 us
  local copies, waits for them, and re-layouts: 26.6 us -> 11.4 us
  between operations: 14.5 us -> 0.68 us
  other arithmetic: 11.5 us -> 3.11 us
    reduce_scatter x3 -> x0, waiting for transfers between devices: 111 us -> none  [scatter(): part = lax.psum_scatter(g, 'mp', scatter_dimension=axis, tiled=True)]
    all_gather x5 -> x0, blocking collectives: 103 us -> none  [the longest x3 64.1 us: gather_columns(): full = lax.all_gather(w, 'mp', axis=0)]
    unnamed x13 -> x0, waiting for transfers between devices: 62.3 us -> none
    pallas_call x3 -> x1, Pallas kernels: 90.8 us -> 135 us  [run(): pl.pallas_call(kernel, out_shape=[jax.ShapeDtypeStruct(*v) for v in outs....]
    psum x1 -> x0, blocking collectives: 39.7 us -> none  [per_device(): lax.psum((three['gg1'], three['gb1'], two['gg2'], two['gb2']), ('dp', 'mp'))]
    all_gather x3 -> x0, waiting for transfers between devices: 30.4 us -> none  [the longest x1 27.1 us: per_device(): backs = lax.all_gather(two['back'].reshape(ND, 2, 32, D), 'mp', axis=0)]
    psum x1 -> x0, waiting for transfers between devices: 19.5 us -> none  [scatter(): return lax.psum(part, 'dp').astype(f32)]
    unnamed x35 -> x13, local copies, waits for them, and re-layouts: 11.4 us -> 0.86 us
  transfers between devices with their start and end apart: 10 -> 0, of which waited for: 9 -> 0; matrix products, arithmetic and copies ran while one was open for 4% -> 0% of each run, Pallas kernels for 2% -> 0%
where the time goes in v2:
time: 150 us
  Pallas kernels  135 us (90%)
  local copies, waits for them, and re-layouts  11.4 us (8%)
  other arithmetic  3.11 us (2%)
    pallas_call x1, Pallas kernels, run(): pl.pallas_call(kernel, out_shape=[jax.ShapeDtypeStruct(*v) for v in outs....  135 us
    reshape x2, local copies, waits for them, and re-layouts, back_to(): return jnp.swapaxes(a.reshape(ND, LOC, D), 0, 1)  6.36 us

profile of v2, /device:TPU:0, one launch (start us, length us, event | category | flops | bytes accessed | tf_op | source)
XLA Modules:
  0.0 150.2 jit_solution(6341541092148085561)
XLA Ops:
  0.6 0.0 copy-start.1
  0.7 2.4 %copy.25 = bf16[2,512,512]{2,1,0:T(8,128)(2,1)} copy(bf16[2,512,512]{2,0,1:T(2,128)(2,1)} %bitcast.26) | data formatting | bytes 2097152 | tf_op jit(solution)/shard_map/transpose | solution.py:895
  3.1 0.0 copy-done.1
  3.1 1.1 copy.26
  4.2 135.0 %shard_map.220 = (bf16[1024,512]{1,0:T(8,128)(2,1)}, f32[1024,512]{1,0:T(8,128)}, bf16[512,512]{1,0:T(8,128)(2,1)}, bf16[512,512]{1,0:T(8,128)(2,1)}, bf16[512,512]{1,0:T(8,128)(2,1)}, /*index=5*/f32[8,512]{1,0:T(8,128)}) custom-call(s32[2]{0:T(128)} %refs_0_.1, bf16[1024,512]{1,0:T(8,128)(2,1)} %bitcast.22, bf16[1024,512]{1,0:T(8,128)(2,1)} %bitcast.23, ...), custom_call_target="tpu_custom_call" | custom-call | tf_op jit(solution)/shard_map/pallas_call | solution.py:863
  139.3 0.0 copy-start
  139.3 3.4 %copy.33 = bf16[2,512,512]{2,0,1:T(2,128)(2,1)} copy(bf16[2,512,512]{2,1,0:T(8,128)(2,1)} %bitcast.29) | data formatting | bytes 2097152 | tf_op jit(solution)/shard_map/reshape | solution.py:979
  142.7 0.0 copy-done
  142.7 0.0 copy-start.5
  142.7 0.0 copy-start.4
  142.7 0.0 copy-start.3
  142.7 2.9 %copy.32 = f32[2,512,512]{2,0,1:T(2,128)} copy(f32[2,512,512]{2,1,0:T(8,128)S(1)} %bitcast.25) | data formatting | bytes 4194304 | tf_op jit(solution)/shard_map/reshape | solution.py:979
  145.7 0.0 copy-start.2
  145.7 0.0 copy-done.5
  145.7 0.6 fusion
  146.3 0.0 copy-done.4
  146.3 1.1 convert_element_type.19
  147.4 0.0 copy-done.3
  147.4 1.1 convert_element_type.20
  148.5 0.0 copy-done.2
  148.5 0.9 convert_bitcast_fusion
  149.4 0.8 copy.29
Async XLA Ops:
  0.6 2.5 %copy-start.1 = (bf16[512,2,512]{2,1,0:T(2,128)(2,1)S(1)}, bf16[512,2,512]{2,1,0:T(2,128)(2,1)}, u32[]{:S(2)}) copy-start(bf16[512,2,512]{2,1,0:T(2,128)(2,1)} %param.25) | copy-start | bytes 3145732
  139.3 3.4 %copy-start = (f32[1024,512]{1,0:T(8,128)S(1)}, f32[1024,512]{1,0:T(8,128)}, u32[]{:S(2)}) copy-start(f32[1024,512]{1,0:T(8,128)} %get-tuple-element.19) | copy-start | bytes 6291460
  142.7 3.0 %copy-start.5 = (f32[8,512]{1,0:T(8,128)S(1)}, f32[8,512]{1,0:T(8,128)}, u32[]{:S(2)}) copy-start(f32[8,512]{1,0:T(8,128)} %get-tuple-element.23) | copy-start | bytes 49156
  142.7 3.5 %copy-start.4 = (bf16[512,512]{1,0:T(8,128)(2,1)S(1)}, bf16[512,512]{1,0:T(8,128)(2,1)}, u32[]{:S(2)}) copy-start(bf16[512,512]{1,0:T(8,128)(2,1)} %get-tuple-element.21) | copy-start | bytes 1572868
  142.7 4.7 %copy-start.3 = (bf16[512,512]{1,0:T(8,128)(2,1)S(1)}, bf16[512,512]{1,0:T(8,128)(2,1)}, u32[]{:S(2)}) copy-start(bf16[512,512]{1,0:T(8,128)(2,1)} %get-tuple-element.22) | copy-start | bytes 1572868
  145.7 2.8 %copy-start.2 = (bf16[512,512]{1,0:T(8,128)(2,1)S(1)}, bf16[512,512]{1,0:T(8,128)(2,1)}, u32[]{:S(2)}) copy-start(bf16[512,512]{1,0:T(8,128)(2,1)} %get-tuple-element.20) | copy-start | bytes 1572868

commit v3 on v2

v3 whole, which is shorter than its diff:
```python
import types

import jax
import jax.numpy as jnp
from jax import lax
from jax.experimental import pallas as pl
from jax.experimental.pallas import tpu as pltpu
from jax.sharding import PartitionSpec as P

HD = 64
BLK = 16
NEG = -1e30
FLOOR = -1e29
EPS = 1e-05
LOC = 512
ND = 2
D = 512
FF = 2048
NMP = 4
HALF = 256
T = ND * LOC
HEADS = D // HD
LEVELS = 7
LOCAL_LEVELS = 5
EXT = 1024
RT = 512
G = [LOC >> lev for lev in range(LEVELS)]
OFF = [sum(G[:lev]) for lev in range(LEVELS)]
bf16 = jnp.bfloat16
f32 = jnp.float32
i32 = jnp.int32


def dot(a, b, ca=1, cb=0):
    return lax.dot_general(a, b, (((ca,), (cb,)), ((), ())), preferred_element_type=f32)


def iota(shape, axis):
    return lax.broadcasted_iota(i32, shape, axis)


def loop(n, body):
    lax.fori_loop(0, n, lambda i, c: (body(i), c)[1], 0)


def rows_at(i, size):
    return pl.ds(pl.multiple_of(i * size, size), size)


def own_groups(e):
    size = jnp.zeros_like(e)
    start = jnp.zeros_like(e)
    for lev in range(LEVELS):
        here = (e >= OFF[lev]) & (e < OFF[lev] + G[lev])
        size = jnp.where(here, 1 << lev, size)
        start = jnp.where(here, (e - OFF[lev]) << lev, start)
    return size, start


def key_groups(e, z):
    size, start = own_groups(e)
    start = start + z * LOC
    near = z + 1 - 2 * lax.rem(z, 2)
    far = 1 - z // 2
    size = jnp.where(e >= OFF[5], 32, size)
    start = jnp.where(e >= OFF[5], near * LOC + (e - OFF[5]) * 32, start)
    size = jnp.where(e >= OFF[6], 64, size)
    start = jnp.where(e >= OFF[6], far * 2 * LOC + (e - OFF[6]) * 64, start)
    return size, start


def count_live(size, start, length):
    return jnp.clip(length - start, 0, size).astype(f32)


def build_tables(r, z, d):
    r.ee[d] = head_map(d)
    length = r.lens[d]
    inv, inv_size = inv_counts(r, z, d)
    r.inv[d] = inv
    r.inv[ND] = inv_size

    def chunk(c):
        at = pl.ds(pl.multiple_of(d * EXT + c * 128, 128), 128)
        e_col = iota((128, 128), 0) + c * 128
        size, start = key_groups(e_col, z)
        r.cc[at, :] = count_live(size, start, length).astype(bf16)
        e_row = iota((1, 128), 1) + c * 128
        size, start = key_groups(e_row, z)
        dead = count_live(size, start, length)
        r.crow[pl.ds(d * (EXT // 128) + c, 1), :] = dead
        q_blk, k_blk = e_col // BLK, jnp.broadcast_to(e_row // BLK, (128, 128))
        span = jnp.where(q_blk // 2 == k_blk // 2, 0.0, NEG)
        same = jnp.where(q_blk == k_blk, 0.0, NEG)
        cross = jnp.where(q_blk == k_blk, NEG, span)
        bias = jnp.where(e_col < LOC, span, jnp.where(e_col < OFF[5], cross, same))
        r.bias[at, :] = jnp.where(jnp.broadcast_to(dead, (128, 128)) > 0.0, bias, NEG).astype(bf16)

    loop(EXT // 128, chunk)


def build_maps(r):
    def tile(c):
        rows = rows_at(c, 128)
        size, start = own_groups(iota((128, LOC), 0) + c * 128 + LOC)
        pos = iota((128, LOC), 1)
        r.pool[rows, :] = ((pos >= start) & (pos < start + size)).astype(f32).astype(bf16)
        size, start = own_groups(iota((128, EXT - LOC), 1) + LOC)
        pos = iota((128, EXT - LOC), 0) + c * 128
        r.unpool[rows, :] = ((pos >= start) & (pos < start + size)).astype(f32).astype(bf16)

    loop((EXT - LOC) // 128, tile)


def inv_counts(r, z, d):
    e = iota((EXT - LOC, 128), 0) + LOC
    size, start = own_groups(e)
    cnt = count_live(size, start + z * LOC, r.lens[d])
    return 1.0 / jnp.maximum(cnt, 1.0), 1.0 / jnp.maximum(size, 1).astype(f32)


def wide(col):
    return jnp.concatenate([col] * (D // 128), axis=1)


def live_rows(r, z, d, first, count):
    pos = iota((count, D), 0) + first + z * LOC
    return pos < r.lens[d]


def stats(v):
    mean = jnp.mean(v, axis=-1, keepdims=True)
    cen = v - mean
    var = jnp.mean(cen * cen, axis=-1, keepdims=True)
    return cen, lax.rsqrt(var + EPS)


def by_document(dst, raw):
    def tile(t):
        v = raw[rows_at(t, 128)].astype(f32)
        for d in range(ND):
            at = pl.ds(pl.multiple_of(d * LOC + t * 128, 128), 128)
            dst[at, :] = v[:, d, :].astype(bf16)

    loop(LOC // 128, tile)


def norm_one(r):
    r.tops[...] = jnp.zeros_like(r.tops)
    r.sumz[...] = jnp.zeros_like(r.sumz)
    r.norms[...] = jnp.zeros_like(r.norms)

    def tile(t):
        rows = rows_at(t, RT)
        cen, rstd = stats(r.x[rows, :].astype(f32))
        r.h1[rows, :] = (cen * rstd * r.g1[...] + r.b1[...]).astype(bf16)

    loop(T // RT, tile)


def ext_rows(d, off, count):
    return pl.ds(d * EXT + off, count)


def attn_weight(r, t):
    return jnp.concatenate([r.wat[s, :, t * 128 : (t + 1) * 128] for s in range(NMP)], axis=1)


def pair_lanes(s):
    return pl.ds(pl.multiple_of(s * 128, 128), 128)


def project(r, z, shards):
    for d in range(ND):

        def tile(t, d=d):
            rows = pl.ds(pl.multiple_of(d * LOC + t * RT, RT), RT)
            at = pl.ds(pl.multiple_of(d * EXT + t * RT, RT), RT)
            w = [r.wat[s, :, 0:384] for s in shards]
            o = dot(r.h1[rows, :], jnp.concatenate(w, axis=1))
            live = iota((RT, 128), 0) + t * RT + z * LOC < r.lens[d]
            for i, s in enumerate(shards):
                lanes = pair_lanes(s)
                q, k, v = (o[:, i * 384 + j * 128 : i * 384 + (j + 1) * 128] for j in range(3))
                r.qe[at, lanes] = (q.astype(bf16).astype(f32) * (HD**-0.5)).astype(bf16)
                r.ke[at, lanes] = jnp.where(live, k, 0.0).astype(bf16)
                r.ve[at, lanes] = jnp.where(live, v, 0.0).astype(bf16)

        loop(LOC // RT, tile)


def pool_levels(r, shards):
    keep = OFF[5] - LOC
    for d in range(ND):
        fine = ext_rows(d, 0, LOC)
        x = [e[fine, pair_lanes(s)] for s in shards for e in (r.qe, r.ke, r.ve)]
        o = dot(r.pool[...], jnp.concatenate(x, axis=1))
        for i, s in enumerate(shards):
            lanes = pair_lanes(s)
            q, k, v = (o[:, i * 384 + j * 128 : i * 384 + (j + 1) * 128] for j in range(3))
            r.qe[ext_rows(d, LOC, LOC), lanes] = (q * r.inv[ND]).astype(bf16)
            k = k * r.inv[d]
            r.ke[ext_rows(d, LOC, keep), lanes] = k[:keep].astype(bf16)
            r.ve[ext_rows(d, LOC, keep), lanes] = v[:keep].astype(bf16)
            r.out5[2 * d, :, lanes] = k[keep : keep + 16].astype(bf16)
            r.out5[2 * d + 1, :, lanes] = v[keep : keep + 16].astype(bf16)
            last = [k[keep + 16 : keep + 24], v[keep + 16 : keep + 24]]
            r.out6[d, :, lanes] = jnp.concatenate(last, axis=0).astype(bf16)


def place_remote(r):
    for d in range(ND):
        for kv, e in enumerate((r.ke, r.ve)):
            far = [r.in6[j, d].astype(f32)[kv * 8 : kv * 8 + 8] for j in range(2)]
            e[ext_rows(d, OFF[5], 16), :] = r.in5[2 * d + kv]
            e[ext_rows(d, OFF[6], 16), :] = jnp.concatenate(far, axis=0).astype(bf16)


def split_heads(pair):
    first = iota(pair.shape, 1) < HD
    zero = jnp.zeros_like(pair)
    return jnp.concatenate([jnp.where(first, pair, zero), jnp.where(first, zero, pair)], axis=0)


def count_lanes(cc, d, p):
    lane = iota(cc.shape, 1)
    zero = jnp.zeros_like(cc)
    a = jnp.where(lane == d * HEADS + 2 * p, cc, zero)
    b = jnp.where(lane == d * HEADS + 2 * p + 1, cc, zero)
    return jnp.concatenate([a, b], axis=0)


def attend_step(r, c, d, s, tops, sums):
    lane = iota((128, 128), 1)
    at = pl.ds(pl.multiple_of(d * EXT + c * 128, 128), 128)
    bias = r.bias[at, :].astype(f32)
    lanes = pair_lanes(s)
    w = dot(r.qe[at, lanes], split_heads(r.ke[at, lanes]), 1, 1)
    parts = []
    for j in range(2):
        sj = w[:, j * 128 : (j + 1) * 128] + bias
        top = jnp.maximum(jnp.max(sj, axis=1, keepdims=True), FLOOR)
        parts.append(jnp.exp(sj - top))
        tops = jnp.where(lane == d * HEADS + 2 * s + j, top, tops)
    e = jnp.concatenate(parts, axis=1).astype(bf16)
    r.wts[pl.ds(pl.multiple_of(((c * ND + d) * 4 + s) * 128, 128), 128), :] = e
    cnt = count_lanes(r.cc[at, :], d, s)
    o = dot(e, jnp.concatenate([split_heads(r.ve[at, lanes]), cnt], axis=1))
    r.num[at, lanes] = o[:, :128]
    return tops, sums + o[:, 128:]


def attend_chunk(r, c, pairs):
    here = rows_at(c, 128)
    tops, sums = r.tops[here, :], r.sumz[here, :]
    for s in pairs:
        for d in range(ND):
            tops, sums = attend_step(r, c, d, s, tops, sums)
    r.tops[here, :] = tops
    r.sumz[here, :] = sums


def attend_own(r, s):
    def two(i):
        attend_chunk(r, 2 * i, (s,))
        attend_chunk(r, 2 * i + 1, (s,))

    loop(3, two)
    attend_chunk(r, 6, (s,))


def combine_sums(r):
    last = pl.ds(OFF[6], G[6])
    top = r.tops[last, :]
    tot = r.sumz[last, :]
    for lev in range(LEVELS - 2, -1, -1):
        n = G[lev]
        for half in range(2):
            r.up[pl.ds(half, n // 2, stride=2), :] = top
            r.up2[pl.ds(half, n // 2, stride=2), :] = tot
        at = pl.ds(OFF[lev], n)
        up_top = r.up[pl.ds(0, n), :]
        own = r.tops[at, :]
        top = jnp.maximum(own, up_top)
        a = jnp.exp(own - top)
        b = jnp.exp(up_top - top)
        tot = a * r.sumz[at, :] + b * r.up2[pl.ds(0, n), :]
        if lev == 0:
            used = iota(tot.shape, 1) < ND * HEADS
            inv = 1.0 / jnp.where(used, tot, 1.0)
            a, b = a * inv, b * inv
        r.fa[at, :] = a
        r.fb[at, :] = b


def high_low(v, axis):
    hi = v.astype(bf16).astype(f32)
    return jnp.concatenate([hi, v - hi], axis=axis).astype(bf16)


def spread(r, fac, d):
    return dot(high_low(fac, 1), r.ee[d])


def head_map(d):
    row = lax.rem(iota((256, D), 0), 128)
    return (row == d * HEADS + iota((256, D), 1) // HD).astype(f32).astype(bf16)


def up_map(n):
    return (iota((n, n), 0) // 2 == lax.rem(iota((n, n), 1), n // 2)).astype(f32).astype(bf16)


def down_map(n):
    return (lax.rem(iota((2 * n, n // 2), 0), n) // 2 == iota((2 * n, n // 2), 1)).astype(f32).astype(bf16)


def combine_values(r):
    for d in range(ND):
        cur = r.num[ext_rows(d, OFF[6], G[6]), :]
        for lev in range(LEVELS - 2, -1, -1):
            n = G[lev]
            parts = []
            step = min(n, 256)
            for t in range(n // step):
                at = pl.ds(OFF[lev] + t * step, step)
                here = ext_rows(d, OFF[lev] + t * step, step)
                fac = spread(r, jnp.concatenate([r.fa[at, :], r.fb[at, :]], axis=0), d)
                up = dot(up_map(step), high_low(cur[t * step // 2 : (t + 1) * step // 2], 0))
                parts.append(fac[:step] * r.num[here, :] + fac[step:] * up)
                if lev == 0:
                    r.ctx[pl.ds(d * LOC + t * step, step), :] = parts[-1].astype(bf16)
                    r.num[here, :] = parts[-1]
            cur = jnp.concatenate(parts, axis=0) if len(parts) > 1 else parts[0]


def spare_rows(t):
    per = LOC // RT
    return pl.ds(pl.multiple_of((t // per) * EXT + LOC + lax.rem(t, per) * RT, RT), RT)


def attn_out(r):
    def tile(t):
        rows = rows_at(t, RT)
        mid = r.x[rows, :].astype(f32) + dot(r.ctx[rows, :], attn_weight(r, 3), 1, 1)
        r.num[spare_rows(t), :] = mid
        cen, rstd = stats(mid)
        r.h2[rows, :] = (cen * rstd * r.g2[...] + r.b2[...]).astype(bf16)

    loop(T // RT, tile)


def ffn_inner(r, f):
    cols = rows_at(f, 512)
    n = 256
    for t in range(T // n):
        rows = pl.ds(t * n, n)
        pre = dot(r.h2[rows, :], r.wup[f])
        ga = dot(r.gy[rows, :], r.wdn[f], 1, 1)
        cdf = 0.5 + 0.5 * lax.erf(pre * (0.5**0.5))
        r.act[rows, cols] = (pre * cdf).astype(bf16)
        pdf = jnp.exp(pre * pre * -0.5) * 0.3989422804014327
        r.gp[rows, cols] = (ga * (cdf + pre * pdf)).astype(bf16)


def ffn_grads(r, f, k):
    cols = rows_at(f, 512)
    r.f_g[k, 0] = dot(r.h2[...], r.gp[:, cols], 0, 0).astype(bf16)
    r.f_g[k, 1] = dot(r.act[:, cols], r.gy[...], 0, 0).astype(bf16)


def norm_back(v, gain, gh, r, row):
    cen, rstd = stats(v)
    xhat = cen * rstd
    r.norms[row : row + 1, :] += jnp.sum(gh * xhat, axis=0, keepdims=True)
    r.norms[row + 1 : row + 2, :] += jnp.sum(gh, axis=0, keepdims=True)
    u = gh * gain
    return rstd * (
        u - jnp.mean(u, axis=-1, keepdims=True) - xhat * jnp.mean(u * xhat, axis=-1, keepdims=True)
    )


def ffn_outer(r, t):
    rows = rows_at(t, RT)
    mid = r.num[spare_rows(t), :]
    ffn = dot(r.act[rows, 0:512], r.wdn[0])
    gh2 = dot(r.gp[rows, 0:512], r.wup[0], 1, 1)
    for f in range(1, NMP):
        cols = slice(f * 512, (f + 1) * 512)
        ffn = ffn + dot(r.act[rows, cols], r.wdn[f])
        gh2 = gh2 + dot(r.gp[rows, cols], r.wup[f], 1, 1)
    r.mx[rows, :] = (mid + ffn).astype(bf16)
    g_mid = r.gy[rows, :].astype(f32) + norm_back(mid, r.g2[...], gh2, r, 2)
    r.gxs[rows, :] = g_mid
    r.gm[rows, :] = g_mid.astype(bf16)


def out_grads(r, z):
    r.gof[...] = dot(r.gm[...], r.ctx[...], 0, 0).astype(bf16)
    for k in range(NMP):
        r.o_g[k, 0] = r.gof[:, pair_lanes(shard_of(z, k))]


def at_lanes(base, s):
    return pl.ds(pl.multiple_of(base + s * 128, 128), 128)


def store_pair(r, d, off, count, v):
    hi = v.astype(bf16)
    r.act[pl.ds(off, count), d * D : (d + 1) * D] = hi
    r.act[pl.ds(off, count), (ND + d) * D : (ND + d + 1) * D] = (v - hi.astype(f32)).astype(bf16)


def context_grads(r):
    def tile(t):
        r.num[spare_rows(t), :] = dot(r.gm[rows_at(t, RT), :], attn_weight(r, 3))

    loop(T // RT, tile)


def attn_back_rows(r):
    lane_head = lax.rem(iota((2 * D, 128), 0), D) // HD
    n = 256
    for t in range(LOC // n):
        at = pl.ds(t * n, n)
        delta = jnp.zeros((n, 128), f32)
        for d in range(ND):
            gctx = r.num[ext_rows(d, LOC + t * n, n), :]
            sel = (lane_head + d * HEADS == iota((2 * D, 128), 1)).astype(f32).astype(bf16)
            delta = delta + dot(high_low(gctx * r.num[ext_rows(d, t * n, n), :], 1), sel)
            fac = spread(r, jnp.concatenate([r.fa[at, :], r.fb[at, :]], axis=0), d)
            store_pair(r, d, t * n, n, fac[:n] * gctx)
            down = high_low(fac[n:] * gctx, 0)
            r.hc[pl.ds((d * LOC + t * n) // 2, n // 2), :] = dot(down_map(n), down, 0, 0)
        r.dl[at, :] = r.fa[at, :] * delta
        r.up[at, :] = r.fb[at, :] * delta
    acc = r.up[pl.ds(0, LOC // 2, stride=2), :] + r.up[pl.ds(1, LOC // 2, stride=2), :]
    for lev in range(1, LEVELS - 1):
        n = G[lev]
        at = pl.ds(OFF[lev], n)
        r.dl[at, :] = r.fa[at, :] * acc
        r.up[pl.ds(0, n), :] = r.fb[at, :] * acc
        acc = r.up[pl.ds(0, n // 2, stride=2), :] + r.up[pl.ds(1, n // 2, stride=2), :]
    r.dl[pl.ds(OFF[6], 2 * G[6]), :] = jnp.concatenate([acc, jnp.zeros_like(acc)], 0)
    for d in range(ND):
        cur = r.hc[pl.ds(d * LOC // 2, LOC // 2), :]
        for lev in range(1, LEVELS - 1):
            n = G[lev]
            parts = []
            step = min(n, 256)
            for t in range(n // step):
                at = pl.ds(OFF[lev] + t * step, step)
                seg = cur[t * step : (t + 1) * step]
                fac = spread(r, jnp.concatenate([r.fa[at, :], r.fb[at, :]], axis=0), d)
                store_pair(r, d, OFF[lev] + t * step, step, fac[:step] * seg)
                down = high_low(fac[step:] * seg, 0)
                parts.append(dot(down_map(step), down, 0, 0))
            cur = jnp.concatenate(parts, axis=0) if len(parts) > 1 else parts[0]
        store_pair(r, d, OFF[6], 2 * G[6], jnp.concatenate([cur, jnp.zeros_like(cur)], axis=0))


def attend_back_step(r, c, fine, s, d):
    top = iota((128, 128), 0) < HD
    lane = iota((128, 128), 1)
    lanes = pair_lanes(s)
    rows = rows_at(c, 128)
    dl = r.dl[rows, :]
    at = pl.ds(pl.multiple_of(d * EXT + c * 128, 128), 128)
    cnt = jnp.broadcast_to(r.crow[pl.ds(d * (EXT // 128) + c, 1), :], (128, 128))
    g = r.act[rows, at_lanes(d * D, s)]
    low = r.act[rows, at_lanes((ND + d) * D, s)]
    q = r.qe[at, lanes]
    kcat = split_heads(r.ke[at, lanes])
    vcat = split_heads(r.ve[at, lanes])
    dp = dot(jnp.concatenate([g, low], axis=1), jnp.concatenate([vcat, vcat], axis=1), 1, 1)
    e = r.wts[pl.ds(pl.multiple_of(((c * ND + d) * 4 + s) * 128, 128), 128), :]
    parts = []
    for j in range(2):
        half = slice(j * 128, (j + 1) * 128)
        mine = jnp.where(lane == d * HEADS + 2 * s + j, dl, 0.0)
        delta = jnp.sum(mine, axis=1, keepdims=True)
        parts.append(e[:, half].astype(f32) * (dp[:, half] - delta * cnt))
    ds = jnp.concatenate(parts, axis=1).astype(bf16)
    dq = dot(ds, kcat)
    dk = dot(q, ds, 0, 0)
    dk = jnp.where(top, dk[:, :128], dk[:, 128:]).T
    if fine:
        r.num[at, lanes] = dq
        r.num[pl.ds(pl.multiple_of(d * EXT + LOC + c * 128, 128), 128), lanes] = dk
    else:
        coarse = at_lanes((ND + d) * D, s)
        r.gp[rows_at(c - LOC // 128, 128), coarse] = dq.astype(bf16)
        r.gp[rows_at(c, 128), coarse] = dk.astype(bf16)


def attend_back_chunk(r, c, fine, pairs):
    for s in pairs:
        for d in range(ND):
            attend_back_step(r, c, fine, s, d)


def values_back(r, c, s):
    top = iota((128, 128), 0) < HD
    rows = rows_at(c, 128)
    for d in range(ND):
        g = r.act[rows, at_lanes(d * D, s)]
        slot = pl.ds(pl.multiple_of(((c * ND + d) * 4 + s) * 128, 128), 128)
        dv = dot(g, r.wts[slot, :], 0, 0)
        r.gp[rows, at_lanes(d * D, s)] = jnp.where(top, dv[:, :128], dv[:, 128:]).T.astype(bf16)


def attend_back_pair(r, s):
    for c in range(4):
        attend_back_chunk(r, c, True, (s,))
    for c in range(4, 7):
        attend_back_chunk(r, c, False, (s,))
    for c in range(7):
        values_back(r, c, s)


def coarse_grad(r, kv, d, first, count, cols):
    base = d * D if kv else (ND + d) * D
    if cols is None:
        return r.gp[pl.ds(first, count), base : base + D]
    return r.gp[pl.ds(first, count), at_lanes(base, cols)]


def save_remote(r):
    for d in range(ND):
        last = []
        for kv in range(2):
            r.out5[2 * d + kv] = coarse_grad(r, kv, d, OFF[5], 16, None)
            last.append(coarse_grad(r, kv, d, OFF[6], 16, None).astype(f32))
        for j in range(2):
            rows = [v[j * 8 : j * 8 + 8] for v in last]
            r.back6[j, d] = jnp.concatenate(rows, axis=0).astype(bf16)


def coarse_rows(r, d, kv, s):
    keep = OFF[5] - LOC
    own = coarse_grad(r, kv, d, LOC, keep, s).astype(f32)
    lanes = pair_lanes(s)
    rest = jnp.zeros((LOC - keep - 24, 128), f32)
    far = r.far6[0, d, :, lanes].astype(f32) + r.far6[1, d, :, lanes].astype(f32)
    near = r.near5[2 * d + kv, :, lanes].astype(f32)
    return jnp.concatenate([own, near, far[kv * 8 : kv * 8 + 8], rest], axis=0)


def unpool(r, z, s):
    lanes = pair_lanes(s)
    for d in range(ND):
        q = r.gp[pl.ds(0, LOC), at_lanes((ND + d) * D, s)].astype(f32) * r.inv[ND]
        k = coarse_rows(r, d, 0, s) * r.inv[d]
        v = coarse_rows(r, d, 1, s)
        o = dot(r.unpool[...], jnp.concatenate([q, k, v], axis=1).astype(bf16))
        rows = pl.ds(d * LOC, LOC)
        fine = ext_rows(d, 0, LOC)
        live = iota((LOC, 128), 0) + z * LOC < r.lens[d]
        q = r.num[fine, lanes] + o[:, :128]
        r.gq[rows, lanes] = (q * (HD**-0.5)).astype(bf16)
        k = r.num[ext_rows(d, LOC, LOC), lanes] + o[:, 128:256]
        r.gk[rows, lanes] = jnp.where(live, k, 0.0).astype(bf16)
        v = r.gp[pl.ds(0, LOC), at_lanes(d * D, s)].astype(f32) + o[:, 256:]
        r.gv[rows, lanes] = jnp.where(live, v, 0.0).astype(bf16)


def attn_grads(r, s, k):
    lanes = pair_lanes(s)
    g = jnp.concatenate([r.gq[:, lanes], r.gk[:, lanes], r.gv[:, lanes]], axis=1)
    r.a_g[k, 0] = dot(r.h1[...], g, 0, 0).astype(bf16)


def input_grads(r, t):
    rows = rows_at(t, RT)
    gh1 = dot(r.gq[rows, :], attn_weight(r, 0), 1, 1)
    gh1 = gh1 + dot(r.gk[rows, :], attn_weight(r, 1), 1, 1)
    gh1 = gh1 + dot(r.gv[rows, :], attn_weight(r, 2), 1, 1)
    x = r.x[rows, :].astype(f32)
    r.gxs[rows, :] = r.gxs[rows, :] + norm_back(x, r.g1[...], gh1, r, 0)


def shard_of(z, k):
    return lax.rem(z + NMP - k, NMP)


def remote(src, dst, send, recv, where):
    return pltpu.make_async_remote_copy(
        src_ref=src, dst_ref=dst, send_sem=send, recv_sem=recv, device_id=where,
        device_id_type=pl.DeviceIdType.MESH,
    )


class Links:
    def __init__(self, r, ndp):
        self.r, self.ndp, self.nq, self.piece = r, ndp, ndp // 2, LOC // ndp
        self.z, self.me = lax.axis_index("mp"), lax.axis_index("dp")
        self.c, self.q = lax.rem(self.me, 2), self.me // 2
        self.other = 2 * self.q + 1 - self.c
        self.near = self.z + 1 - 2 * lax.rem(self.z, 2)
        self.far = (1 - self.z // 2) * 2
        self.par = lax.rem(self.z, 2)
        self.sent = []

    def mp_peer(self, k):
        return lax.rem(self.z + k, NMP)

    def dp_peer(self, k):
        return lax.rem(self.me + k, self.ndp)

    def quarter(self, j):
        return lax.rem(self.q + j, self.nq)

    def piece_rows(self, q):
        return pl.ds(pl.multiple_of(self.c * HALF + q * self.piece, self.piece), self.piece)

    def rows_of(self, dev):
        first = lax.rem(dev, 2) * HALF + (dev // 2) * self.piece
        return pl.ds(pl.multiple_of(first, self.piece), self.piece)

    def half(self, c):
        return pl.ds(pl.multiple_of(c * HALF, HALF), HALF)

    def send(self, src, dst, send, recv, where):
        copy = remote(src, dst, send, recv, where)
        copy.start()
        self.sent.append(copy)

    def arrive(self, dst, send, recv, where):
        remote(dst, dst, send, recv, where).wait_recv()

    def greet(self):
        sem = pltpu.get_barrier_semaphore()
        for k in range(1, NMP):
            pl.semaphore_signal(sem, inc=1, device_id={"mp": self.mp_peer(k)})
        for k in range(1, self.ndp):
            pl.semaphore_signal(sem, inc=1, device_id={"dp": self.dp_peer(k)})

    def barrier(self):
        pl.semaphore_wait(pltpu.get_barrier_semaphore(), NMP + self.ndp - 2)

    def gather_z(self, m, k):
        w, cols = self.weights[m]
        i = m * 3 + k - 1
        piece = w.at[self.z, self.rows_of(self.me), cols]
        self.send(piece, piece, self.r.wz_s.at[i], self.r.wz_r.at[i], {"mp": self.mp_peer(k)})

    def gather_plane(self, m, k):
        w, cols = self.weights[m]
        i = m * 3 + k - 1
        piece = w.at[shard_of(self.z, k), self.rows_of(self.me), cols]
        self.arrive(piece, self.r.wz_s.at[i], self.r.wz_r.at[i], {"mp": self.mp_peer(k)})
        for j in range(1, self.nq):
            n = i * (self.nq - 1) + j - 1
            where = {"dp": 2 * self.quarter(j) + self.c}
            self.send(piece, piece, self.r.wp_s.at[n], self.r.wp_r.at[n], where)

    def gather_core(self, m, k):
        w, cols = self.weights[m]
        i = m * 3 + k - 1
        shard = shard_of(self.z, k)
        for j in range(1, self.nq):
            n = i * (self.nq - 1) + j - 1
            got = w.at[shard, self.piece_rows(self.quarter(self.nq - j)), cols]
            where = {"dp": 2 * self.quarter(j) + self.c}
            self.arrive(got, self.r.wp_s.at[n], self.r.wp_r.at[n], where)
        start(self.gather_core_copies(m, k))

    def gather_core_copies(self, m, k):
        w, cols = self.weights[m]
        i = m * 3 + k - 1
        part = w.at[shard_of(self.z, k), self.half(self.c), cols]
        return [remote(part, part, self.r.wc_s.at[i], self.r.wc_r.at[i], {"dp": self.other})]

    def gather_done(self, m, k):
        w, cols = self.weights[m]
        i = m * 3 + k - 1
        part = w.at[shard_of(self.z, k), self.half(1 - self.c), cols]
        self.arrive(part, self.r.wc_s.at[i], self.r.wc_r.at[i], {"dp": self.other})

    def coarse_copies(self, here5, here6, there5, there6, sems):
        a, b = sems
        send = [remote(here5, there5, a.at[0], b.at[0], {"mp": self.near})]
        for j in range(2):
            where = {"mp": self.far + j}
            dst = there6.at[self.par]
            send.append(remote(here6[j], dst, a.at[1 + j], b.at[1 + self.par], where))
        return send

    def coarse_start(self, *args):
        self.coarse = self.coarse_copies(*args)
        start(self.coarse)

    def coarse_arrive(self, there5, there6, sems):
        a, b = sems
        self.arrive(there5, a.at[0], b.at[0], {"mp": self.near})
        for j in range(2):
            self.arrive(there6.at[j], a.at[1 + j], b.at[1 + j], {"mp": self.far + j})

    def coarse_send(self):
        r = self.r
        self.coarse_start(r.out5, (r.out6, r.out6), r.in5, r.in6, (r.cf_s, r.cf_r))

    def coarse_wait(self):
        r = self.r
        self.coarse_arrive(r.in5, r.in6, (r.cf_s, r.cf_r))

    def coarse_clear(self):
        for copy in self.coarse:
            copy.wait_send()

    def coarse_back(self):
        r = self.r
        here = (r.back6.at[0], r.back6.at[1])
        self.coarse_start(r.out5, here, r.near5, r.far6, (r.cb_s, r.cb_r))

    def coarse_back_wait(self):
        r = self.r
        self.coarse_arrive(r.near5, r.far6, (r.cb_s, r.cb_r))

    def norms_z(self):
        r = self.r
        r.nz[self.z] = r.norms[...]
        for k in range(1, NMP):
            dst = r.nz.at[self.z]
            where = {"mp": self.mp_peer(k)}
            self.send(r.norms, dst, r.nz_s.at[k - 1], r.nz_r.at[k - 1], where)

    def norms_dp(self):
        r = self.r
        for k in range(1, NMP):
            got = r.nz.at[self.mp_peer(NMP - k)]
            self.arrive(got, r.nz_s.at[k - 1], r.nz_r.at[k - 1], {"mp": self.mp_peer(k)})
        tot = r.nz[0]
        for k in range(1, NMP):
            tot = tot + r.nz[k]
        r.np[self.me] = tot
        for k in range(1, self.ndp):
            dst = r.np.at[self.me]
            where = {"dp": self.dp_peer(k)}
            self.send(dst, dst, r.np_s.at[k - 1], r.np_r.at[k - 1], where)

    def norms_done(self):
        r = self.r
        for k in range(1, self.ndp):
            got = r.np.at[self.dp_peer(self.ndp - k)]
            self.arrive(got, r.np_s.at[k - 1], r.np_r.at[k - 1], {"dp": self.dp_peer(k)})
        tot = r.np[0]
        for k in range(1, self.ndp):
            tot = tot + r.np[k]
        r.onorm[...] = tot

    def finish(self):
        cores = [c for m in range(4) for k in (1, 2, 3) for c in self.gather_core_copies(m, k)]
        for copy in self.sent + cores:
            copy.wait_send()


def start(copies):
    for copy in copies:
        copy.start()


class Sum:
    def __init__(self, net, r, name):
        self.net = net
        for n in ("g", "rc", "rp", "pz", "rz", "fin", "c_s", "c_r", "p_s", "p_r", "z_s", "z_r", "s_s", "s_r"):
            setattr(self, n, getattr(r, name + "_" + n))
        self.parts = self.g.shape[1]

    def core_copies(self, k):
        net = self.net
        src = self.g.at[k, :, net.half(1 - net.c), :]
        return [remote(src, self.rc.at[k], self.c_s.at[k], self.c_r.at[k], {"dp": net.other})]

    def plane_copies(self, k):
        net, copies = self.net, []
        for j in range(1, net.nq):
            n = k * (net.nq - 1) + j - 1
            to = net.quarter(j)
            src = self.g.at[k, :, net.piece_rows(to), :]
            where = {"dp": 2 * to + net.c}
            copies.append(remote(src, self.rp.at[k, j - 1], self.p_s.at[n], self.p_r.at[n], where))
        return copies

    def z_copies(self, k):
        where = {"mp": shard_of(self.net.z, k)}
        src, dst = self.pz.at[k - 1], self.rz.at[k - 1]
        return [remote(src, dst, self.z_s.at[k - 1], self.z_r.at[k - 1], where)]

    def share_copies(self):
        net, copies = self.net, []
        part = self.fin.at[:, net.rows_of(net.me), :]
        for j in range(1, net.nq):
            where = {"dp": 2 * net.quarter(j) + net.c}
            copies.append(remote(part, part, self.s_s.at[j - 1], self.s_r.at[j - 1], where))
        return copies

    def share_core_copies(self):
        net = self.net
        n = net.nq - 1
        part = self.fin.at[:, net.half(net.c), :]
        return [remote(part, part, self.s_s.at[n], self.s_r.at[n], {"dp": net.other})]

    def core(self, k):
        start(self.core_copies(k))

    def plane(self, k):
        net = self.net
        net.arrive(self.rc.at[k], self.c_s.at[k], self.c_r.at[k], {"dp": net.other})

        def add(i):
            a, b = i // 2, lax.rem(i, 2)
            rows = pl.ds(pl.multiple_of(net.c * HALF + b * 128, 128), 128)
            more = self.rc[k, a, rows_at(b, 128), :].astype(f32)
            self.g[k, a, rows, :] = (self.g[k, a, rows, :].astype(f32) + more).astype(bf16)

        loop(2 * self.parts, add)
        start(self.plane_copies(k))

    def total(self, k):
        net = self.net
        for j in range(1, net.nq):
            n = k * (net.nq - 1) + j - 1
            where = {"dp": 2 * net.quarter(j) + net.c}
            net.arrive(self.rp.at[k, j - 1], self.p_s.at[n], self.p_r.at[n], where)
        tots = []
        for a in range(self.parts):
            tot = self.g[k, a, net.piece_rows(net.q), :].astype(f32)
            for j in range(net.nq - 1):
                tot = tot + self.rp[k, j, a].astype(f32)
            tots.append(tot)
        return tots

    def pass_on(self, k):
        for a, tot in enumerate(self.total(k)):
            self.pz[k - 1, a] = tot.astype(bf16)
        start(self.z_copies(k))

    def share(self):
        net = self.net
        tots = self.total(0)
        for k in range(1, NMP):
            where = {"mp": shard_of(net.z, k)}
            net.arrive(self.rz.at[k - 1], self.z_s.at[k - 1], self.z_r.at[k - 1], where)
            tots = [tot + self.rz[k - 1, a].astype(f32) for a, tot in enumerate(tots)]
        mine = net.rows_of(net.me)
        for a, tot in enumerate(tots):
            self.fin[a, mine, :] = tot.astype(bf16)
        start(self.share_copies())

    def share_core(self):
        net = self.net
        for j in range(1, net.nq):
            got = self.fin.at[:, net.piece_rows(net.quarter(net.nq - j)), :]
            where = {"dp": 2 * net.quarter(j) + net.c}
            net.arrive(got, self.s_s.at[j - 1], self.s_r.at[j - 1], where)
        start(self.share_core_copies())

    def done(self):
        net = self.net
        n = net.nq - 1
        part = self.fin.at[:, net.half(1 - net.c), :]
        net.arrive(part, self.s_s.at[n], self.s_r.at[n], {"dp": net.other})

    def finish(self):
        def step(k):
            for copy in self.core_copies(k) + self.plane_copies(k):
                copy.wait_send()

        loop(NMP, step)
        last = [copy for k in range(1, NMP) for copy in self.z_copies(k)]
        for copy in last + self.share_copies() + self.share_core_copies():
            copy.wait_send()


def whole_kernel(ndp, r):
    net = Links(r, ndp)
    z = net.z
    r.gq, r.gk, r.gv = (e.at[pl.ds(0, T), :] for e in (r.qe, r.ke, r.ve))
    net.weights = (
        (r.wat, pl.ds(0, 384)),
        (r.wup, pl.ds(0, 512)),
        (r.wdn, pl.ds(0, 512)),
        (r.wat, pl.ds(384, 128)),
    )
    r.mx, r.gof = r.h2, r.pool
    r.fa, r.fb = r.tops, r.sumz
    net_f, net_o, net_a = (Sum(net, r, n) for n in "foa")
    shard = [shard_of(z, k) for k in range(NMP)]
    loads = [pltpu.make_async_copy(r.x_in, r.raw, r.ld.at[0])]
    for i, w in enumerate((r.w_query, r.w_key, r.w_value)):
        dst = r.wat.at[z, :, pl.ds(i * 128, 128)]
        loads.append(pltpu.make_async_copy(w, dst, r.ld.at[1 + i]))
    loads.append(pltpu.make_async_copy(r.w_up, r.wup.at[z], r.ld.at[4]))
    loads.append(pltpu.make_async_copy(r.w_down, r.wdn.at[z], r.ld.at[5]))
    start(loads)
    net.greet()
    loads[0].wait()
    by_document(r.x, r.raw)
    load_gy = pltpu.make_async_copy(r.gy_in, r.raw, r.ld.at[6])
    load_gy.start()
    norm_one(r)
    r.wat[z, :, pl.ds(384, 128)] = r.w_output[...].T
    for copy in loads[1:4]:
        copy.wait()
    net.barrier()
    for m in (0, 3):
        for k in (1, 2, 3):
            net.gather_z(m, k)
    for copy in loads[4:]:
        copy.wait()
    build_tables(r, z, 0)
    build_tables(r, z, 1)
    for m in (0, 3):
        for k in (1, 2, 3):
            net.gather_plane(m, k)
    for k in (1, 2, 3):
        net.gather_z(1, k)
        net.gather_z(2, k)
    build_maps(r)
    project(r, z, shard[:1])
    pool_levels(r, shard[:1])
    for k in (1, 2, 3):
        net.gather_core(0, k)
    attend_own(r, shard[0])
    for m in (1, 2):
        net.gather_plane(m, 1)
    for k in (1, 2, 3):
        net.gather_done(0, k)
    project(r, z, shard[1:])
    for k in (1, 2, 3):
        net.gather_core(3, k)
    for m in (1, 2):
        net.gather_plane(m, 2)
    pool_levels(r, shard[1:])
    net.coarse_send()
    for m in (1, 2):
        net.gather_plane(m, 3)
    for c in range(7):
        attend_chunk(r, c, shard[1:])
    net.coarse_wait()
    net.coarse_clear()
    place_remote(r)
    attend_chunk(r, EXT // 128 - 1, range(NMP))
    combine_sums(r)
    load_gy.wait()
    by_document(r.gy, r.raw)
    combine_values(r)
    for k in (1, 2, 3):
        net.gather_done(3, k)
    attn_out(r)

    def ffn_step(k):
        f = shard_of(z, k)

        @pl.when(k > 0)
        def _():
            net.gather_done(1, k)
            net.gather_done(2, k)

        ffn_inner(r, f)

        @pl.when(k < NMP - 1)
        def _():
            net.gather_core(1, k + 1)
            net.gather_core(2, k + 1)

        ffn_grads(r, f, k)
        net_f.core(k)

        @pl.when(k > 0)
        def _():
            net_f.plane(k - 1)

    loop(NMP, ffn_step)
    ffn_outer(r, 0)
    net_f.plane(3)
    ffn_outer(r, 1)
    put_mixed = pltpu.make_async_copy(r.mx, r.mixed, r.st.at[0])
    put_mixed.start()
    out_grads(r, z)
    for k in range(NMP):
        net_o.core(k)
    net_f.pass_on(1)
    context_grads(r)
    attn_back_rows(r)
    for k in range(NMP):
        net_o.plane(k)
    attend_back_chunk(r, EXT // 128 - 1, False, range(NMP))
    for s in range(NMP):
        values_back(r, 7, s)
    save_remote(r)
    net.coarse_back()
    net_f.pass_on(2)

    def back_step(i):
        k = lax.rem(i + 1, NMP)
        s = shard_of(z, k)
        attend_back_pair(r, s)

        @pl.when(i == 0)
        def _():
            net.coarse_back_wait()

        unpool(r, z, s)

        @pl.when(i > 0)
        def _():
            net_a.plane(i)

        attn_grads(r, s, k)
        net_a.core(k)

        @pl.when(i == 0)
        def _():
            net_f.pass_on(3)
            for n in range(1, NMP):
                net_o.pass_on(n)

        @pl.when(i == 1)
        def _():
            net_f.share()

        @pl.when(i == 2)
        def _():
            net_o.share()
            net_f.share_core()

        @pl.when(i > 1)
        def _():
            net_a.pass_on(i - 1)

    loop(NMP, back_step)
    input_grads(r, 0)
    net_a.plane(0)
    net_o.share_core()
    input_grads(r, 1)
    net_a.pass_on(3)
    net.norms_z()
    put_gx = pltpu.make_async_copy(r.gxs, r.gx, r.st.at[1])
    put_gx.start()
    net_f.done()
    net_o.done()
    stores = [put_mixed, put_gx]
    for i, (a, b) in enumerate(((r.f_fin, r.ofn), (r.o_fin, r.oot), (r.a_fin, r.oat))):
        stores.append(pltpu.make_async_copy(a, b, r.st.at[2 + i]))
    start(stores[2:4])
    net_a.share()
    net.norms_dp()
    net_a.share_core()
    net.norms_done()
    net_a.done()
    start(stores[4:])
    for copy in stores:
        copy.wait()
    net.coarse_clear()
    net.finish()
    for each in (net_f, net_o, net_a):
        each.finish()


FAR_OUTS = ("mixed", "gx", "ofn", "oot", "oat")


def run(body, ins, outs, scratch, sems):
    names = list(ins) + list(outs) + list(scratch) + list(sems)

    def kernel(*refs):
        body(types.SimpleNamespace(**dict(zip(names, refs))))

    result = pl.pallas_call(
        kernel,
        out_shape=[jax.ShapeDtypeStruct(*v) for v in outs.values()],
        in_specs=[pl.BlockSpec(memory_space=space) for _, space in ins.values()],
        out_specs=[
            pl.BlockSpec(memory_space=pl.ANY if n in FAR_OUTS else pltpu.VMEM) for n in outs
        ],
        scratch_shapes=[pltpu.VMEM(*v) for v in scratch.values()]
        + [pltpu.SemaphoreType.DMA((n,)) for n in sems.values()],
        compiler_params=pltpu.CompilerParams(
            vmem_limit_bytes=63 * 1024 * 1024, collective_id=0, has_side_effects=True
        ),
    )(*[a for a, _ in ins.values()])
    return dict(zip(outs, result))


def per_device(
    ndp,
    tokens,
    lengths,
    gain_one,
    shift_one,
    w_query,
    w_key,
    w_value,
    w_output,
    gain_two,
    shift_two,
    w_up,
    w_down,
    cotangent,
):
    g1, b1, g2, b2 = (v.reshape(1, D) for v in (gain_one, shift_one, gain_two, shift_two))
    nq, piece = ndp // 2, LOC // ndp
    vmem, any_space = pltpu.VMEM, pl.ANY
    ins = dict(
        lens=(lengths, pltpu.SMEM),
        x_in=(tokens, any_space),
        gy_in=(cotangent, any_space),
        g1=(g1, vmem),
        b1=(b1, vmem),
        g2=(g2, vmem),
        b2=(b2, vmem),
        w_query=(w_query, any_space),
        w_key=(w_key, any_space),
        w_value=(w_value, any_space),
        w_output=(w_output, vmem),
        w_up=(w_up, any_space),
        w_down=(w_down, any_space),
    )
    outs = dict(
        mixed=((T, D), bf16),
        gx=((T, D), f32),
        ofn=((2, D, 512), bf16),
        oot=((1, D, 128), bf16),
        oat=((1, D, 384), bf16),
        onorm=((8, D), f32),
    )
    scratch = dict(
        x=((T, D), bf16),
        gy=((T, D), bf16),
        gxs=((T, D), f32),
        inv=((ND + 1, EXT - LOC, 128), f32),
        wat=((NMP, D, 512), bf16),
        wup=((NMP, D, 512), bf16),
        wdn=((NMP, 512, D), bf16),
        h1=((T, D), bf16),
        qe=((ND * EXT, D), bf16),
        ke=((ND * EXT, D), bf16),
        ve=((ND * EXT, D), bf16),
        pool=((EXT - LOC, LOC), bf16),
        unpool=((LOC, EXT - LOC), bf16),
        cc=((ND * EXT, 128), bf16),
        bias=((ND * EXT, 128), bf16),
        wts=((64 * 128, 256), bf16),
        num=((ND * EXT, D), f32),
        tops=((EXT, 128), f32),
        sumz=((EXT, 128), f32),
        up=((LOC, 128), f32),
        up2=((LOC, 128), f32),
        ctx=((T, D), bf16),
        h2=((T, D), bf16),
        act=((T, FF), bf16),
        gp=((T, FF), bf16),
        gm=((T, D), bf16),
        hc=((T // 2, D), f32),
        dl=((EXT, 128), f32),
        ee=((ND, 256, D), bf16),
        crow=((ND * EXT // 128, 128), f32),
        raw=((LOC, ND, D), bf16),
        out5=((2 * ND, 16, D), bf16),
        out6=((ND, 16, D), bf16),
        in5=((2 * ND, 16, D), bf16),
        in6=((2, ND, 16, D), bf16),
        back6=((2, ND, 16, D), bf16),
        near5=((2 * ND, 16, D), bf16),
        far6=((2, ND, 16, D), bf16),
        norms=((8, D), f32),
        nz=((NMP, 8, D), f32),
        np=((ndp, 8, D), f32),
    )
    counts = dict(wz=12, wp=12 * (nq - 1), wc=12, cf=3, cb=3, nz=3, np=ndp - 1)
    for n, a, cols in (("f", 2, 512), ("o", 1, 128), ("a", 1, 384)):
        scratch[n + "_g"] = ((NMP, a, 512, cols), bf16)
        scratch[n + "_rc"] = ((NMP, a, HALF, cols), bf16)
        scratch[n + "_rp"] = ((NMP, nq - 1, a, piece, cols), bf16)
        scratch[n + "_pz"] = ((NMP - 1, a, piece, cols), bf16)
        scratch[n + "_rz"] = ((NMP - 1, a, piece, cols), bf16)
        scratch[n + "_fin"] = ((a, 512, cols), bf16)
        counts.update({n + "_c": NMP, n + "_p": NMP * (nq - 1), n + "_z": NMP - 1, n + "_s": nq})
    sems = dict(ld=7, st=5)
    for n, count in counts.items():
        sems[n + "_s"] = count
        sems[n + "_r"] = count
    o = run(lambda r: whole_kernel(ndp, r), ins, outs, scratch, sems)

    outs = emit(o)
    return (*outs, *(o["onorm"][i] for i in range(4)))


def emit_kernel(mixed, gx, fn, at, ot, o_mixed, o_gx, o_q, o_k, o_v, o_o, o_up, o_dn):
    for d in range(ND):
        o_mixed[:, d, :] = mixed[d]
        o_gx[:, d, :] = gx[d]
    for i, out in enumerate((o_q, o_k, o_v)):
        out[...] = at[0, :, i * 128 : (i + 1) * 128].astype(f32)
    o_up[...] = fn[0].astype(f32)
    o_dn[...] = fn[1].astype(f32)
    o_o[...] = ot[0].astype(f32).T


def emit(o):
    n = 4
    rows = LOC // n

    def tiles(*shape, axis):
        block = tuple(rows if i == axis else size for i, size in enumerate(shape))
        return pl.BlockSpec(block, lambda i: tuple(i if a == axis else 0 for a in range(len(shape))))

    doc = tiles(ND, LOC, D, axis=1)
    pos = tiles(LOC, ND, D, axis=0)
    third, whole = tiles(512, 128, axis=0), tiles(512, D, axis=0)
    shape = jax.ShapeDtypeStruct
    return pl.pallas_call(
        emit_kernel,
        grid=(n,),
        in_specs=[
            doc,
            doc,
            tiles(2, 512, 512, axis=1),
            tiles(1, 512, 384, axis=1),
            tiles(1, 512, 128, axis=1),
        ],
        out_specs=[pos, pos, third, third, third, tiles(128, D, axis=1), whole, whole],
        out_shape=[shape((LOC, ND, D), bf16), shape((LOC, ND, D), f32)]
        + [shape((D, 128), f32)] * 3
        + [shape((128, D), f32), shape((D, 512), f32), shape((512, D), f32)],
    )(o["mixed"].reshape(ND, LOC, D), o["gx"].reshape(ND, LOC, D), o["ofn"], o["oat"], o["oot"])


def solution(mesh):
    tok = P("mp", "dp", None)
    col, row, rep = P(None, "mp"), P("mp", None), P()
    ndp = mesh.shape["dp"]
    return jax.shard_map(
        lambda *args: per_device(ndp, *args),
        mesh=mesh,
        in_specs=(tok, P("dp"), rep, rep, col, col, col, row, rep, rep, col, row, tok),
        out_specs=(tok, tok, col, col, col, row, col, row, rep, rep, rep, rep),
        check_vma=False,
    )
```

time: 150 us -> 123 us (0.82)
  Pallas kernels: 135 us -> 120 us
  local copies, waits for them, and re-layouts: 11.4 us -> 1.46 us
  other arithmetic: 3.11 us -> 0 us
    pallas_call x1, Pallas kernels: 135 us -> 114 us  [run(): pl.pallas_call(kernel, out_shape=[jax.ShapeDtypeStruct(*v) for v in outs....]
    reshape x2 -> x0, local copies, waits for them, and re-layouts: 6.36 us -> none  [back_to(): return jnp.swapaxes(a.reshape(ND, LOC, D), 0, 1)]
    pallas_call x0 -> x1, Pallas kernels: none -> 5.88 us  [emit(): pl.pallas_call(emit_kernel, grid=(n,), in_specs=[doc, doc, tiles(2, 512,...]
    transpose x2 -> x0, local copies, waits for them, and re-layouts: 3.58 us -> none  [the longest x1 2.45 us: per_device(): x = jnp.swapaxes(tokens, 0, 1).reshape(T, D)]
    convert_element_type x2 -> x0, other arithmetic: 2.21 us -> none  [the longest x1 1.1 us: per_device(): o['odn'].astype(f32)]
where the time goes in v3:
time: 123 us; the launch traced here: 122 us
  Pallas kernels  120 us (98%)
  local copies, waits for them, and re-layouts  1.46 us (1%)
    pallas_call x1, Pallas kernels, run(): pl.pallas_call(kernel, out_shape=[jax.ShapeDtypeStruct(*v) for v in outs....  114 us
    pallas_call x1, Pallas kernels, emit(): pl.pallas_call(emit_kernel, grid=(n,), in_specs=[doc, doc, tiles(2, 512,...  5.88 us

profile of v3, /device:TPU:0, one launch (start us, length us, event | category | flops | bytes accessed | tf_op | source)
XLA Modules:
  0.0 121.9 jit_solution(10542032317537315772)
XLA Ops:
  0.6 113.7 %shard_map.220 = (bf16[1024,512]{1,0:T(8,128)(2,1)}, f32[1024,512]{1,0:T(8,128)}, bf16[2,512,512]{2,1,0:T(8,128)(2,1)}, bf16[1,512,128]{2,1,0:T(8,128)(2,1)}, bf...) custom-call(s32[2]{0:T(128)} %refs_0_.1, bf16[512,2,512]{2,1,0:T(2,128)(2,1)} %refs_1_.1, bf16[512,2,512]{2,1,0:T(2,128)(2,1)} %refs_2_.1, ...), custom_call_target="tpu_custom_call" | custom-call | tf_op jit(solution)/shard_map/pallas_call | solution.py:1071
  114.3 1.5 %fusion = (f32[1,512]{1,0:T(1,128)}, f32[1,512]{1,0:T(1,128)}, f32[1,512]{1,0:T(1,128)}, f32[1,512]{1,0:T(1,128)}) fusion(f32[8,512]{1,0:T(8,128)} %get-tuple-element.39), kind=kLoop, calls=%fused_computation | loop fusion | bytes 16384 | tf_op jit(solution)/shard_map/slice | solution.py:1188
  115.8 5.9 %shard_map.221 = (bf16[512,2,512]{2,1,0:T(2,128)(2,1)}, f32[512,2,512]{2,1,0:T(2,128)}, f32[512,128]{1,0:T(8,128)}, f32[512,128]{1,0:T(8,128)}, f32[512,128]{1,0...) custom-call(bf16[2,512,512]{2,1,0:T(8,128)(2,1)} %bitcast.11, f32[2,512,512]{2,1,0:T(8,128)} %bitcast.10, ...), custom_call_target="tpu_custom_call" | custom-call | tf_op jit(solution)/shard_map/pallas_call | solution.py:1214

commit v4 on v3

--- a/solution.py
+++ b/solution.py
@@ -638,43 +638,45 @@
     def barrier(self):
         pl.semaphore_wait(pltpu.get_barrier_semaphore(), NMP + self.ndp - 2)
 
+    def gather_peers(self):
+        for j in range(1, self.nq):
+            yield self.quarter(j), self.piece_rows(self.quarter(self.nq - j))
+
+    def part(self, m, shard, rows):
+        w, cols = self.weights[m]
+        return w.at[shard, :, rows, :] if cols is None else w.at[shard, rows, cols]
+
     def gather_z(self, m, k):
-        w, cols = self.weights[m]
         i = m * 3 + k - 1
-        piece = w.at[self.z, self.rows_of(self.me), cols]
+        piece = self.part(m, self.z, self.rows_of(self.me))
         self.send(piece, piece, self.r.wz_s.at[i], self.r.wz_r.at[i], {"mp": self.mp_peer(k)})
 
     def gather_plane(self, m, k):
-        w, cols = self.weights[m]
         i = m * 3 + k - 1
-        piece = w.at[shard_of(self.z, k), self.rows_of(self.me), cols]
+        piece = self.part(m, shard_of(self.z, k), self.rows_of(self.me))
         self.arrive(piece, self.r.wz_s.at[i], self.r.wz_r.at[i], {"mp": self.mp_peer(k)})
-        for j in range(1, self.nq):
-            n = i * (self.nq - 1) + j - 1
-            where = {"dp": 2 * self.quarter(j) + self.c}
+        for j, (to, _) in enumerate(self.gather_peers()):
+            n = i * (self.nq - 1) + j
+            where = {"dp": 2 * to + self.c}
             self.send(piece, piece, self.r.wp_s.at[n], self.r.wp_r.at[n], where)
 
     def gather_core(self, m, k):
-        w, cols = self.weights[m]
         i = m * 3 + k - 1
         shard = shard_of(self.z, k)
-        for j in range(1, self.nq):
-            n = i * (self.nq - 1) + j - 1
-            got = w.at[shard, self.piece_rows(self.quarter(self.nq - j)), cols]
-            where = {"dp": 2 * self.quarter(j) + self.c}
-            self.arrive(got, self.r.wp_s.at[n], self.r.wp_r.at[n], where)
+        for j, (to, rows) in enumerate(self.gather_peers()):
+            n = i * (self.nq - 1) + j
+            got = self.part(m, shard, rows)
+            self.arrive(got, self.r.wp_s.at[n], self.r.wp_r.at[n], {"dp": 2 * to + self.c})
         start(self.gather_core_copies(m, k))
 
     def gather_core_copies(self, m, k):
-        w, cols = self.weights[m]
         i = m * 3 + k - 1
-        part = w.at[shard_of(self.z, k), self.half(self.c), cols]
+        part = self.part(m, shard_of(self.z, k), self.half(self.c))
         return [remote(part, part, self.r.wc_s.at[i], self.r.wc_r.at[i], {"dp": self.other})]
 
     def gather_done(self, m, k):
-        w, cols = self.weights[m]
         i = m * 3 + k - 1
-        part = w.at[shard_of(self.z, k), self.half(1 - self.c), cols]
+        part = self.part(m, shard_of(self.z, k), self.half(1 - self.c))
         self.arrive(part, self.r.wc_s.at[i], self.r.wc_r.at[i], {"dp": self.other})
 
     def coarse_copies(self, here5, here6, there5, there6, sems):
@@ -750,9 +752,12 @@
         r.onorm[...] = tot
 
     def finish(self):
-        cores = [c for m in range(4) for k in (1, 2, 3) for c in self.gather_core_copies(m, k)]
-        for copy in self.sent + cores:
-            copy.wait_send()
+        wait(self.sent)
+        self.sent = []
+
+    def finish_cores(self):
+        cores = [c for m in range(3) for k in (1, 2, 3) for c in self.gather_core_copies(m, k)]
+        wait(cores)
 
 
 def start(copies):
@@ -760,9 +765,14 @@
         copy.start()
 
 
+def wait(copies):
+    for copy in copies:
+        copy.wait_send()
+
+
 class Sum:
     def __init__(self, net, r, name):
-        self.net = net
+        self.net, self.together = net, name == "o"
         for n in ("g", "rc", "rp", "pz", "rz", "fin", "c_s", "c_r", "p_s", "p_r", "z_s", "z_r", "s_s", "s_r"):
             setattr(self, n, getattr(r, name + "_" + n))
         self.parts = self.g.shape[1]
@@ -801,12 +811,50 @@
         part = self.fin.at[:, net.half(net.c), :]
         return [remote(part, part, self.s_s.at[n], self.s_r.at[n], {"dp": net.other})]
 
+    def all_core_copies(self):
+        net = self.net
+        src = self.g.at[:, :, net.half(1 - net.c), :]
+        return [remote(src, self.rc, self.c_s.at[0], self.c_r.at[0], {"dp": net.other})]
+
+    def all_plane_copies(self):
+        net, copies = self.net, []
+        for j in range(1, net.nq):
+            to = net.quarter(j)
+            src = self.g.at[:, :, net.piece_rows(to), :]
+            where = {"dp": 2 * to + net.c}
+            sems = self.p_s.at[j - 1], self.p_r.at[j - 1]
+            copies.append(remote(src, self.rp.at[:, j - 1], *sems, where))
+        return copies
+
+    def all_core(self):
+        start(self.all_core_copies())
+
+    def all_plane(self):
+        net = self.net
+        net.arrive(self.rc, self.c_s.at[0], self.c_r.at[0], {"dp": net.other})
+        for k in range(NMP):
+            self.add_half(k)
+        start(self.all_plane_copies())
+
+    def all_pass_on(self):
+        net = self.net
+        for j in range(1, net.nq):
+            where = {"dp": 2 * net.quarter(j) + net.c}
+            net.arrive(self.rp.at[:, j - 1], self.p_s.at[j - 1], self.p_r.at[j - 1], where)
+        for k in range(1, NMP):
+            self.pass_on(k)
+
     def core(self, k):
         start(self.core_copies(k))
 
     def plane(self, k):
         net = self.net
         net.arrive(self.rc.at[k], self.c_s.at[k], self.c_r.at[k], {"dp": net.other})
+        self.add_half(k)
+        start(self.plane_copies(k))
+
+    def add_half(self, k):
+        net = self.net
 
         def add(i):
             a, b = i // 2, lax.rem(i, 2)
@@ -815,11 +863,10 @@
             self.g[k, a, rows, :] = (self.g[k, a, rows, :].astype(f32) + more).astype(bf16)
 
         loop(2 * self.parts, add)
-        start(self.plane_copies(k))
 
     def total(self, k):
         net = self.net
-        for j in range(1, net.nq):
+        for j in range(1, net.nq if not self.together else 1):
             n = k * (net.nq - 1) + j - 1
             where = {"dp": 2 * net.quarter(j) + net.c}
             net.arrive(self.rp.at[k, j - 1], self.p_s.at[n], self.p_r.at[n], where)
@@ -863,24 +910,24 @@
         net.arrive(part, self.s_s.at[n], self.s_r.at[n], {"dp": net.other})
 
     def finish(self):
-        def step(k):
-            for copy in self.core_copies(k) + self.plane_copies(k):
-                copy.wait_send()
-
-        loop(NMP, step)
-        last = [copy for k in range(1, NMP) for copy in self.z_copies(k)]
-        for copy in last + self.share_copies() + self.share_core_copies():
-            copy.wait_send()
+        if self.together:
+            wait(self.all_core_copies() + self.all_plane_copies())
+        else:
+            loop(NMP, lambda k: wait(self.core_copies(k) + self.plane_copies(k)))
+        wait([copy for k in range(1, NMP) for copy in self.z_copies(k)])
+
+    def finish_share(self):
+        wait(self.share_copies() + self.share_core_copies())
 
 
 def whole_kernel(ndp, r):
     net = Links(r, ndp)
+    r.wup, r.wdn = r.wff.at[:, 0], r.wff.at[:, 1]
     z = net.z
     r.gq, r.gk, r.gv = (e.at[pl.ds(0, T), :] for e in (r.qe, r.ke, r.ve))
     net.weights = (
         (r.wat, pl.ds(0, 384)),
-        (r.wup, pl.ds(0, 512)),
-        (r.wdn, pl.ds(0, 512)),
+        (r.wff, None),
         (r.wat, pl.ds(384, 128)),
     )
     r.mx, r.gof = r.h2, r.pool
@@ -904,40 +951,39 @@
     for copy in loads[1:4]:
         copy.wait()
     net.barrier()
-    for m in (0, 3):
+    for m in (0, 2):
         for k in (1, 2, 3):
             net.gather_z(m, k)
     for copy in loads[4:]:
         copy.wait()
     build_tables(r, z, 0)
     build_tables(r, z, 1)
-    for m in (0, 3):
-        for k in (1, 2, 3):
-            net.gather_plane(m, k)
+    net.gather_z(1, 1)
     for k in (1, 2, 3):
-        net.gather_z(1, k)
-        net.gather_z(2, k)
+        net.gather_plane(0, k)
+    for k in (1, 2, 3):
+        net.gather_plane(2, k)
+    net.gather_z(1, 2)
     build_maps(r)
     project(r, z, shard[:1])
     pool_levels(r, shard[:1])
+    net.gather_z(1, 3)
     for k in (1, 2, 3):
         net.gather_core(0, k)
     attend_own(r, shard[0])
-    for m in (1, 2):
-        net.gather_plane(m, 1)
+    net.gather_plane(1, 1)
     for k in (1, 2, 3):
         net.gather_done(0, k)
     project(r, z, shard[1:])
     for k in (1, 2, 3):
-        net.gather_core(3, k)
-    for m in (1, 2):
-        net.gather_plane(m, 2)
+        net.gather_core(2, k)
     pool_levels(r, shard[1:])
     net.coarse_send()
-    for m in (1, 2):
-        net.gather_plane(m, 3)
+    net.gather_plane(1, 2)
     for c in range(7):
         attend_chunk(r, c, shard[1:])
+        if c == 2:
+            net.gather_plane(1, 3)
     net.coarse_wait()
     net.coarse_clear()
     place_remote(r)
@@ -947,7 +993,7 @@
     by_document(r.gy, r.raw)
     combine_values(r)
     for k in (1, 2, 3):
-        net.gather_done(3, k)
+        net.gather_done(2, k)
     attn_out(r)
 
     def ffn_step(k):
@@ -956,14 +1002,12 @@
         @pl.when(k > 0)
         def _():
             net.gather_done(1, k)
-            net.gather_done(2, k)
 
         ffn_inner(r, f)
 
         @pl.when(k < NMP - 1)
         def _():
             net.gather_core(1, k + 1)
-            net.gather_core(2, k + 1)
 
         ffn_grads(r, f, k)
         net_f.core(k)
@@ -979,19 +1023,16 @@
     put_mixed = pltpu.make_async_copy(r.mx, r.mixed, r.st.at[0])
     put_mixed.start()
     out_grads(r, z)
-    for k in range(NMP):
-        net_o.core(k)
-    net_f.pass_on(1)
+    net_o.all_core()
     context_grads(r)
     attn_back_rows(r)
-    for k in range(NMP):
-        net_o.plane(k)
+    net_f.pass_on(1)
+    net_o.all_plane()
     attend_back_chunk(r, EXT // 128 - 1, False, range(NMP))
     for s in range(NMP):
         values_back(r, 7, s)
     save_remote(r)
     net.coarse_back()
-    net_f.pass_on(2)
 
     def back_step(i):
         k = lax.rem(i + 1, NMP)
@@ -1004,27 +1045,29 @@
 
         unpool(r, z, s)
 
+        attn_grads(r, s, k)
+        net_a.core(k)
+
         @pl.when(i > 0)
         def _():
             net_a.plane(i)
 
-        attn_grads(r, s, k)
-        net_a.core(k)
-
         @pl.when(i == 0)
         def _():
-            net_f.pass_on(3)
-            for n in range(1, NMP):
-                net_o.pass_on(n)
+            net_f.pass_on(2)
 
         @pl.when(i == 1)
         def _():
-            net_f.share()
+            net_f.pass_on(3)
+            net_o.all_pass_on()
 
         @pl.when(i == 2)
         def _():
+            net_f.share()
+
+        @pl.when(i == 3)
+        def _():
             net_o.share()
-            net_f.share_core()
 
         @pl.when(i > 1)
         def _():
@@ -1034,11 +1077,17 @@
     input_grads(r, 0)
     net_a.plane(0)
     net_o.share_core()
+    net_f.share_core()
     input_grads(r, 1)
     net_a.pass_on(3)
+    net.finish()
     net.norms_z()
     put_gx = pltpu.make_async_copy(r.gxs, r.gx, r.st.at[1])
     put_gx.start()
+    net.coarse_clear()
+    net.finish_cores()
+    for each in (net_f, net_o):
+        each.finish()
     net_f.done()
     net_o.done()
     stores = [put_mixed, put_gx]
@@ -1053,10 +1102,10 @@
     start(stores[4:])
     for copy in stores:
         copy.wait()
-    net.coarse_clear()
+    net_a.finish()
+    for each in (net_f, net_o, net_a):
+        each.finish_share()
     net.finish()
-    for each in (net_f, net_o, net_a):
-        each.finish()
 
 
 FAR_OUTS = ("mixed", "gx", "ofn", "oot", "oat")
@@ -1132,8 +1181,7 @@
         gxs=((T, D), f32),
         inv=((ND + 1, EXT - LOC, 128), f32),
         wat=((NMP, D, 512), bf16),
-        wup=((NMP, D, 512), bf16),
-        wdn=((NMP, 512, D), bf16),
+        wff=((NMP, 2, 512, 512), bf16),
         h1=((T, D), bf16),
         qe=((ND * EXT, D), bf16),
         ke=((ND * EXT, D), bf16),
@@ -1169,7 +1217,7 @@
         nz=((NMP, 8, D), f32),
         np=((ndp, 8, D), f32),
     )
-    counts = dict(wz=12, wp=12 * (nq - 1), wc=12, cf=3, cb=3, nz=3, np=ndp - 1)
+    counts = dict(wz=9, wp=9 * (nq - 1), wc=9, cf=3, cb=3, nz=3, np=ndp - 1)
     for n, a, cols in (("f", 2, 512), ("o", 1, 128), ("a", 1, 384)):
         scratch[n + "_g"] = ((NMP, a, 512, cols), bf16)
         scratch[n + "_rc"] = ((NMP, a, HALF, cols), bf16)
@@ -1185,10 +1233,12 @@
     o = run(lambda r: whole_kernel(ndp, r), ins, outs, scratch, sems)
 
     outs = emit(o)
-    return (*outs, *(o["onorm"][i] for i in range(4)))
-
-
-def emit_kernel(mixed, gx, fn, at, ot, o_mixed, o_gx, o_q, o_k, o_v, o_o, o_up, o_dn):
+    return outs
+
+
+def emit_kernel(mixed, gx, fn, at, ot, norms, o_mixed, o_gx, o_q, o_k, o_v, o_o, o_up, o_dn, *o_norms):
+    for i, out in enumerate(o_norms):
+        out[...] = norms[i, :]
     for d in range(ND):
         o_mixed[:, d, :] = mixed[d]
         o_gx[:, d, :] = gx[d]
@@ -1200,7 +1250,7 @@
 
 
 def emit(o):
-    n = 4
+    n = 2
     rows = LOC // n
 
     def tiles(*shape, axis):
@@ -1220,12 +1270,15 @@
             tiles(2, 512, 512, axis=1),
             tiles(1, 512, 384, axis=1),
             tiles(1, 512, 128, axis=1),
+            tiles(8, D, axis=None),
         ],
-        out_specs=[pos, pos, third, third, third, tiles(128, D, axis=1), whole, whole],
+        out_specs=[pos, pos, third, third, third, tiles(128, D, axis=1), whole, whole]
+        + [tiles(D, axis=None)] * 4,
         out_shape=[shape((LOC, ND, D), bf16), shape((LOC, ND, D), f32)]
         + [shape((D, 128), f32)] * 3
-        + [shape((128, D), f32), shape((D, 512), f32), shape((512, D), f32)],
-    )(o["mixed"].reshape(ND, LOC, D), o["gx"].reshape(ND, LOC, D), o["ofn"], o["oat"], o["oot"])
+        + [shape((128, D), f32), shape((D, 512), f32), shape((512, D), f32)]
+        + [shape((D,), f32)] * 4,
+    )(o["mixed"].reshape(ND, LOC, D), o["gx"].reshape(ND, LOC, D), o["ofn"], o["oat"], o["oot"], o["onorm"])
 
 
 def solution(mesh):

time: 123 us -> 117 us (0.951)
  Pallas kernels: 120 us -> 116 us
  local copies, waits for them, and re-layouts: 1.46 us -> 0 us
    pallas_call x1, Pallas kernels: 114 us -> 111 us  [run(): pl.pallas_call(kernel, out_shape=[jax.ShapeDtypeStruct(*v) for v in outs....]
    slice x1 -> x0, local copies, waits for them, and re-layouts: 1.46 us -> none  [per_device(): return (*outs, *(o['onorm'][i] for i in range(4)))]
    pallas_call x1, Pallas kernels: 5.88 us -> 4.52 us  [emit(): pl.pallas_call(emit_kernel, grid=(n,), in_specs=[doc, doc, tiles(2, 512,...]
where the time goes in v4:
time: 117 us; the launch traced here: 116 us
  Pallas kernels  116 us (99%)
    pallas_call x1, Pallas kernels, run(): pl.pallas_call(kernel, out_shape=[jax.ShapeDtypeStruct(*v) for v in outs....  111 us
    pallas_call x1, Pallas kernels, emit(): pl.pallas_call(emit_kernel, grid=(n,), in_specs=[doc, doc, tiles(2, 512,...  4.52 us

profile of v4, /device:TPU:0, one launch (start us, length us, event | category | flops | bytes accessed | tf_op | source)
XLA Modules:
  0.0 116.5 jit_solution(18131855947342561576)
XLA Ops:
  0.6 111.1 %shard_map.220 = (bf16[1024,512]{1,0:T(8,128)(2,1)}, f32[1024,512]{1,0:T(8,128)}, bf16[2,512,512]{2,1,0:T(8,128)(2,1)}, bf16[1,512,128]{2,1,0:T(8,128)(2,1)}, bf...) custom-call(s32[2]{0:T(128)} %refs_0_.1, bf16[512,2,512]{2,1,0:T(2,128)(2,1)} %refs_1_.1, bf16[512,2,512]{2,1,0:T(2,128)(2,1)} %refs_2_.1, ...), custom_call_target="tpu_custom_call" | custom-call | tf_op jit(solution)/shard_map/pallas_call | solution.py:1120
  111.8 4.5 %shard_map.221 = (bf16[512,2,512]{2,1,0:T(2,128)(2,1)}, f32[512,2,512]{2,1,0:T(2,128)}, f32[512,128]{1,0:T(8,128)}, f32[512,128]{1,0:T(8,128)}, f32[512,128]{1,0...) custom-call(bf16[2,512,512]{2,1,0:T(8,128)(2,1)} %bitcast.7, ...), custom_call_target="tpu_custom_call" | custom-call | tf_op jit(solution)/shard_map/pallas_call | solution.py:1264
